TPU v7x, 256 devices: a whole 4x4x8 slice. The times are simulated.
256 devices in a mesh: grid: 16 (over z, y_lo), dom: 16 (over y_hi, x, core).
Axes of the slice: x: 4, y: 4 (y_hi: 2, y_lo: 2; y = y_hi * 2 + y_lo), z: 8, core: 2. Of those that a mesh axis runs over, the one named last changes fastest.
Arguments:
- initial: float32 [16, 512, 64, 128], P('grid', 'dom'), may hold values from -6 to 6
- diffusion: float32 [16, 5], P('grid'), may hold values from 0.02 to 0.09
- drift: float32 [16, 5], P('grid'), may hold values from -0.15 to 0.15
- levels: int32 [16, 3], P('grid'), may hold values from 1 to 3, as said below
- weights: int32 [16], P('grid'), may hold values from -1 to 2, as said below
Outputs:
- stepped: float32 [16, 512, 64, 128], P('grid', 'dom')
- combined: float32 [512, 8, 8, 8, 128], P('dom')
Inputs may be any that keep to these rules, and one draw needn't show every extreme that they name: Each row holds three levels whose sum is 6; grid 0 has a level 1 and a level 3. `weights`: every coefficient is one of -1, 1, 2.
All inputs are finite; a program needn't handle non-finite values.
Results may differ from a plain program's by a relative error of at most 0.00013.
Values sent between devices are 32-bit elements; how exact they have to be, the bound alone decides.
No kernel may reach another device: no remote copies, remote signals or barrier semaphores. Data moves between devices by JAX's collectives and lax.ppermute only.
A program may use at most 128 MiB of HBM per device.

v0:
```python
import jax
import jax.numpy as jnp
import numpy as np
from jax import lax
from jax.sharding import PartitionSpec as P

STEPS = 4
MLEN = 8


def with_halo(x, sides, width):
    for axis, dim in sides:
        size, length = (lax.axis_size(axis), x.shape[dim])
        up = [(i, (i + 1) % size) for i in range(size - 1)]
        down = [(j, i) for i, j in up]
        last = lax.slice_in_dim(x, length - width, length, axis=dim)
        first = lax.slice_in_dim(x, 0, width, axis=dim)
        before = lax.ppermute(last, axis, up)
        after = lax.ppermute(first, axis, down)
        x = jnp.concatenate([before, x, after], axis=dim)
    return x


def nodal_matrix(length_dim):
    matrix = np.eye(length_dim)
    stride = length_dim // 2
    while stride >= 1:
        for position in range(stride, length_dim, 2 * stride):
            matrix[position] = matrix[position] + 0.5 * matrix[position - stride]
            if position + stride < length_dim:
                matrix[position] = matrix[position] + 0.5 * matrix[position + stride]
        stride = stride // 2
    return matrix


def along_dim(values, matrix, dimension):
    product = jnp.tensordot(
        jnp.asarray(matrix, jnp.float32),
        values,
        axes=((1,), (dimension,)),
        precision=lax.Precision.HIGHEST,
    )
    return jnp.moveaxis(product, 0, dimension)


def mid_coords(level_row, point_count):
    places = jnp.arange(point_count, dtype=jnp.int32)
    lengths = jnp.left_shift(jnp.ones((3,), jnp.int32), level_row)
    offsets = [level_row[1] + level_row[2], level_row[2], jnp.zeros((), jnp.int32)]
    coords = [
        jnp.bitwise_and(jnp.right_shift(places, offsets[dimension]), lengths[dimension] - 1)
        for dimension in range(3)
    ]
    return (coords, lengths)


def mid_operator(level_row, spread_rate, drift_rate, point_count):
    coords, lengths = mid_coords(level_row, point_count)
    matrix = jnp.zeros((point_count, point_count), jnp.float32)
    identity = jnp.eye(point_count, dtype=jnp.float32)
    for dimension in range(3):
        aligned = jnp.ones((point_count, point_count), bool)
        for other in range(3):
            if other != dimension:
                aligned = aligned & (coords[other][:, None] == coords[other][None, :])
        upper_hit = aligned & (coords[dimension][None, :] == coords[dimension][:, None] + 1)
        lower_hit = aligned & (coords[dimension][None, :] == coords[dimension][:, None] - 1)
        spread_now = spread_rate[dimension + 1]
        drift_now = drift_rate[dimension + 1]
        matrix = (
            matrix
            + upper_hit.astype(jnp.float32) * (spread_now + 0.5 * drift_now)
            + lower_hit.astype(jnp.float32) * (spread_now - 0.5 * drift_now)
        )
        matrix = matrix - 2.0 * spread_now * identity
    return matrix


def mid_surplus(level_row, point_count):
    coords, lengths = mid_coords(level_row, point_count)
    matrix = jnp.ones((point_count, point_count), jnp.float32)
    for dimension in range(3):
        row_place = coords[dimension][:, None]
        col_place = coords[dimension][None, :]
        stride = jnp.bitwise_and(row_place, -row_place)
        interior = row_place > 0
        factor = (
            (row_place == col_place).astype(jnp.float32)
            - 0.5 * (interior & (col_place == row_place - stride)).astype(jnp.float32)
            - 0.5
            * (
                interior
                & (col_place == row_place + stride)
                & (row_place + stride < lengths[dimension])
            ).astype(jnp.float32)
        )
        matrix = matrix * factor
    return matrix


def inject_matrix(level_row, point_count, full_len):
    coords, lengths = mid_coords(level_row, point_count)
    target = jnp.zeros((point_count,), jnp.int32)
    for dimension in range(3):
        target = target + coords[dimension] * (full_len // lengths[dimension]) * full_len ** (
            2 - dimension
        )
    return (jnp.arange(full_len**3, dtype=jnp.int32)[:, None] == target[None, :]).astype(
        jnp.float32
    )


def advance(values_now, spread_rate, drift_rate, operator):
    centre = values_now[1:-1]
    upper_side = values_now[2:]
    lower_side = values_now[:-2]
    updated = (
        centre
        + spread_rate[0] * (upper_side + lower_side - 2.0 * centre)
        + 0.5 * drift_rate[0] * (upper_side - lower_side)
    )
    updated = updated + jnp.einsum("pq,rql->rpl", operator, centre, precision=lax.Precision.HIGHEST)
    padded = jnp.pad(centre, ((0, 0), (0, 0), (1, 1)))
    last_len = centre.shape[2]
    upper_side = padded[:, :, 2:]
    lower_side = padded[:, :, :last_len]
    updated = (
        updated
        + spread_rate[4] * (upper_side + lower_side - 2.0 * centre)
        + 0.5 * drift_rate[4] * (upper_side - lower_side)
    )
    return updated


def finish(share_part):
    row_count = share_part.shape[0]
    last_share = share_part.shape[2]
    shaped = share_part.reshape(row_count, MLEN, MLEN, MLEN, last_share)
    for dimension in range(1, 4):
        shaped = along_dim(shaped, nodal_matrix(MLEN), dimension)
    return shaped


def per_device(initial, diffusion, drift, levels, weights):
    values_now = initial[0]
    spread_rate = diffusion[0]
    drift_rate = drift[0]
    level_row = levels[0]
    point_count = values_now.shape[1]
    operator = mid_operator(level_row, spread_rate, drift_rate, point_count)
    for step_number in range(STEPS):
        padded = with_halo(values_now, (("dom", 0),), 1)
        values_now = advance(padded, spread_rate, drift_rate, operator)
    stepped = values_now[None]
    surplus = jnp.einsum(
        "pq,rql->rpl",
        mid_surplus(level_row, point_count),
        values_now,
        precision=lax.Precision.HIGHEST,
    )
    grid_scale = weights[0].astype(jnp.float32) / lax.axis_size("grid")
    weighted = (
        jnp.einsum(
            "fp,rpl->rfl",
            inject_matrix(level_row, point_count, MLEN),
            surplus,
            precision=lax.Precision.HIGHEST,
        )
        * grid_scale
    )
    combined = finish(lax.psum(weighted, "grid"))
    return (stepped, combined)


def solution(mesh):
    in_specs = (
        P("grid", "dom", None, None),
        P("grid", None),
        P("grid", None),
        P("grid", None),
        P("grid"),
    )
    out_specs = (P("grid", "dom", None, None), P("dom", None, None, None, None))
    return jax.shard_map(
        per_device, mesh=mesh, in_specs=in_specs, out_specs=out_specs, check_vma=False
    )
```

profile of v0, /device:TPU:6, one launch (start us, length us, event | category | flops | bytes accessed | tf_op | source)
XLA Modules:
  0.0 532.2 jit_solution(15986025874108397605)
XLA Ops:
  7.2 0.8 slice_bitcast_fusion
  8.0 1.9 collective-permute-start.1
  9.9 3.6 collective-permute-start
  13.6 0.7 broadcast_shift-left_fusion
  14.2 0.6 fusion.94
  22.5 1.4 fusion.93
  25.2 0.7 multiply_add_fusion.4
  25.9 0.7 broadcast_compare_fusion.4
  26.6 1.5 fusion.96
  28.1 1.5 fusion.95
  38.4 6.6 %multiply_add_fusion.3 = f32[32,64,128]{2,1,0:T(8,128)S(1)} fusion(f32[32,64,128]{2,1,0:T(8,128)} %bitcast.90, f32[1,64,128]{2,1,0:T(8,128)S(1)} %collective-permute-done, f32[1,64,128]{2,1,0:T(8,128)S(1)} %collective-permute-done.1, f32[]{:T(128)} %bitcast.22, f32[]{:T(128)} %bitcast.21, f32[]{:T(128)} %bitcast.4, f32[]{:T(128)} %bitcast.1, f32[]{:T(128)} %bitcast.18, ...), kind=kOutput, calls=%fused_computation.32 | convolution fusion | flops 206192640 | bytes 3224064 | tf_op jit(solution)/shard_map/pq,rql->rpl/dot_general | solution.py:122
  45.0 3.4 collective-permute-start.3
  48.5 2.2 collective-permute-start.2
  50.6 0.6 broadcast_compare_fusion.5
  51.2 5.2 collective-permute-done.2
  56.4 3.1 multiply_add_fusion.2
  59.6 8.2 %collective-permute-start.5 = (f32[1,64,128]{2,1,0:T(8,128)S(1)}, f32[1,64,128]{2,1,0:T(8,128)S(1)}, u32[]{:S(2)}, u32[]{:S(2)}) collective-permute-start(f32[1,64,128]{2,1,0:T(8,128)S(1)} %get-tuple-element.7), channel_id=1, source_target_pairs={{0,1},{1,2},{2,3},{3,4},{4,5},{5,6},{6,7},{7,8},{8,9},{9,10},{10,1... | collective-permute-start | bytes 98312 | tf_op jit(solution)/shard_map/ppermute | solution.py:18
  67.7 1.9 collective-permute-start.4
  69.7 1.6 collective-permute-done.4
  71.2 3.1 multiply_add_fusion.1
  74.4 7.3 %collective-permute-start.7 = (f32[1,64,128]{2,1,0:T(8,128)S(1)}, f32[1,64,128]{2,1,0:T(8,128)S(1)}, u32[]{:S(2)}, u32[]{:S(2)}) collective-permute-start(f32[1,64,128]{2,1,0:T(8,128)S(1)} %get-tuple-element.5), channel_id=1, source_target_pairs={{0,1},{1,2},{2,3},{3,4},{4,5},{5,6},{6,7},{7,8},{8,9},{9,10},{10,1... | collective-permute-start | bytes 98312 | tf_op jit(solution)/shard_map/ppermute | solution.py:18
  81.7 1.9 collective-permute-start.6
  83.6 0.7 broadcast_compare_fusion
  85.2 3.1 multiply_add_fusion
  88.3 1.2 convolution_bitcast_fusion.1
  89.5 6.3 %multiply_bitcast_fusion = f32[32,512,128]{1,2,0:T(8,128)} fusion(f32[]{:T(128)} %bitcast.30, f32[32,64,128]{2,1,0:T(8,128)S(1)} %convolution_bitcast_fusion.1, s32[64]{0:T(128)S(1)} %get-tuple-element.2), kind=kOutput, calls=%fused_computation.4 | convolution fusion | flops 1612742656 | bytes 9437444 | tf_op jit(solution)/shard_map/fp,rpl->rfl/dot_general | solution.py:163
  95.8 9.0 %copy.11 = f32[32,512,128]{2,1,0:T(8,128)} copy(f32[32,512,128]{1,2,0:T(8,128)} %multiply_bitcast_fusion) | data formatting | bytes 16777216 | tf_op jit(solution)/shard_map/mul | solution.py:163
  104.8 14.5 %copy.12 = f32[32,8,8,8,128]{4,1,3,2,0:T(8,128)} copy(f32[32,8,8,8,128]{4,3,2,1,0:T(8,128)} %bitcast.88) | data formatting | bytes 16777216 | tf_op jit(solution)/shard_map/reshape | solution.py:138
  119.3 372.2 %all-reduce.6.cloned.1.call-done = f32[32,8,8,8,128]{4,1,3,2,0:T(8,128)} async-done(((f32[32,8,8,8,128]{4,1,3,2,0:T(8,128)}), f32[32,8,8,8,128]{4,1,3,2,0:T(8,128)}) %all-reduce.6.cloned.1.call-update) | async-done | bytes 8388624 | tf_op jit(solution)/shard_map/psum | solution.py:171
  491.5 10.6 %convolution_bitcast_fusion = f32[32,8,8,8,128]{4,1,3,2,0:T(8,128)S(1)} fusion(f32[32,8,8,8,128]{4,1,3,2,0:T(8,128)} %all-reduce.6.cloned.1.call-done, f32[8,8,1,1,1]{1,0,4,3,2:T(8,128)S(1)} %copy-done.1), kind=kOutput, calls=%fused_computation.7 | convolution fusion | flops 201326592 | bytes 16777472 | tf_op jit(solution)/shard_map/dot_general | solution.py:37
  502.1 13.4 %fusion.4 = f32[32,8,8,8,128]{4,2,3,1,0:T(8,128)S(1)} fusion(f32[8,8,1,1,1]{1,0,4,3,2:T(8,128)S(1)} %copy-done.1, f32[32,8,8,8,128]{4,1,3,2,0:T(8,128)S(1)} %convolution_bitcast_fusion), kind=kOutput, calls=%fused_computation.5 | convolution fusion | flops 201326592 | bytes 16777472 | tf_op jit(solution)/shard_map/dot_general | solution.py:37
  515.5 9.6 %fusion.7 = f32[32,8,8,8,128]{4,3,2,1,0:T(8,128)} fusion(f32[8,8,1,1,1]{1,0,4,3,2:T(8,128)S(1)} %copy-done.1, f32[32,8,8,8,128]{4,2,3,1,0:T(8,128)S(1)} %fusion.4), kind=kOutput, calls=%fused_computation.6 | convolution fusion | flops 201326592 | bytes 16777472 | tf_op jit(solution)/shard_map/dot_general | solution.py:37
  (19 shorter events, 0.4 us)
Async XLA Ops:
  7.2 484.4 %all-reduce.6.cloned.1.call-start = ((), (), s32[]{:S(2)}) async-start(), calls=%async_computation | async-start | bytes 16777216 | tf_op jit(solution)/shard_map/psum | solution.py:171
  8.0 30.4 %collective-permute-start.1 = (f32[1,64,128]{2,1,0:T(8,128)S(1)}, f32[1,64,128]{2,1,0:T(8,128)S(1)}, u32[]{:S(2)}, u32[]{:S(2)}) collective-permute-start(f32[1,64,128]{2,1,0:T(8,128)S(1)} %get-tuple-element.11), channel_id=1, source_target_pairs={{0,1},{1,2},{2,3},{3,4},{4,5},{5,6},{6,7},{7,8},{8,9},{9,10},{10,1... | collective-permute-start | bytes 98312 | tf_op jit(solution)/shard_map/ppermute | solution.py:18
  9.9 28.5 %collective-permute-start = (f32[1,64,128]{2,1,0:T(8,128)S(1)}, f32[1,64,128]{2,1,0:T(8,128)S(1)}, u32[]{:S(2)}, u32[]{:S(2)}) collective-permute-start(f32[1,64,128]{2,1,0:T(8,128)S(1)} %get-tuple-element.12), channel_id=1, source_target_pairs={{1,0},{2,1},{3,2},{4,3},{5,4},{6,5},{7,6},{8,7},{9,8},{10,9},{11,1... | collective-permute-start | bytes 98312 | tf_op jit(solution)/shard_map/ppermute | solution.py:19
  45.0 6.2 %collective-permute-start.3 = (f32[1,64,128]{2,1,0:T(8,128)S(1)}, f32[1,64,128]{2,1,0:T(8,128)S(1)}, u32[]{:S(2)}, u32[]{:S(2)}) collective-permute-start(f32[1,64,128]{2,1,0:T(8,128)S(1)} %get-tuple-element.9), channel_id=1, source_target_pairs={{0,1},{1,2},{2,3},{3,4},{4,5},{5,6},{6,7},{7,8},{8,9},{9,10},{10,1... | collective-permute-start | bytes 98312 | tf_op jit(solution)/shard_map/ppermute | solution.py:18
  48.5 7.9 %collective-permute-start.2 = (f32[1,64,128]{2,1,0:T(8,128)S(1)}, f32[1,64,128]{2,1,0:T(8,128)S(1)}, u32[]{:S(2)}, u32[]{:S(2)}) collective-permute-start(f32[1,64,128]{2,1,0:T(8,128)S(1)} %get-tuple-element.10), channel_id=1, source_target_pairs={{1,0},{2,1},{3,2},{4,3},{5,4},{6,5},{7,6},{8,7},{9,8},{10,9},{11,1... | collective-permute-start | bytes 98312 | tf_op jit(solution)/shard_map/ppermute | solution.py:19
  59.6 10.1 %collective-permute-start.5 = (f32[1,64,128]{2,1,0:T(8,128)S(1)}, f32[1,64,128]{2,1,0:T(8,128)S(1)}, u32[]{:S(2)}, u32[]{:S(2)}) collective-permute-start(f32[1,64,128]{2,1,0:T(8,128)S(1)} %get-tuple-element.7), channel_id=1, source_target_pairs={{0,1},{1,2},{2,3},{3,4},{4,5},{5,6},{6,7},{7,8},{8,9},{9,10},{10,1... | collective-permute-start | bytes 98312 | tf_op jit(solution)/shard_map/ppermute | solution.py:18
  67.7 3.5 collective-permute-start.4
  74.4 10.5 %collective-permute-start.7 = (f32[1,64,128]{2,1,0:T(8,128)S(1)}, f32[1,64,128]{2,1,0:T(8,128)S(1)}, u32[]{:S(2)}, u32[]{:S(2)}) collective-permute-start(f32[1,64,128]{2,1,0:T(8,128)S(1)} %get-tuple-element.5), channel_id=1, source_target_pairs={{0,1},{1,2},{2,3},{3,4},{4,5},{5,6},{6,7},{7,8},{8,9},{9,10},{10,1... | collective-permute-start | bytes 98312 | tf_op jit(solution)/shard_map/ppermute | solution.py:18
  81.7 3.5 collective-permute-start.6
  88.3 16.5 %copy-start = (f32[32,64,128]{2,1,0:T(8,128)}, f32[32,64,128]{2,1,0:T(8,128)S(1)}, u32[]{:S(2)}) copy-start(f32[32,64,128]{2,1,0:T(8,128)S(1)} %multiply_add_fusion) | copy-start | bytes 3145732
  119.3 372.2 %copy-start.1 = (f32[8,8,1,1,1]{1,0,4,3,2:T(8,128)S(1)}, f32[8,8,1,1,1]{1,0,4,3,2:T(8,128)}, u32[]{:S(2)}) copy-start(f32[8,8,1,1,1]{1,0,4,3,2:T(8,128)} %constant.85) | copy-start | bytes 772
Sparse Core Ops, SparseCore 0:
  119.4 372.0 all-reduce.5
where the time goes:
time: 541 us; the launch traced here: 532 us
  waiting for transfers between devices  379 us (70%)
  matrix products  57 us (11%)
  between operations  32.9 us (6%)
  starting transfers between devices  30.4 us (6%)
  local copies, waits for them, and re-layouts  29.3 us (5%)
    psum x1, waiting for transfers between devices, per_device(): combined = finish(lax.psum(weighted, 'grid'))  372 us
    dot_general x3, matrix products, along_dim(): jnp.tensordot(jnp.asarray(matrix, jnp.float32), values, axes=((1,), (dime...  33.6 us
    ppermute x4, starting transfers between devices, with_halo(): before = lax.ppermute(last, axis, up)  20.7 us
    dot_general x4, matrix products, advance(): jnp.einsum('pq,rql->rpl', operator, centre, precision=lax.Precision.HIGHEST)  16 us
    reshape x1, local copies, waits for them, and re-layouts, finish(): shaped = share_part.reshape(row_count, MLEN, MLEN, MLEN, last_share)  14.5 us
  transfers between devices with their start and end apart: 9, of which 4 were waited for; matrix products, arithmetic and copies ran while one was open for 2% of the time, Pallas kernels for 0%

commit v1 on v0

v1 whole, which is shorter than its diff:
```python
import itertools

import jax
import jax.numpy as jnp
import numpy as np
from jax import lax
from jax.experimental import pallas as pl
from jax.experimental.pallas import tpu as pltpu
from jax.sharding import PartitionSpec as P

STEPS = 4
MLEN = 8
FINEST = 3
LEVEL_SUM = 6
ZLEN = 8


def rank_of(coordinate):
    if coordinate % 4 == 0:
        return 1
    return 2 if coordinate % 2 == 0 else 3


def union_points():
    points = []
    for first in (0, 4, 2, 6, 1, 3, 5, 7):
        for second, third in itertools.product(range(MLEN), repeat=2):
            if rank_of(first) + rank_of(second) + rank_of(third) <= LEVEL_SUM:
                points.append((first, second, third))
    return np.array(points, np.int32)


POINTS = union_points()
COUNT = len(POINTS)


def nodal_matrix(length_dim):
    matrix = np.eye(length_dim)
    stride = length_dim // 2
    while stride >= 1:
        for position in range(stride, length_dim, 2 * stride):
            matrix[position] = matrix[position] + 0.5 * matrix[position - stride]
            if position + stride < length_dim:
                matrix[position] = matrix[position] + 0.5 * matrix[position + stride]
        stride = stride // 2
    return matrix


def fill_matrix():
    nodal = nodal_matrix(MLEN)
    matrix = np.zeros((MLEN, MLEN, MLEN, COUNT))
    for column, (first, second, third) in enumerate(POINTS):
        matrix[first, :, :, column] = np.outer(nodal[:, second], nodal[:, third])
    return matrix.reshape(MLEN**3, COUNT)


def split_three(values):
    high = values.astype(jnp.bfloat16)
    rest = values - high.astype(jnp.float32)
    middle = rest.astype(jnp.bfloat16)
    low = (rest - middle.astype(jnp.float32)).astype(jnp.bfloat16)
    return high, middle, low


def exact_dot(matrix, values):
    total = None
    for part in split_three(values):
        term = jnp.dot(matrix, part, preferred_element_type=jnp.float32)
        total = term if total is None else total + term
    return total


def step_kernel(
    rows, points, place_ref, level_ref, spread_ref, drift_ref, start_ref, before_ref, after_ref,
    stepped_ref, *rest
):
    parts = rest[:ZLEN]
    first, second, final, coef_ref, load_sem, store_sem = rest[ZLEN:]
    halo = STEPS
    share = rows // ZLEN
    loads = [
        pltpu.make_async_copy(before_ref, first.at[pl.ds(0, halo * points)], load_sem.at[0]),
        pltpu.make_async_copy(start_ref, first.at[pl.ds(halo * points, rows * points)], load_sem.at[1]),
        pltpu.make_async_copy(
            after_ref, first.at[pl.ds((halo + rows) * points, halo * points)], load_sem.at[2]
        ),
    ]
    for load in loads:
        load.start()

    place = lax.broadcasted_iota(jnp.int32, (points, 128), 0)
    lane = lax.broadcasted_iota(jnp.int32, (8, 128), 1)
    offsets = [level_ref[0, 1] + level_ref[0, 2], level_ref[0, 2], jnp.int32(0)]
    strides = []
    centre_rate = 1.0 - 2.0 * spread_ref[0, 0] - 2.0 * spread_ref[0, 4]
    for dim in range(3):
        length = jnp.left_shift(jnp.int32(1), level_ref[0, dim])
        coord = jnp.bitwise_and(jnp.right_shift(place, offsets[dim]), length - 1)
        spread, drift = spread_ref[0, dim + 1], 0.5 * drift_ref[0, dim + 1]
        coef_ref[2 * dim] = jnp.where(coord < length - 1, spread + drift, 0.0)
        coef_ref[2 * dim + 1] = jnp.where(coord > 0, spread - drift, 0.0)
        strides.append(jnp.left_shift(jnp.int32(1), offsets[dim]))
        centre_rate = centre_rate - 2.0 * spread
    row_up = spread_ref[0, 0] + 0.5 * drift_ref[0, 0]
    row_down = spread_ref[0, 0] - 0.5 * drift_ref[0, 0]
    lane_up = jnp.where(lane < 127, spread_ref[0, 4] + 0.5 * drift_ref[0, 4], 0.0)
    lane_down = jnp.where(lane > 0, spread_ref[0, 4] - 0.5 * drift_ref[0, 4], 0.0)
    keep_low = place_ref[1].astype(jnp.float32)
    keep_high = place_ref[2].astype(jnp.float32)

    for load in loads:
        load.wait()

    def advance(source, target, step, target_base):
        low, high = step, 2 * halo + rows - step

        def tile(tile_index, carry):
            base = pl.multiple_of(tile_index * 8, 8)
            coefs = [coef_ref[i, pl.ds(base, 8), :] for i in range(6)]

            def update(row, below, centre, above):
                offset = row * points + base
                total = centre * centre_rate + above * row_up + below * row_down
                total = total + pltpu.roll(centre, 127, 1) * lane_up
                total = total + pltpu.roll(centre, 1, 1) * lane_down
                for dim in range(3):
                    total = total + source[pl.ds(offset + strides[dim], 8), :] * coefs[2 * dim]
                    total = total + source[pl.ds(offset - strides[dim], 8), :] * coefs[2 * dim + 1]
                return total

            def store(row, value):
                offset = pl.multiple_of((row - target_base) * points + base, 8)
                target[pl.ds(offset, 8), :] = value

            def at(row):
                return source[pl.ds(pl.multiple_of(row * points + base, 8), 8), :]

            below, centre = at(low - 1), at(low)
            for row in range(low, halo):
                above = at(row + 1)
                store(row, update(row, below, centre, above) * keep_low)
                below, centre = centre, above

            def group(index, pair):
                below, centre = pair
                for k in range(8):
                    row = halo + index * 8 + k
                    above = at(row + 1)
                    store(row, update(row, below, centre, above))
                    below, centre = centre, above
                return below, centre

            below, centre = lax.fori_loop(0, rows // 8, group, (below, centre))
            for row in range(halo + rows, high):
                above = at(row + 1)
                store(row, update(row, below, centre, above) * keep_high)
                below, centre = centre, above
            return carry

        lax.fori_loop(0, points // 8, tile, 0)

    advance(first, second, 1, 0)
    advance(second, first, 2, 0)
    advance(first, second, 3, 0)
    advance(second, final, 4, halo)

    stores = [pltpu.make_async_copy(final, stepped_ref, store_sem.at[ZLEN])]
    for index, part in enumerate(parts):
        begin = pl.multiple_of(jnp.bitwise_xor(place_ref[0], index) * (share * points), 8)
        stores.append(
            pltpu.make_async_copy(final.at[pl.ds(begin, share * points)], part, store_sem.at[index])
        )
    for copy in stores:
        copy.start()
    for copy in stores:
        copy.wait()


def step_rows(place, levels, spread, drift, start, before, after):
    rows, points, lanes = start.shape
    share = rows // ZLEN * points
    flat = lambda v: v.reshape(-1, lanes)
    anywhere = pl.BlockSpec(memory_space=pl.ANY)
    scalars = pl.BlockSpec(memory_space=pltpu.SMEM)
    total = rows + 2 * STEPS
    outs = pl.pallas_call(
        lambda *refs: step_kernel(rows, points, *refs),
        out_shape=[jax.ShapeDtypeStruct((rows * points, lanes), jnp.float32)]
        + [jax.ShapeDtypeStruct((share, lanes), jnp.float32)] * ZLEN,
        in_specs=[scalars] * 4 + [anywhere] * 3,
        out_specs=[anywhere] * (1 + ZLEN),
        scratch_shapes=[
            pltpu.VMEM((total * points, lanes), jnp.float32),
            pltpu.VMEM((total * points, lanes), jnp.float32),
            pltpu.VMEM((rows * points, lanes), jnp.float32),
            pltpu.VMEM((6, points, lanes), jnp.float32),
            pltpu.SemaphoreType.DMA((3,)),
            pltpu.SemaphoreType.DMA((ZLEN + 1,)),
        ],
        compiler_params=pltpu.CompilerParams(vmem_limit_bytes=24 * 2**20),
        cost_estimate=pl.CostEstimate(
            flops=25 * STEPS * total * points * lanes, bytes_accessed=16 * rows * points * lanes,
            transcendentals=0,
        ),
        name="step_rows",
    )(place, levels, spread, drift, flat(start), flat(before), flat(after))
    return outs[0].reshape(rows, points, lanes), outs[1:]


def combine_kernel(share, points, matrix_ref, *refs):
    out_ref = refs[-1]
    matrix = matrix_ref[...]
    for row in range(share):
        stack = [ref[row * points : (row + 1) * points, :] for ref in refs[:-1]]
        out_ref[row] = exact_dot(matrix, jnp.concatenate(stack, axis=0))


def combine(matrix, pieces, share):
    lanes = pieces[0].shape[1]
    points = pieces[0].shape[0] // share
    return pl.pallas_call(
        lambda *refs: combine_kernel(share, points, *refs),
        out_shape=jax.ShapeDtypeStruct((share, COUNT, lanes), jnp.float32),
        compiler_params=pltpu.CompilerParams(vmem_limit_bytes=24 * 2**20),
        cost_estimate=pl.CostEstimate(
            flops=6 * share * matrix.size * lanes, bytes_accessed=4 * 2**20, transcendentals=0
        ),
        name="combine",
    )(matrix, *pieces)


def fill_kernel(chunks, width, with_base, where_ref, matrix_ref, *refs):
    sources = refs[:chunks]
    out_ref, scratch, sems = refs[chunks + with_base :]
    matrix = matrix_ref[...]
    copies = []
    points = MLEN**2
    for index, source in enumerate(sources):
        for row in range(width):
            flat = exact_dot(matrix, source[row])
            at = lambda c: flat[c * points : (c + 1) * points]
            nodal = [None] * MLEN
            nodal[0] = at(0)
            nodal[4] = at(4) + 0.5 * nodal[0]
            nodal[2] = at(2) + 0.5 * (nodal[0] + nodal[4])
            nodal[6] = at(6) + 0.5 * nodal[4]
            nodal[1] = at(1) + 0.5 * (nodal[0] + nodal[2])
            nodal[3] = at(3) + 0.5 * (nodal[2] + nodal[4])
            nodal[5] = at(5) + 0.5 * (nodal[4] + nodal[6])
            nodal[7] = at(7) + 0.5 * nodal[6]
            for c in range(MLEN):
                scratch[index * width + row, c * points : (c + 1) * points, :] = nodal[c]
        copy = pltpu.make_async_copy(
            scratch.at[pl.ds(index * width, width)],
            out_ref.at[pl.ds(where_ref[index], width)],
            sems.at[index],
        )
        copy.start()
        copies.append(copy)
    for copy in copies:
        copy.wait()


def fill(where, matrix, sources, rows, base):
    width, _, lanes = sources[0].shape
    chunks = len(sources)
    with_base = 0 if base is None else 1
    args = [where, matrix, *sources] + ([base] if with_base else [])
    anywhere = pl.BlockSpec(memory_space=pl.ANY)
    vector = pl.BlockSpec(memory_space=pltpu.VMEM)
    return pl.pallas_call(
        lambda *refs: fill_kernel(chunks, width, with_base, *refs),
        out_shape=jax.ShapeDtypeStruct((rows, MLEN**3, lanes), jnp.float32),
        in_specs=[pl.BlockSpec(memory_space=pltpu.SMEM)] + [vector] * (1 + chunks) + [anywhere] * with_base,
        out_specs=anywhere,
        input_output_aliases={2 + chunks: 0} if with_base else {},
        scratch_shapes=[
            pltpu.VMEM((chunks * width, MLEN**3, lanes), jnp.float32),
            pltpu.SemaphoreType.DMA((chunks,)),
        ],
        compiler_params=pltpu.CompilerParams(vmem_limit_bytes=24 * 2**20),
        cost_estimate=pl.CostEstimate(
            flops=6 * chunks * width * matrix.size * lanes,
            bytes_accessed=4 * chunks * width * (MLEN**3 + COUNT) * lanes,
            transcendentals=0,
        ),
        name="fill",
    )(*args)


def placing_matrix(levels, scale, point_count):
    grids = levels.shape[0]
    shape = (COUNT, grids * point_count)
    column = lax.broadcasted_iota(jnp.int32, shape, 1) % point_count
    spread = lambda v: jnp.repeat(v, point_count)[None, :]
    level = [spread(levels[:, dim]) for dim in range(3)]
    offsets = [level[1] + level[2], level[2], jnp.zeros_like(level[0])]
    matrix = jnp.broadcast_to(spread(scale), shape)
    for dim in range(3):
        length = jnp.left_shift(jnp.ones_like(level[dim]), level[dim])
        coord = jnp.bitwise_and(jnp.right_shift(column, offsets[dim]), length - 1)
        shift = FINEST - level[dim]
        target = jnp.asarray(POINTS[:, dim])[:, None]
        row = jnp.right_shift(target, shift)
        present = jnp.left_shift(row, shift) == target
        stride = jnp.bitwise_and(row, -row)
        near = (row > 0) & ((coord == row - stride) | (coord == row + stride))
        factor = (coord == row).astype(jnp.float32) - 0.5 * near.astype(jnp.float32)
        matrix = matrix * jnp.where(present, factor, 0.0)
    return matrix.astype(jnp.bfloat16)


def per_device(initial, diffusion, drift, levels, weights):
    values = initial[0]
    rows, points, _ = values.shape
    share = rows // ZLEN
    dom_size = lax.axis_size("dom")
    grid_size = lax.axis_size("grid")
    columns = grid_size // ZLEN
    dom = lax.axis_index("dom")
    grid = lax.axis_index("grid")
    z, y = grid // columns, grid % columns

    facts = lax.all_gather(jnp.concatenate([levels[0], weights]), "grid")

    up = [(i, i + 1) for i in range(dom_size - 1)]
    down = [(j, i) for i, j in up]
    before = lax.ppermute(values[rows - STEPS :], "dom", up)
    after = lax.ppermute(values[:STEPS], "dom", down)
    place = jnp.stack([z, (dom > 0).astype(jnp.int32), (dom < dom_size - 1).astype(jnp.int32)])
    stepped, parts = step_rows(place, levels, diffusion, drift, values, before, after)

    pieces = [parts[0]] + [
        lax.ppermute(parts[k], "grid", [(i, i ^ (k * columns)) for i in range(grid_size)])
        for k in range(1, ZLEN)
    ]
    members = jnp.bitwise_xor(z, jnp.arange(ZLEN, dtype=jnp.int32)) * columns + y
    chosen = facts[members]
    matrix = placing_matrix(chosen[:, :3], chosen[:, 3].astype(jnp.float32) / grid_size, points)
    partial = combine(matrix, pieces, share)
    other = lax.ppermute(partial, "grid", [(i, i ^ 1) for i in range(grid_size)])
    half = share // 2
    ups = [partial[:half] + other[:half], partial[half:] + other[half:]]
    downs = list(ups)

    plus = [(i, (i + columns) % grid_size) for i in range(grid_size)]
    minus = [(j, i) for i, j in plus]
    matrix = jnp.asarray(fill_matrix(), jnp.bfloat16)
    begin = lambda source, part: source % ZLEN * share + part * half
    combined = fill(jnp.stack([begin(z, 0), begin(z, 1)]), matrix, ups, rows, None)
    for hop in range(1, ZLEN // 2):
        ups = [lax.ppermute(v, "grid", plus) for v in ups]
        downs = [lax.ppermute(v, "grid", minus) for v in downs]
        where = jnp.stack(
            [begin(z - hop + ZLEN, s) for s in range(2)] + [begin(z + hop, s) for s in range(2)]
        )
        combined = fill(where, matrix, ups + downs, rows, combined)
    last = [lax.ppermute(ups[0], "grid", plus), lax.ppermute(downs[1], "grid", minus)]
    where = jnp.stack([begin(z + ZLEN // 2, s) for s in range(2)])
    combined = fill(where, matrix, last, rows, combined)
    return stepped[None], combined.reshape(rows, MLEN, MLEN, MLEN, -1)


def solution(mesh):
    in_specs = (
        P("grid", "dom", None, None),
        P("grid", None),
        P("grid", None),
        P("grid", None),
        P("grid"),
    )
    out_specs = (P("grid", "dom", None, None), P("dom", None, None, None, None))
    return jax.shard_map(
        per_device, mesh=mesh, in_specs=in_specs, out_specs=out_specs, check_vma=False
    )
```

time: 541 us -> 140 us (0.26); the launches traced: 532 us -> 140 us
  waiting for transfers between devices: 379 us -> 36.4 us
  matrix products: 57 us -> 0 us
  Pallas kernels: 0 us -> 33.6 us
  between operations: 32.9 us -> 2.37 us
  local copies, waits for them, and re-layouts: 29.3 us -> 7.82 us
  blocking collectives: 0 us -> 18.7 us
  starting transfers between devices: 30.4 us -> 37.9 us
    psum x1 -> x0, waiting for transfers between devices: 372 us -> none  [per_device(): combined = finish(lax.psum(weighted, 'grid'))]
    dot_general x9 -> x0, matrix products: 57 us -> none  [the longest x3 33.6 us: along_dim(): jnp.tensordot(jnp.asarray(matrix, jnp.float32), values, axes=((1,), (dime...]
    pallas_call x0 -> x7, Pallas kernels: none -> 33.6 us  [the longest x1 18.5 us: step_rows(): pl.pallas_call(lambda *refs: step_kernel(rows, points, *refs), out_shape=...]
    ppermute x8 -> x24, waiting for transfers between devices: 6.98 us -> 36.4 us  [the longest x7 18.4 us: per_device(): lax.ppermute(parts[k], 'grid', [(i, i ^ k * columns) for i in range(grid_...]
    unnamed x0 -> x1, blocking collectives: none -> 18.7 us
    reshape x1 -> x0, local copies, waits for them, and re-layouts: 14.5 us -> none  [finish(): shaped = share_part.reshape(row_count, MLEN, MLEN, MLEN, last_share)]
    mul x1 -> x0, local copies, waits for them, and re-layouts: 9.02 us -> none  [per_device(): jnp.einsum('fp,rpl->rfl', inject_matrix(level_row, point_count, MLEN), su...]
    ppermute x8 -> x24, starting transfers between devices: 30.4 us -> 37.9 us  [the longest x6 19.4 us: per_device(): downs = [lax.ppermute(v, 'grid', minus) for v in downs]]
  transfers between devices with their start and end apart: 9 -> 24, of which waited for: 4 -> 10; matrix products, arithmetic and copies ran while one was open for 2% -> 4% of each run, Pallas kernels for 0% -> 8%
where the time goes in v1:
time: 140 us
  starting transfers between devices  37.9 us (27%)
  waiting for transfers between devices  36.4 us (26%)
  Pallas kernels  33.6 us (24%)
  blocking collectives  18.7 us (13%)
  local copies, waits for them, and re-layouts  7.82 us (6%)
  other arithmetic  3.26 us (2%)
  between operations  2.37 us (2%)
    ppermute x6, starting transfers between devices, per_device(): downs = [lax.ppermute(v, 'grid', minus) for v in downs]  19.4 us
    unnamed x1, blocking collectives  18.7 us
    pallas_call x1, Pallas kernels, step_rows(): pl.pallas_call(lambda *refs: step_kernel(rows, points, *refs), out_shape=...  18.5 us
    ppermute x7, waiting for transfers between devices, per_device(): lax.ppermute(parts[k], 'grid', [(i, i ^ k * columns) for i in range(grid_...  18.4 us
    pallas_call x5, Pallas kernels, fill(): pl.pallas_call(lambda *refs: fill_kernel(chunks, width, with_base, *refs)...  14.2 us
    ppermute x1, waiting for transfers between devices, per_device(): lax.ppermute(partial, 'grid', [(i, i ^ 1) for i in range(grid_size)])  9.71 us
    ppermute x7, starting transfers between devices, per_device(): lax.ppermute(parts[k], 'grid', [(i, i ^ k * columns) for i in range(grid_...  9.06 us
    ppermute x6, waiting for transfers between devices, per_device(): ups = [lax.ppermute(v, 'grid', plus) for v in ups]  8.32 us
  transfers between devices with their start and end apart: 24, of which 10 were waited for; matrix products, arithmetic and copies ran while one was open for 4% of the time, Pallas kernels for 8%

profile of v1, /device:TPU:6, one launch (start us, length us, event | category | flops | bytes accessed | tf_op | source)
XLA Modules:
  0.0 140.1 jit_solution(4802509381299279470)
XLA Ops:
  1.7 1.9 %collective-permute-start = (f32[4,64,128]{2,1,0:T(8,128)S(1)}, f32[4,64,128]{2,1,0:T(8,128)S(1)}, u32[]{:S(2)}, u32[]{:S(2)}) collective-permute-start(f32[4,64,128]{2,1,0:T(8,128)S(1)} %get-tuple-element.25), channel_id=1, source_target_pairs={{0,1},{1,2},{2,3},{3,4},{4,5},{5,6},{6,7},{7,8},{8,9},{9,10},{10,1... | collective-permute-start | bytes 393224 | tf_op jit(solution)/shard_map/ppermute | solution.py:328
  3.6 3.6 %collective-permute-start.1 = (f32[4,64,128]{2,1,0:T(8,128)S(1)}, f32[4,64,128]{2,1,0:T(8,128)S(1)}, u32[]{:S(2)}, u32[]{:S(2)}) collective-permute-start(f32[4,64,128]{2,1,0:T(8,128)S(1)} %get-tuple-element.24), channel_id=1, source_target_pairs={{1,0},{2,1},{3,2},{4,3},{5,4},{6,5},{7,6},{8,7},{9,8},{10,9},{11,1... | collective-permute-start | bytes 393224 | tf_op jit(solution)/shard_map/ppermute | solution.py:329
  8.0 1.3 dynamic-slice
  10.7 18.7 %all-reduce = s32[64]{0:T(128)S(1)} all-reduce(s32[64]{0:T(128)S(1)} %add_dynamic-update-slice_fusion), channel_id=2, replica_groups=mesh['grid'=16,'dom'=16] {'grid'}, use_global_device_ids=true, to_apply=%add | all-reduce | flops 64 | bytes 512
  34.1 18.5 %step_rows.1 = (f32[2048,128]{1,0:T(8,128)}, f32[256,128]{1,0:T(8,128)S(1)}, f32[256,128]{1,0:T(8,128)S(1)}, f32[256,128]{1,0:T(8,128)S(1)}, f32[256,128]{1,0:T(...) custom-call(s32[3]{0:T(128)S(1)} %pad_add_fusion.refs_0_, ...), custom_call_target="tpu_custom_call" | custom-call | flops 32768000 | bytes 4194304 | tf_op jit(solution)/shard_map/step_rows/pallas_call | solution.py:186
  53.7 1.5 %collective-permute-start.3 = (f32[256,128]{1,0:T(8,128)S(1)}, f32[256,128]{1,0:T(8,128)S(1)}, u32[]{:S(2)}, u32[]{:S(2)}) collective-permute-start(f32[256,128]{1,0:T(8,128)S(1)} %get-tuple-element.14), channel_id=1, source_target_pairs={{0,64},{16,80},{32,96},{48,112},{64,0},{80,16},{96,32},{112,48},{1... | collective-permute-start | bytes 393224 | tf_op jit(solution)/shard_map/ppermute | solution.py:334
  55.6 1.9 %collective-permute-start.4 = (f32[256,128]{1,0:T(8,128)S(1)}, f32[256,128]{1,0:T(8,128)S(1)}, u32[]{:S(2)}, u32[]{:S(2)}) collective-permute-start(f32[256,128]{1,0:T(8,128)S(1)} %get-tuple-element.15), channel_id=1, source_target_pairs={{0,96},{16,112},{32,64},{48,80},{64,32},{80,48},{96,0},{112,16},{1... | collective-permute-start | bytes 393224 | tf_op jit(solution)/shard_map/ppermute | solution.py:334
  57.5 1.4 %collective-permute-start.5 = (f32[256,128]{1,0:T(8,128)S(1)}, f32[256,128]{1,0:T(8,128)S(1)}, u32[]{:S(2)}, u32[]{:S(2)}) collective-permute-start(f32[256,128]{1,0:T(8,128)S(1)} %get-tuple-element.16), channel_id=1, source_target_pairs={{0,128},{16,144},{32,160},{48,176},{64,192},{80,208},{96,224},{112... | collective-permute-start | bytes 393224 | tf_op jit(solution)/shard_map/ppermute | solution.py:334
  59.0 3.1 %collective-permute-start.6 = (f32[256,128]{1,0:T(8,128)S(1)}, f32[256,128]{1,0:T(8,128)S(1)}, u32[]{:S(2)}, u32[]{:S(2)}) collective-permute-start(f32[256,128]{1,0:T(8,128)S(1)} %get-tuple-element.17), channel_id=1, source_target_pairs={{0,160},{16,176},{32,128},{48,144},{64,224},{80,240},{96,192},{112... | collective-permute-start | bytes 393224 | tf_op jit(solution)/shard_map/ppermute | solution.py:334
  62.1 10.3 %collective-permute-done.3.refs_3_ = f32[256,128]{1,0:T(8,128)S(1)} collective-permute-done((f32[256,128]{1,0:T(8,128)S(1)}, f32[256,128]{1,0:T(8,128)S(1)}, u32[]{:S(2)}, u32[]{:S(2)}) %collective-permute-start.3) | collective-permute-done | bytes 131104 | tf_op jit(solution)/shard_map/ppermute | solution.py:334
  72.4 1.5 %multiply_convert_fusion.refs_0_ = bf16[208,512]{1,0:T(8,128)(2,1)S(1)} fusion(s32[512]{0:T(512)S(1)} %get-tuple-element.29, s32[512]{0:T(512)S(1)} %get-tuple-element.30, s32[208]{0:T(256)} %constant.146.clone, s32[512]{0:T(512)S(1)} %get-tuple-element.31, s32[512]{0:T(512)S(1)} %broadcast_in_dim_reshape.13, s32[512]{0:T(512)S(1)} %get-tuple-element.32, ...), kind=kLoop, calls=%fused_computation.37 | loop fusion | flops 6602752 | bytes 238528 | tf_op jit(solution)/shard_map/convert_element_type | solution.py:310
  73.9 1.5 %collective-permute-done.6.refs_6_ = f32[256,128]{1,0:T(8,128)S(1)} collective-permute-done((f32[256,128]{1,0:T(8,128)S(1)}, f32[256,128]{1,0:T(8,128)S(1)}, u32[]{:S(2)}, u32[]{:S(2)}) %collective-permute-start.6) | collective-permute-done | bytes 131104 | tf_op jit(solution)/shard_map/ppermute | solution.py:334
  75.4 3.1 %collective-permute-done.7.refs_7_ = f32[256,128]{1,0:T(8,128)S(1)} collective-permute-done((f32[256,128]{1,0:T(8,128)S(1)}, f32[256,128]{1,0:T(8,128)S(1)}, u32[]{:S(2)}, u32[]{:S(2)}) %collective-permute-start.7) | collective-permute-done | bytes 131104 | tf_op jit(solution)/shard_map/ppermute | solution.py:334
  78.5 3.5 %collective-permute-done.8.refs_8_ = f32[256,128]{1,0:T(8,128)S(1)} collective-permute-done((f32[256,128]{1,0:T(8,128)S(1)}, f32[256,128]{1,0:T(8,128)S(1)}, u32[]{:S(2)}, u32[]{:S(2)}) %collective-permute-start.8) | collective-permute-done | bytes 131104 | tf_op jit(solution)/shard_map/ppermute | solution.py:334
  83.4 9.7 %collective-permute-done.9 = f32[4,208,128]{2,1,0:T(8,128)S(1)} collective-permute-done((f32[4,208,128]{2,1,0:T(8,128)S(1)}, f32[4,208,128]{2,1,0:T(8,128)S(1)}, u32[]{:S(2)}, u32[]{:S(2)}) %collective-permute-start.9) | collective-permute-done | bytes 426016 | tf_op jit(solution)/shard_map/ppermute | solution.py:341
  93.2 3.2 %collective-permute-start.14 = (f32[2,208,128]{2,1,0:T(8,128)S(1)}, f32[2,208,128]{2,1,0:T(8,128)S(1)}, u32[]{:S(2)}, u32[]{:S(2)}) collective-permute-start(f32[2,208,128]{2,1,0:T(8,128)S(1)} %get-tuple-element.26.refs_3_), channel_id=1, source_target_pairs={{32,0},{48,16},{64,32},{80,48},{96,64},{112,80},{128,96},{144,112}... | collective-permute-start | bytes 638984 | tf_op jit(solution)/shard_map/ppermute | solution.py:353
  96.5 3.2 %collective-permute-start.21 = (f32[2,208,128]{2,1,0:T(8,128)S(1)}, f32[2,208,128]{2,1,0:T(8,128)S(1)}, u32[]{:S(2)}, u32[]{:S(2)}) collective-permute-start(f32[2,208,128]{2,1,0:T(8,128)S(1)} %get-tuple-element.27.refs_2_), channel_id=1, source_target_pairs={{32,0},{48,16},{64,32},{80,48},{96,64},{112,80},{128,96},{144,112}... | collective-permute-start | bytes 638984 | tf_op jit(solution)/shard_map/ppermute | solution.py:353
  99.8 2.8 %collective-permute-done.10.refs_2_ = f32[2,208,128]{2,1,0:T(8,128)S(1)} collective-permute-done((f32[2,208,128]{2,1,0:T(8,128)S(1)}, f32[2,208,128]{2,1,0:T(8,128)S(1)}, u32[]{:S(2)}, u32[]{:S(2)}) %collective-permute-start.10) | collective-permute-done | bytes 213024 | tf_op jit(solution)/shard_map/ppermute | solution.py:352
  102.6 3.2 %collective-permute-start.15 = (f32[2,208,128]{2,1,0:T(8,128)S(1)}, f32[2,208,128]{2,1,0:T(8,128)S(1)}, u32[]{:S(2)}, u32[]{:S(2)}) collective-permute-start(f32[2,208,128]{2,1,0:T(8,128)S(1)} %collective-permute-done.14.refs_5_), channel_id=1, source_target_pairs={{32,0},{48,16},{64,32},{80,48},{96,64},{112,80},{128,96},{144,112}... | collective-permute-start | bytes 638984 | tf_op jit(solution)/shard_map/ppermute | solution.py:353
  105.9 1.2 collective-permute-done.18.refs_3_
  107.1 3.2 %collective-permute-start.22 = (f32[2,208,128]{2,1,0:T(8,128)S(1)}, f32[2,208,128]{2,1,0:T(8,128)S(1)}, u32[]{:S(2)}, u32[]{:S(2)}) collective-permute-start(f32[2,208,128]{2,1,0:T(8,128)S(1)} %collective-permute-done.21.refs_4_), channel_id=1, source_target_pairs={{32,0},{48,16},{64,32},{80,48},{96,64},{112,80},{128,96},{144,112}... | collective-permute-start | bytes 638984 | tf_op jit(solution)/shard_map/ppermute | solution.py:353
  110.4 1.5 %collective-permute-done.11.refs_2_ = f32[2,208,128]{2,1,0:T(8,128)S(1)} collective-permute-done((f32[2,208,128]{2,1,0:T(8,128)S(1)}, f32[2,208,128]{2,1,0:T(8,128)S(1)}, u32[]{:S(2)}, u32[]{:S(2)}) %collective-permute-start.11) | collective-permute-done | bytes 213024 | tf_op jit(solution)/shard_map/ppermute | solution.py:352
  112.0 3.2 %collective-permute-start.16 = (f32[2,208,128]{2,1,0:T(8,128)S(1)}, f32[2,208,128]{2,1,0:T(8,128)S(1)}, u32[]{:S(2)}, u32[]{:S(2)}) collective-permute-start(f32[2,208,128]{2,1,0:T(8,128)S(1)} %collective-permute-done.15.refs_5_), channel_id=1, source_target_pairs={{32,0},{48,16},{64,32},{80,48},{96,64},{112,80},{128,96},{144,112}... | collective-permute-start | bytes 638984 | tf_op jit(solution)/shard_map/ppermute | solution.py:353
  115.3 1.2 collective-permute-done.19.refs_3_
  116.5 3.2 %collective-permute-start.23 = (f32[2,208,128]{2,1,0:T(8,128)S(1)}, f32[2,208,128]{2,1,0:T(8,128)S(1)}, u32[]{:S(2)}, u32[]{:S(2)}) collective-permute-start(f32[2,208,128]{2,1,0:T(8,128)S(1)} %collective-permute-done.22.refs_4_), channel_id=1, source_target_pairs={{32,0},{48,16},{64,32},{80,48},{96,64},{112,80},{128,96},{144,112}... | collective-permute-start | bytes 638984 | tf_op jit(solution)/shard_map/ppermute | solution.py:353
  119.8 1.5 %collective-permute-done.12.refs_2_ = f32[2,208,128]{2,1,0:T(8,128)S(1)} collective-permute-done((f32[2,208,128]{2,1,0:T(8,128)S(1)}, f32[2,208,128]{2,1,0:T(8,128)S(1)}, u32[]{:S(2)}, u32[]{:S(2)}) %collective-permute-start.12) | collective-permute-done | bytes 213024 | tf_op jit(solution)/shard_map/ppermute | solution.py:352
  121.4 3.2 %collective-permute-start.17 = (f32[2,208,128]{2,1,0:T(8,128)S(1)}, f32[2,208,128]{2,1,0:T(8,128)S(1)}, u32[]{:S(2)}, u32[]{:S(2)}) collective-permute-start(f32[2,208,128]{2,1,0:T(8,128)S(1)} %collective-permute-done.16.refs_5_), channel_id=1, source_target_pairs={{32,0},{48,16},{64,32},{80,48},{96,64},{112,80},{128,96},{144,112}... | collective-permute-start | bytes 638984 | tf_op jit(solution)/shard_map/ppermute | solution.py:358
  125.6 2.3 %fill.5.refs_6_ = f32[32,512,128]{2,1,0:T(8,128)} custom-call(s32[2]{0:T(128)S(1)} %pad_add_fusion.5.refs_0_, bf16[512,208]{1,0:T(8,128)(2,1)S(1)} %copy-done, f32[2,208,128]{2,1,0:T(8,128)S(1)} %get-tuple-element.27.refs_2_, f32[2,208,128]{2,1,0:T(8,128)S(1)} %get-tuple-element.26.refs_3_), custom_call_target="tpu_custom_call" | custom-call | flops 327155712 | bytes 1474560 | tf_op jit(solution)/shard_map/fill/pallas_call | solution.py:271
  127.9 3.2 %fill.6.refs_6_ = f32[32,512,128]{2,1,0:T(8,128)} custom-call(s32[4]{0:T(128)S(1)} %pad_add_fusion.4.refs_0_, bf16[512,208]{1,0:T(8,128)(2,1)S(1)} %copy-done.1, f32[2,208,128]{2,1,0:T(8,128)S(1)} %collective-permute-done.10.refs_2_, f32[2,208,128]{2,1,0:T(8,128)S(1)} %collective-permute-done.18.refs_3_, ...), custom_call_target="tpu_custom_call", output_to_operand_aliasing={{}: (6, {})} | custom-call | flops 654311424 | bytes 2949120 | tf_op jit(solution)/shard_map/fill/pallas_call | solution.py:271
  131.1 3.2 %fill.7.refs_6_ = f32[32,512,128]{2,1,0:T(8,128)} custom-call(s32[4]{0:T(128)S(1)} %pad_add_fusion.3.refs_0_, bf16[512,208]{1,0:T(8,128)(2,1)S(1)} %copy-done.1, f32[2,208,128]{2,1,0:T(8,128)S(1)} %collective-permute-done.11.refs_2_, f32[2,208,128]{2,1,0:T(8,128)S(1)} %collective-permute-done.19.refs_3_, ...), custom_call_target="tpu_custom_call", output_to_operand_aliasing={{}: (6, {})} | custom-call | flops 654311424 | bytes 2949120 | tf_op jit(solution)/shard_map/fill/pallas_call | solution.py:271
  134.3 3.2 %fill.8.refs_4_ = f32[32,512,128]{2,1,0:T(8,128)} custom-call(s32[4]{0:T(128)S(1)} %pad_add_fusion.2.refs_0_, bf16[512,208]{1,0:T(8,128)(2,1)S(1)} %copy-done.1, f32[2,208,128]{2,1,0:T(8,128)S(1)} %collective-permute-done.12.refs_2_, f32[2,208,128]{2,1,0:T(8,128)S(1)} %collective-permute-done.20.refs_3_, ...), custom_call_target="tpu_custom_call", output_to_operand_aliasing={{}: (6, {})} | custom-call | flops 654311424 | bytes 2949120 | tf_op jit(solution)/shard_map/fill/pallas_call | solution.py:271
  137.5 2.3 %fill.9 = f32[32,512,128]{2,1,0:T(8,128)} custom-call(s32[2]{0:T(128)S(1)} %pad_add_fusion.1.refs_0_, bf16[512,208]{1,0:T(8,128)(2,1)S(1)} %copy-done.1, f32[2,208,128]{2,1,0:T(8,128)S(1)} %collective-permute-done.13.refs_2_, f32[2,208,128]{2,1,0:T(8,128)S(1)} %collective-permute-done.17.refs_3_, ...), custom_call_target="tpu_custom_call", output_to_operand_aliasing={{}: (4, {})} | custom-call | flops 327155712 | bytes 1474560 | tf_op jit(solution)/shard_map/fill/pallas_call | solution.py:271
  (67 shorter events, 10.9 us)
Async XLA Ops:
  0.6 127.3 %copy-start.1 = (bf16[512,208]{1,0:T(8,128)(2,1)S(1)}, bf16[512,208]{1,0:T(8,128)(2,1)}, u32[]{:S(2)}) copy-start(bf16[512,208]{1,0:T(8,128)(2,1)} %constant.147.clone.refs_1_) | copy-start | bytes 638980
  1.7 29.2 %collective-permute-start = (f32[4,64,128]{2,1,0:T(8,128)S(1)}, f32[4,64,128]{2,1,0:T(8,128)S(1)}, u32[]{:S(2)}, u32[]{:S(2)}) collective-permute-start(f32[4,64,128]{2,1,0:T(8,128)S(1)} %get-tuple-element.25), channel_id=1, source_target_pairs={{0,1},{1,2},{2,3},{3,4},{4,5},{5,6},{6,7},{7,8},{8,9},{9,10},{10,1... | collective-permute-start | bytes 393224 | tf_op jit(solution)/shard_map/ppermute | solution.py:328
  3.6 27.3 %collective-permute-start.1 = (f32[4,64,128]{2,1,0:T(8,128)S(1)}, f32[4,64,128]{2,1,0:T(8,128)S(1)}, u32[]{:S(2)}, u32[]{:S(2)}) collective-permute-start(f32[4,64,128]{2,1,0:T(8,128)S(1)} %get-tuple-element.24), channel_id=1, source_target_pairs={{1,0},{2,1},{3,2},{4,3},{5,4},{6,5},{7,6},{8,7},{9,8},{10,9},{11,1... | collective-permute-start | bytes 393224 | tf_op jit(solution)/shard_map/ppermute | solution.py:329
  30.9 1.2 copy-start.2
  32.1 0.7 copy-start.3
  32.8 0.7 copy-start.4
  33.4 0.7 copy-start.5
  52.6 9.5 %collective-permute-start.2 = (f32[256,128]{1,0:T(8,128)S(1)}, f32[256,128]{1,0:T(8,128)S(1)}, u32[]{:S(2)}, u32[]{:S(2)}) collective-permute-start(f32[256,128]{1,0:T(8,128)S(1)} %get-tuple-element.13), channel_id=1, source_target_pairs={{0,32},{16,48},{32,0},{48,16},{64,96},{80,112},{96,64},{112,80},{1... | collective-permute-start | bytes 393224 | tf_op jit(solution)/shard_map/ppermute | solution.py:334
  53.7 18.7 %collective-permute-start.3 = (f32[256,128]{1,0:T(8,128)S(1)}, f32[256,128]{1,0:T(8,128)S(1)}, u32[]{:S(2)}, u32[]{:S(2)}) collective-permute-start(f32[256,128]{1,0:T(8,128)S(1)} %get-tuple-element.14), channel_id=1, source_target_pairs={{0,64},{16,80},{32,96},{48,112},{64,0},{80,16},{96,32},{112,48},{1... | collective-permute-start | bytes 393224 | tf_op jit(solution)/shard_map/ppermute | solution.py:334
  55.6 18.3 %collective-permute-start.4 = (f32[256,128]{1,0:T(8,128)S(1)}, f32[256,128]{1,0:T(8,128)S(1)}, u32[]{:S(2)}, u32[]{:S(2)}) collective-permute-start(f32[256,128]{1,0:T(8,128)S(1)} %get-tuple-element.15), channel_id=1, source_target_pairs={{0,96},{16,112},{32,64},{48,80},{64,32},{80,48},{96,0},{112,16},{1... | collective-permute-start | bytes 393224 | tf_op jit(solution)/shard_map/ppermute | solution.py:334
  57.5 16.4 %collective-permute-start.5 = (f32[256,128]{1,0:T(8,128)S(1)}, f32[256,128]{1,0:T(8,128)S(1)}, u32[]{:S(2)}, u32[]{:S(2)}) collective-permute-start(f32[256,128]{1,0:T(8,128)S(1)} %get-tuple-element.16), channel_id=1, source_target_pairs={{0,128},{16,144},{32,160},{48,176},{64,192},{80,208},{96,224},{112... | collective-permute-start | bytes 393224 | tf_op jit(solution)/shard_map/ppermute | solution.py:334
  59.0 16.4 %collective-permute-start.6 = (f32[256,128]{1,0:T(8,128)S(1)}, f32[256,128]{1,0:T(8,128)S(1)}, u32[]{:S(2)}, u32[]{:S(2)}) collective-permute-start(f32[256,128]{1,0:T(8,128)S(1)} %get-tuple-element.17), channel_id=1, source_target_pairs={{0,160},{16,176},{32,128},{48,144},{64,224},{80,240},{96,192},{112... | collective-permute-start | bytes 393224 | tf_op jit(solution)/shard_map/ppermute | solution.py:334
  62.1 16.4 %collective-permute-start.7 = (f32[256,128]{1,0:T(8,128)S(1)}, f32[256,128]{1,0:T(8,128)S(1)}, u32[]{:S(2)}, u32[]{:S(2)}) collective-permute-start(f32[256,128]{1,0:T(8,128)S(1)} %get-tuple-element.18), channel_id=1, source_target_pairs={{0,192},{16,208},{32,224},{48,240},{64,128},{80,144},{96,160},{112... | collective-permute-start | bytes 393224 | tf_op jit(solution)/shard_map/ppermute | solution.py:334
  72.4 9.6 %collective-permute-start.8 = (f32[256,128]{1,0:T(8,128)S(1)}, f32[256,128]{1,0:T(8,128)S(1)}, u32[]{:S(2)}, u32[]{:S(2)}) collective-permute-start(f32[256,128]{1,0:T(8,128)S(1)} %get-tuple-element.19), channel_id=1, source_target_pairs={{0,224},{16,240},{32,192},{48,208},{64,160},{80,176},{96,128},{112... | collective-permute-start | bytes 393224 | tf_op jit(solution)/shard_map/ppermute | solution.py:334
  82.9 10.2 %collective-permute-start.9 = (f32[4,208,128]{2,1,0:T(8,128)S(1)}, f32[4,208,128]{2,1,0:T(8,128)S(1)}, u32[]{:S(2)}, u32[]{:S(2)}) collective-permute-start(f32[4,208,128]{2,1,0:T(8,128)S(1)} %combine.1), channel_id=1, source_target_pairs={{0,16},{16,0},{32,48},{48,32},{64,80},{80,64},{96,112},{112,96},{1... | collective-permute-start | bytes 1277960 | tf_op jit(solution)/shard_map/ppermute | solution.py:341
  93.1 9.4 %collective-permute-start.10 = (f32[2,208,128]{2,1,0:T(8,128)S(1)}, f32[2,208,128]{2,1,0:T(8,128)S(1)}, u32[]{:S(2)}, u32[]{:S(2)}) collective-permute-start(f32[2,208,128]{2,1,0:T(8,128)S(1)} %get-tuple-element.27.refs_2_), channel_id=1, source_target_pairs={{0,32},{16,48},{32,64},{48,80},{64,96},{80,112},{96,128},{112,144}... | collective-permute-start | bytes 638984 | tf_op jit(solution)/shard_map/ppermute | solution.py:352
  93.2 9.3 %collective-permute-start.14 = (f32[2,208,128]{2,1,0:T(8,128)S(1)}, f32[2,208,128]{2,1,0:T(8,128)S(1)}, u32[]{:S(2)}, u32[]{:S(2)}) collective-permute-start(f32[2,208,128]{2,1,0:T(8,128)S(1)} %get-tuple-element.26.refs_3_), channel_id=1, source_target_pairs={{32,0},{48,16},{64,32},{80,48},{96,64},{112,80},{128,96},{144,112}... | collective-permute-start | bytes 638984 | tf_op jit(solution)/shard_map/ppermute | solution.py:353
  96.5 10.7 %collective-permute-start.18 = (f32[2,208,128]{2,1,0:T(8,128)S(1)}, f32[2,208,128]{2,1,0:T(8,128)S(1)}, u32[]{:S(2)}, u32[]{:S(2)}) collective-permute-start(f32[2,208,128]{2,1,0:T(8,128)S(1)} %get-tuple-element.26.refs_3_), channel_id=1, source_target_pairs={{0,32},{16,48},{32,64},{48,80},{64,96},{80,112},{96,128},{112,144}... | collective-permute-start | bytes 638984 | tf_op jit(solution)/shard_map/ppermute | solution.py:352
  96.5 10.7 %collective-permute-start.21 = (f32[2,208,128]{2,1,0:T(8,128)S(1)}, f32[2,208,128]{2,1,0:T(8,128)S(1)}, u32[]{:S(2)}, u32[]{:S(2)}) collective-permute-start(f32[2,208,128]{2,1,0:T(8,128)S(1)} %get-tuple-element.27.refs_2_), channel_id=1, source_target_pairs={{32,0},{48,16},{64,32},{80,48},{96,64},{112,80},{128,96},{144,112}... | collective-permute-start | bytes 638984 | tf_op jit(solution)/shard_map/ppermute | solution.py:353
  102.6 9.4 %collective-permute-start.11 = (f32[2,208,128]{2,1,0:T(8,128)S(1)}, f32[2,208,128]{2,1,0:T(8,128)S(1)}, u32[]{:S(2)}, u32[]{:S(2)}) collective-permute-start(f32[2,208,128]{2,1,0:T(8,128)S(1)} %collective-permute-done.10.refs_2_), channel_id=1, source_target_pairs={{0,32},{16,48},{32,64},{48,80},{64,96},{80,112},{96,128},{112,144}... | collective-permute-start | bytes 638984 | tf_op jit(solution)/shard_map/ppermute | solution.py:352
  102.6 9.4 %collective-permute-start.15 = (f32[2,208,128]{2,1,0:T(8,128)S(1)}, f32[2,208,128]{2,1,0:T(8,128)S(1)}, u32[]{:S(2)}, u32[]{:S(2)}) collective-permute-start(f32[2,208,128]{2,1,0:T(8,128)S(1)} %collective-permute-done.14.refs_5_), channel_id=1, source_target_pairs={{32,0},{48,16},{64,32},{80,48},{96,64},{112,80},{128,96},{144,112}... | collective-permute-start | bytes 638984 | tf_op jit(solution)/shard_map/ppermute | solution.py:353
  107.1 9.4 %collective-permute-start.19 = (f32[2,208,128]{2,1,0:T(8,128)S(1)}, f32[2,208,128]{2,1,0:T(8,128)S(1)}, u32[]{:S(2)}, u32[]{:S(2)}) collective-permute-start(f32[2,208,128]{2,1,0:T(8,128)S(1)} %collective-permute-done.18.refs_3_), channel_id=1, source_target_pairs={{0,32},{16,48},{32,64},{48,80},{64,96},{80,112},{96,128},{112,144}... | collective-permute-start | bytes 638984 | tf_op jit(solution)/shard_map/ppermute | solution.py:352
  107.1 9.4 %collective-permute-start.22 = (f32[2,208,128]{2,1,0:T(8,128)S(1)}, f32[2,208,128]{2,1,0:T(8,128)S(1)}, u32[]{:S(2)}, u32[]{:S(2)}) collective-permute-start(f32[2,208,128]{2,1,0:T(8,128)S(1)} %collective-permute-done.21.refs_4_), channel_id=1, source_target_pairs={{32,0},{48,16},{64,32},{80,48},{96,64},{112,80},{128,96},{144,112}... | collective-permute-start | bytes 638984 | tf_op jit(solution)/shard_map/ppermute | solution.py:353
  112.0 9.4 %collective-permute-start.12 = (f32[2,208,128]{2,1,0:T(8,128)S(1)}, f32[2,208,128]{2,1,0:T(8,128)S(1)}, u32[]{:S(2)}, u32[]{:S(2)}) collective-permute-start(f32[2,208,128]{2,1,0:T(8,128)S(1)} %collective-permute-done.11.refs_2_), channel_id=1, source_target_pairs={{0,32},{16,48},{32,64},{48,80},{64,96},{80,112},{96,128},{112,144}... | collective-permute-start | bytes 638984 | tf_op jit(solution)/shard_map/ppermute | solution.py:352
  112.0 9.4 %collective-permute-start.16 = (f32[2,208,128]{2,1,0:T(8,128)S(1)}, f32[2,208,128]{2,1,0:T(8,128)S(1)}, u32[]{:S(2)}, u32[]{:S(2)}) collective-permute-start(f32[2,208,128]{2,1,0:T(8,128)S(1)} %collective-permute-done.15.refs_5_), channel_id=1, source_target_pairs={{32,0},{48,16},{64,32},{80,48},{96,64},{112,80},{128,96},{144,112}... | collective-permute-start | bytes 638984 | tf_op jit(solution)/shard_map/ppermute | solution.py:353
  116.5 17.8 %collective-permute-start.20 = (f32[2,208,128]{2,1,0:T(8,128)S(1)}, f32[2,208,128]{2,1,0:T(8,128)S(1)}, u32[]{:S(2)}, u32[]{:S(2)}) collective-permute-start(f32[2,208,128]{2,1,0:T(8,128)S(1)} %collective-permute-done.19.refs_3_), channel_id=1, source_target_pairs={{0,32},{16,48},{32,64},{48,80},{64,96},{80,112},{96,128},{112,144}... | collective-permute-start | bytes 638984 | tf_op jit(solution)/shard_map/ppermute | solution.py:352
  116.5 17.8 %collective-permute-start.23 = (f32[2,208,128]{2,1,0:T(8,128)S(1)}, f32[2,208,128]{2,1,0:T(8,128)S(1)}, u32[]{:S(2)}, u32[]{:S(2)}) collective-permute-start(f32[2,208,128]{2,1,0:T(8,128)S(1)} %collective-permute-done.22.refs_4_), channel_id=1, source_target_pairs={{32,0},{48,16},{64,32},{80,48},{96,64},{112,80},{128,96},{144,112}... | collective-permute-start | bytes 638984 | tf_op jit(solution)/shard_map/ppermute | solution.py:353
  121.4 16.2 %collective-permute-start.13 = (f32[2,208,128]{2,1,0:T(8,128)S(1)}, f32[2,208,128]{2,1,0:T(8,128)S(1)}, u32[]{:S(2)}, u32[]{:S(2)}) collective-permute-start(f32[2,208,128]{2,1,0:T(8,128)S(1)} %collective-permute-done.12.refs_2_), channel_id=1, source_target_pairs={{0,32},{16,48},{32,64},{48,80},{64,96},{80,112},{96,128},{112,144}... | collective-permute-start | bytes 638984 | tf_op jit(solution)/shard_map/ppermute | solution.py:358
  121.4 16.2 %collective-permute-start.17 = (f32[2,208,128]{2,1,0:T(8,128)S(1)}, f32[2,208,128]{2,1,0:T(8,128)S(1)}, u32[]{:S(2)}, u32[]{:S(2)}) collective-permute-start(f32[2,208,128]{2,1,0:T(8,128)S(1)} %collective-permute-done.16.refs_5_), channel_id=1, source_target_pairs={{32,0},{48,16},{64,32},{80,48},{96,64},{112,80},{128,96},{144,112}... | collective-permute-start | bytes 638984 | tf_op jit(solution)/shard_map/ppermute | solution.py:358
  124.6 0.9 copy-start

commit v2 on v1

v2 whole, which is shorter than its diff:
```python
import itertools

import jax
import jax.numpy as jnp
import numpy as np
from jax import lax
from jax.experimental import pallas as pl
from jax.experimental.pallas import tpu as pltpu
from jax.sharding import PartitionSpec as P

STEPS = 4
MLEN = 8
FINEST = 3
LEVEL_SUM = 6
ZLEN = 8


def rank_of(coordinate):
    if coordinate % 4 == 0:
        return 1
    return 2 if coordinate % 2 == 0 else 3


def union_points():
    points = []
    for first in (0, 4, 2, 6, 1, 3, 5, 7):
        for second, third in itertools.product(range(MLEN), repeat=2):
            if rank_of(first) + rank_of(second) + rank_of(third) <= LEVEL_SUM:
                points.append((first, second, third))
    return np.array(points, np.int32)


POINTS = union_points()
COUNT = len(POINTS)
SUB = 64
META = 8
TRIPLES = ((1, 2), (1, 3), (2, 1), (2, 2), (2, 3), (3, 1), (3, 2))
GROUPS = (((0, 48), (0,)), ((48, 96), (4,)), ((96, 160), (2, 6)), ((160, 208), (1, 3, 5, 7)))


def nodal_matrix(length_dim):
    matrix = np.eye(length_dim)
    stride = length_dim // 2
    while stride >= 1:
        for position in range(stride, length_dim, 2 * stride):
            matrix[position] = matrix[position] + 0.5 * matrix[position - stride]
            if position + stride < length_dim:
                matrix[position] = matrix[position] + 0.5 * matrix[position + stride]
        stride = stride // 2
    return matrix


def fill_matrix():
    nodal = nodal_matrix(MLEN)
    square = MLEN**2
    matrix = np.zeros((MLEN, MLEN, MLEN, COUNT))
    for column, (first, second, third) in enumerate(POINTS):
        matrix[first, :, :, column] = np.outer(nodal[:, second], nodal[:, third])
    matrix = matrix.reshape(MLEN, square, COUNT)
    packed = np.zeros((MLEN * square, 256))
    begin = 0
    for (low, high), members in GROUPS:
        block = matrix[list(members), :, low:high].reshape(-1, high - low)
        packed[begin : begin + len(block), : 3 * (high - low)] = np.tile(block, (1, 3))
        begin += len(block)
    return packed

def placing_table():
    tables = []
    for first, second in TRIPLES:
        level = (first, second, LEVEL_SUM - first - second)
        length = [2**v for v in level]
        surplus = np.ones((1, 1))
        for n in length:
            surplus = np.kron(surplus, np.round(2.0 * np.linalg.inv(nodal_matrix(n))) / 2.0)
        target = np.zeros((COUNT, SUB))
        for column, coords in enumerate(itertools.product(*[range(n) for n in length])):
            point = [c * (MLEN // n) for c, n in zip(coords, length)]
            target[np.all(POINTS == point, axis=1), column] = 1.0
        tables.append(np.tile(target @ surplus, (1, 3)))
    return np.stack(tables)


def split_three(values):
    high = values.astype(jnp.bfloat16)
    rest = values - high.astype(jnp.float32)
    middle = rest.astype(jnp.bfloat16)
    low = (rest - middle.astype(jnp.float32)).astype(jnp.bfloat16)
    return high, middle, low


def step_kernel(rows, points, facts_ref, start_ref, before_ref, after_ref, stepped_ref, *rest):
    parts = rest[: 2 * ZLEN]
    first, second, final, coef_ref, load_sem, store_sem = rest[2 * ZLEN :]
    halo = STEPS
    share = rows // ZLEN
    half = share // 2 * points
    block = 2 * half + META
    loads = [
        pltpu.make_async_copy(before_ref, first.at[pl.ds(0, halo * points)], load_sem.at[0]),
        pltpu.make_async_copy(start_ref, first.at[pl.ds(halo * points, rows * points)], load_sem.at[1]),
        pltpu.make_async_copy(
            after_ref, first.at[pl.ds((halo + rows) * points, halo * points)], load_sem.at[2]
        ),
    ]
    for load in loads:
        load.start()

    member = facts_ref[0].astype(jnp.int32)
    keep_low, keep_high = facts_ref[1], facts_ref[2]
    levels = [facts_ref[3 + dim].astype(jnp.int32) for dim in range(3)]
    weight = facts_ref[6]
    spread = [facts_ref[7 + dim] for dim in range(5)]
    drift = [0.5 * facts_ref[12 + dim] for dim in range(5)]

    place = lax.broadcasted_iota(jnp.int32, (points, 128), 0)
    lane = lax.broadcasted_iota(jnp.int32, (8, 128), 1)
    sublane = lax.broadcasted_iota(jnp.int32, (META, 128), 0)
    offsets = [levels[1] + levels[2], levels[2], jnp.int32(0)]
    strides = []
    centre_rate = 1.0 - 2.0 * spread[0] - 2.0 * spread[4]
    for dim in range(3):
        length = jnp.left_shift(jnp.int32(1), levels[dim])
        coord = jnp.bitwise_and(jnp.right_shift(place, offsets[dim]), length - 1)
        coef_ref[2 * dim] = jnp.where(coord < length - 1, spread[dim + 1] + drift[dim + 1], 0.0)
        coef_ref[2 * dim + 1] = jnp.where(coord > 0, spread[dim + 1] - drift[dim + 1], 0.0)
        strides.append(jnp.left_shift(jnp.int32(1), offsets[dim]))
        centre_rate = centre_rate - 2.0 * spread[dim + 1]
    row_up, row_down = spread[0] + drift[0], spread[0] - drift[0]
    lane_up = jnp.where(lane < 127, spread[4] + drift[4], 0.0)
    lane_down = jnp.where(lane > 0, spread[4] - drift[4], 0.0)
    triple = (3 * levels[0] + levels[1] - 5).astype(jnp.float32)
    for group in range(ZLEN):
        final[group * block + half : group * block + half + META, :] = jnp.where(
            sublane == 0, triple, weight
        )

    for load in loads:
        load.wait()

    def advance(source, target, step, locate):
        low, high = step, 2 * halo + rows - step

        def tile(tile_index, carry):
            base = pl.multiple_of(tile_index * 8, 8)
            coefs = [coef_ref[i, pl.ds(base, 8), :] for i in range(6)]

            def at(row):
                return source[pl.ds(pl.multiple_of(row * points + base, 8), 8), :]

            below, centre = at(low - 1), at(low)
            for row in range(low, high):
                above = at(row + 1)
                offset = row * points + base
                total = centre * centre_rate + above * row_up + below * row_down
                total = total + pltpu.roll(centre, 127, 1) * lane_up
                total = total + pltpu.roll(centre, 1, 1) * lane_down
                for dim in range(3):
                    total = total + source[pl.ds(offset + strides[dim], 8), :] * coefs[2 * dim]
                    total = total + source[pl.ds(offset - strides[dim], 8), :] * coefs[2 * dim + 1]
                if row < halo:
                    total = total * keep_low
                if row >= halo + rows:
                    total = total * keep_high
                target[pl.ds(pl.multiple_of(locate(row) + base, 8), 8), :] = total
                below, centre = centre, above
            return carry

        lax.fori_loop(0, points // 8, tile, 0, unroll=2)

    def located(row):
        group, inner = divmod(row - halo, share)
        return group * block + inner * points + (META if inner >= share // 2 else 0)

    advance(first, second, 1, lambda row: row * points)
    advance(second, first, 2, lambda row: row * points)
    advance(first, second, 3, lambda row: row * points)
    advance(second, final, 4, located)

    stores = []
    for index in range(ZLEN):
        begin = pl.multiple_of(jnp.bitwise_xor(member, index) * block, 8)
        stores.append((final.at[pl.ds(begin, half + META)], parts[index]))
    for index in range(ZLEN):
        begin = pl.multiple_of(jnp.bitwise_xor(member, index) * block + half + META, 8)
        stores.append((final.at[pl.ds(begin, half)], parts[ZLEN + index]))
    for index in range(2 * ZLEN):
        begin = index // 2 * block + index % 2 * (half + META)
        stores.append(
            (final.at[pl.ds(begin, half)], stepped_ref.at[pl.ds(index * half, half)])
        )
    copies = [
        pltpu.make_async_copy(source, target, store_sem.at[index])
        for index, (source, target) in enumerate(stores)
    ]
    for copy in copies:
        copy.start()
    for copy in copies:
        copy.wait()


def step_rows(facts, start, before, after):
    rows, points, lanes = start.shape
    half = rows // ZLEN // 2 * points
    flat = lambda v: v.reshape(-1, lanes)
    anywhere = pl.BlockSpec(memory_space=pl.ANY)
    total = rows + 2 * STEPS
    outs = pl.pallas_call(
        lambda *refs: step_kernel(rows, points, *refs),
        out_shape=[jax.ShapeDtypeStruct((rows * points, lanes), jnp.float32)]
        + [jax.ShapeDtypeStruct((half + META, lanes), jnp.float32)] * ZLEN
        + [jax.ShapeDtypeStruct((half, lanes), jnp.float32)] * ZLEN,
        in_specs=[pl.BlockSpec(memory_space=pltpu.SMEM)] + [anywhere] * 3,
        out_specs=[anywhere] * (1 + 2 * ZLEN),
        scratch_shapes=[
            pltpu.VMEM((total * points, lanes), jnp.float32),
            pltpu.VMEM((total * points, lanes), jnp.float32),
            pltpu.VMEM((ZLEN * (2 * half + META), lanes), jnp.float32),
            pltpu.VMEM((6, points, lanes), jnp.float32),
            pltpu.SemaphoreType.DMA((3,)),
            pltpu.SemaphoreType.DMA((4 * ZLEN,)),
        ],
        compiler_params=pltpu.CompilerParams(vmem_limit_bytes=24 * 2**20),
        cost_estimate=pl.CostEstimate(
            flops=25 * STEPS * total * points * lanes, bytes_accessed=16 * rows * points * lanes,
            transcendentals=0,
        ),
        name="step_rows",
    )(facts, flat(start), flat(before), flat(after))
    return outs[0].reshape(rows, points, lanes), outs[1 : 1 + ZLEN], outs[1 + ZLEN :]


def combine_kernel(grids, table_ref, *refs):
    headed, pieces, out_ref = refs[:ZLEN], refs[:-1][-ZLEN:], refs[-1]
    width, _, lanes = out_ref.shape
    half = width * SUB
    total = None
    for head, piece in zip(headed, pieces):
        triple = jnp.clip(jnp.max(head[half : half + 1, :]).astype(jnp.int32), 0, len(TRIPLES) - 1)
        scale = jnp.max(head[half + 1 : half + 2, :]) / grids
        wide = jnp.concatenate([piece[r * SUB : (r + 1) * SUB, :] for r in range(width)], axis=1)
        stack = jnp.concatenate(split_three(wide * scale), axis=0)
        term = jnp.dot(table_ref[triple], stack, preferred_element_type=jnp.float32)
        total = term if total is None else total + term
    for row in range(width):
        out_ref[row] = total[:, row * lanes : (row + 1) * lanes]


def combine(table, headed, pieces, width, grids):
    lanes = headed[0].shape[1]
    arrays = list(headed) + ([] if pieces is None else list(pieces))
    return pl.pallas_call(
        lambda *refs: combine_kernel(grids, *refs),
        out_shape=jax.ShapeDtypeStruct((width, COUNT, lanes), jnp.float32),
        compiler_params=pltpu.CompilerParams(vmem_limit_bytes=24 * 2**20),
        cost_estimate=pl.CostEstimate(
            flops=2 * ZLEN * 3 * SUB * COUNT * width * lanes, bytes_accessed=2**20, transcendentals=0
        ),
        name="combine",
    )(table, *arrays)


def fill_kernel(chunks, width, with_base, where_ref, matrix_ref, *refs):
    sources = refs[:chunks]
    out_ref, scratch, sems = refs[chunks + with_base :]
    square = MLEN**2
    copies = []
    for index, source in enumerate(sources):
        lanes = source.shape[2]
        parts = split_three(jnp.concatenate([source[row] for row in range(width)], axis=1))
        level = {}
        begin = 0
        for (low, high), members in GROUPS:
            block = matrix_ref[begin : begin + square * len(members), : 3 * (high - low)]
            stack = jnp.concatenate([part[low:high] for part in parts], axis=0)
            result = jnp.dot(block, stack, preferred_element_type=jnp.float32)
            for k, member in enumerate(members):
                level[member] = result[k * square : (k + 1) * square]
            begin += square * len(members)
        nodal = dict(level)
        nodal[4] = level[4] + 0.5 * nodal[0]
        nodal[2] = level[2] + 0.5 * (nodal[0] + nodal[4])
        nodal[6] = level[6] + 0.5 * nodal[4]
        for odd in (1, 3, 5):
            nodal[odd] = level[odd] + 0.5 * (nodal[odd - 1] + nodal[odd + 1])
        nodal[7] = level[7] + 0.5 * nodal[6]
        for row in range(width):
            for c in range(MLEN):
                scratch[index * width + row, c * square : (c + 1) * square, :] = nodal[c][
                    :, row * lanes : (row + 1) * lanes
                ]
        copy = pltpu.make_async_copy(
            scratch.at[pl.ds(index * width, width)],
            out_ref.at[pl.ds(where_ref[index], width)],
            sems.at[index],
        )
        copy.start()
        copies.append(copy)
    for copy in copies:
        copy.wait()


def fill(where, matrix, sources, rows, base):
    width, _, lanes = sources[0].shape
    chunks = len(sources)
    with_base = 0 if base is None else 1
    args = [where, matrix, *sources] + ([base] if with_base else [])
    anywhere = pl.BlockSpec(memory_space=pl.ANY)
    vector = pl.BlockSpec(memory_space=pltpu.VMEM)
    return pl.pallas_call(
        lambda *refs: fill_kernel(chunks, width, with_base, *refs),
        out_shape=jax.ShapeDtypeStruct((rows, MLEN**3, lanes), jnp.float32),
        in_specs=[pl.BlockSpec(memory_space=pltpu.SMEM)] + [vector] * (1 + chunks) + [anywhere] * with_base,
        out_specs=anywhere,
        input_output_aliases={2 + chunks: 0} if with_base else {},
        scratch_shapes=[
            pltpu.VMEM((chunks * width, MLEN**3, lanes), jnp.float32),
            pltpu.SemaphoreType.DMA((chunks,)),
        ],
        compiler_params=pltpu.CompilerParams(vmem_limit_bytes=24 * 2**20),
        cost_estimate=pl.CostEstimate(
            flops=6 * chunks * width * matrix.size * lanes,
            bytes_accessed=4 * chunks * width * (MLEN**3 + COUNT) * lanes,
            transcendentals=0,
        ),
        name="fill",
    )(*args)


def per_device(initial, diffusion, drift, levels, weights):
    values = initial[0]
    rows, points, _ = values.shape
    share = rows // ZLEN
    half = share // 2
    dom_size = lax.axis_size("dom")
    grid_size = lax.axis_size("grid")
    columns = grid_size // ZLEN
    dom = lax.axis_index("dom")
    z = lax.axis_index("grid") // columns
    swap = lambda v, bits: lax.ppermute(v, "grid", [(i, i ^ bits) for i in range(grid_size)])

    up = [(i, i + 1) for i in range(dom_size - 1)]
    down = [(j, i) for i, j in up]
    before = lax.ppermute(values[rows - STEPS :], "dom", up)
    after = lax.ppermute(values[:STEPS], "dom", down)
    place = jnp.stack([z, (dom > 0).astype(jnp.int32), (dom < dom_size - 1).astype(jnp.int32)])
    facts = jnp.concatenate([place, levels[0], weights]).astype(jnp.float32)
    facts = jnp.concatenate([facts, diffusion[0], drift[0]])
    stepped, headed, others = step_rows(facts, values, before, after)

    headed = [headed[0]] + [swap(headed[k], k * columns) for k in range(1, ZLEN)]
    others = [others[0]] + [swap(others[k], k * columns) for k in range(1, ZLEN)]
    table = jnp.asarray(placing_table(), jnp.bfloat16)
    sums = []
    for pieces in (None, others):
        partial = combine(table, headed, pieces, half, grid_size)
        sums.append(partial + swap(partial, 1))

    plus = [(i, (i + columns) % grid_size) for i in range(grid_size)]
    minus = [(j, i) for i, j in plus]
    matrix = jnp.asarray(fill_matrix(), jnp.bfloat16)
    begin = lambda source, part: source % ZLEN * share + part * half
    ups, downs = sums, sums
    chunks, where = list(sums), [begin(z, 0), begin(z, 1)]
    combined = None
    for hop in range(1, ZLEN // 2):
        next_ups = [lax.ppermute(v, "grid", plus) for v in ups]
        next_downs = [lax.ppermute(v, "grid", minus) for v in downs]
        if hop > 1:
            combined = fill(jnp.stack(where), matrix, chunks, rows, combined)
            chunks, where = [], []
            next_ups, next_downs, combined = lax.optimization_barrier(
                (next_ups, next_downs, combined)
            )
        ups, downs = next_ups, next_downs
        chunks = chunks + ups + downs
        where = where + [begin(z - hop + ZLEN, s) for s in range(2)]
        where = where + [begin(z + hop, s) for s in range(2)]
    last = [lax.ppermute(ups[0], "grid", plus), lax.ppermute(downs[1], "grid", minus)]
    combined = fill(jnp.stack(where), matrix, chunks, rows, combined)
    last, combined = lax.optimization_barrier((last, combined))
    where = [begin(z + ZLEN // 2, s) for s in range(2)]
    combined = fill(jnp.stack(where), matrix, last, rows, combined)
    return stepped[None], combined.reshape(rows, MLEN, MLEN, MLEN, -1)


def solution(mesh):
    in_specs = (
        P("grid", "dom", None, None),
        P("grid", None),
        P("grid", None),
        P("grid", None),
        P("grid"),
    )
    out_specs = (P("grid", "dom", None, None), P("dom", None, None, None, None))
    return jax.shard_map(
        per_device, mesh=mesh, in_specs=in_specs, out_specs=out_specs, check_vma=False
    )
```

time: 140 us -> 120 us (0.86); the launches traced: 140 us -> 118 us
  starting transfers between devices: 37.9 us -> 58.8 us
  blocking collectives: 18.7 us -> 0 us
  Pallas kernels: 33.6 us -> 19 us
  waiting for transfers between devices: 36.4 us -> 31.2 us
  other arithmetic: 3.26 us -> 1.04 us
  local copies, waits for them, and re-layouts: 7.82 us -> 6.27 us
    ppermute x20 -> x28, starting transfers between devices: 29.1 us -> 51.3 us  [the longest x16 32.4 us: per_device(): lax.ppermute(v, 'grid', [(i, i ^ bits) for i in range(grid_size)])]
    unnamed x1 -> x0, blocking collectives: 18.7 us -> none
    ppermute x20 -> x28, waiting for transfers between devices: 36.4 us -> 27.2 us  [the longest x16 18.9 us: per_device(): lax.ppermute(v, 'grid', [(i, i ^ bits) for i in range(grid_size)])]
    pallas_call x1, Pallas kernels: 18.5 us -> 9.42 us  [step_rows(): pl.pallas_call(lambda *refs: step_kernel(rows, points, *refs), out_shape=...]
    pallas_call x5 -> x4, Pallas kernels: 14.2 us -> 8.55 us  [fill(): pl.pallas_call(lambda *refs: fill_kernel(chunks, width, with_base, *refs)...]
    ppermute x1, waiting for transfers between devices: 0.01 us -> 1.97 us  [per_device(): before = lax.ppermute(values[rows - STEPS:], 'dom', up)]
    ppermute x1, starting transfers between devices: 3.24 us -> 1.49 us  [per_device(): lax.ppermute(downs[1], 'grid', minus)]
    ppermute x1, starting transfers between devices: 0.01 us -> 1.75 us  [per_device(): lax.ppermute(ups[0], 'grid', plus)]
  transfers between devices with their start and end apart: 24 -> 32, of which waited for: 10 -> 15; matrix products, arithmetic and copies ran while one was open for 4% -> 2% of each run, Pallas kernels for 8% -> 6%
where the time goes in v2:
time: 120 us; the launch traced here: 118 us
  starting transfers between devices  58.8 us (49%)
  waiting for transfers between devices  31.2 us (26%)
  Pallas kernels  19 us (16%)
  local copies, waits for them, and re-layouts  6.27 us (5%)
  between operations  1.59 us (1%)
    ppermute x16, starting transfers between devices, per_device(): lax.ppermute(v, 'grid', [(i, i ^ bits) for i in range(grid_size)])  32.4 us
    ppermute x16, waiting for transfers between devices, per_device(): lax.ppermute(v, 'grid', [(i, i ^ bits) for i in range(grid_size)])  18.9 us
    ppermute x6, starting transfers between devices, per_device(): next_downs = [lax.ppermute(v, 'grid', minus) for v in downs]  16.9 us
    pallas_call x1, Pallas kernels, step_rows(): pl.pallas_call(lambda *refs: step_kernel(rows, points, *refs), out_shape=...  9.42 us
    pallas_call x4, Pallas kernels, fill(): pl.pallas_call(lambda *refs: fill_kernel(chunks, width, with_base, *refs)...  8.55 us
    ppermute x6, waiting for transfers between devices, per_device(): next_ups = [lax.ppermute(v, 'grid', plus) for v in ups]  7.99 us
    unnamed x10, local copies, waits for them, and re-layouts  4.42 us
  transfers between devices with their start and end apart: 32, of which 15 were waited for; matrix products, arithmetic and copies ran while one was open for 2% of the time, Pallas kernels for 6%

profile of v2, /device:TPU:6, one launch (start us, length us, event | category | flops | bytes accessed | tf_op | source)
XLA Modules:
  0.0 117.9 jit_solution(17618571405543114113)
XLA Ops:
  1.7 2.2 %collective-permute-start.1 = (f32[4,64,128]{2,1,0:T(8,128)S(1)}, f32[4,64,128]{2,1,0:T(8,128)S(1)}, u32[]{:S(2)}, u32[]{:S(2)}) collective-permute-start(f32[4,64,128]{2,1,0:T(8,128)S(1)} %get-tuple-element.62), channel_id=1, source_target_pairs={{1,0},{2,1},{3,2},{4,3},{5,4},{6,5},{7,6},{8,7},{9,8},{10,9},{11,1... | collective-permute-start | bytes 393224 | tf_op jit(solution)/shard_map/ppermute | solution.py:345
  3.9 2.2 %collective-permute-start = (f32[4,64,128]{2,1,0:T(8,128)S(1)}, f32[4,64,128]{2,1,0:T(8,128)S(1)}, u32[]{:S(2)}, u32[]{:S(2)}) collective-permute-start(f32[4,64,128]{2,1,0:T(8,128)S(1)} %get-tuple-element.63), channel_id=1, source_target_pairs={{0,1},{1,2},{2,3},{3,4},{4,5},{5,6},{6,7},{7,8},{8,9},{9,10},{10,1... | collective-permute-start | bytes 393224 | tf_op jit(solution)/shard_map/ppermute | solution.py:344
  8.2 2.0 %collective-permute-done = f32[4,64,128]{2,1,0:T(8,128)S(1)} collective-permute-done((f32[4,64,128]{2,1,0:T(8,128)S(1)}, f32[4,64,128]{2,1,0:T(8,128)S(1)}, u32[]{:S(2)}, u32[]{:S(2)}) %collective-permute-start) | collective-permute-done | bytes 131104 | tf_op jit(solution)/shard_map/ppermute | solution.py:344
  11.4 9.4 %step_rows.1 = (f32[2048,128]{1,0:T(8,128)}, f32[136,128]{1,0:T(8,128)S(1)}, f32[136,128]{1,0:T(8,128)S(1)}, f32[136,128]{1,0:T(8,128)S(1)}, f32[136,128]{1,0:T(...) custom-call(f32[17]{0:T(128)S(1)} %pad_maximum_fusion.refs_0_, ...), custom_call_target="tpu_custom_call" | custom-call | flops 32768000 | bytes 4194304 | tf_op jit(solution)/shard_map/step_rows/pallas_call | solution.py:208
  20.8 2.2 %collective-permute-start.12 = (f32[128,128]{1,0:T(8,128)S(1)}, f32[128,128]{1,0:T(8,128)S(1)}, u32[]{:S(2)}, u32[]{:S(2)}) collective-permute-start(f32[128,128]{1,0:T(8,128)S(1)} %get-tuple-element.42), channel_id=1, source_target_pairs={{0,32},{16,48},{32,0},{48,16},{64,96},{80,112},{96,64},{112,80},{1... | collective-permute-start | bytes 196616 | tf_op jit(solution)/shard_map/ppermute | solution.py:340
  23.0 3.3 %collective-permute-start.13 = (f32[128,128]{1,0:T(8,128)S(1)}, f32[128,128]{1,0:T(8,128)S(1)}, u32[]{:S(2)}, u32[]{:S(2)}) collective-permute-start(f32[128,128]{1,0:T(8,128)S(1)} %get-tuple-element.43), channel_id=1, source_target_pairs={{0,64},{16,80},{32,96},{48,112},{64,0},{80,16},{96,32},{112,48},{1... | collective-permute-start | bytes 196616 | tf_op jit(solution)/shard_map/ppermute | solution.py:340
  26.3 6.5 %collective-permute-start.15 = (f32[128,128]{1,0:T(8,128)S(1)}, f32[128,128]{1,0:T(8,128)S(1)}, u32[]{:S(2)}, u32[]{:S(2)}) collective-permute-start(f32[128,128]{1,0:T(8,128)S(1)} %get-tuple-element.45), channel_id=1, source_target_pairs={{0,128},{16,144},{32,160},{48,176},{64,192},{80,208},{96,224},{112... | collective-permute-start | bytes 196616 | tf_op jit(solution)/shard_map/ppermute | solution.py:340
  32.9 2.3 %collective-permute-start.3 = (f32[136,128]{1,0:T(8,128)S(1)}, f32[136,128]{1,0:T(8,128)S(1)}, u32[]{:S(2)}, u32[]{:S(2)}) collective-permute-start(f32[136,128]{1,0:T(8,128)S(1)} %get-tuple-element.35), channel_id=1, source_target_pairs={{0,64},{16,80},{32,96},{48,112},{64,0},{80,16},{96,32},{112,48},{1... | collective-permute-start | bytes 208904 | tf_op jit(solution)/shard_map/ppermute | solution.py:340
  35.2 4.7 %collective-permute-start.17 = (f32[128,128]{1,0:T(8,128)S(1)}, f32[128,128]{1,0:T(8,128)S(1)}, u32[]{:S(2)}, u32[]{:S(2)}) collective-permute-start(f32[128,128]{1,0:T(8,128)S(1)} %get-tuple-element.47), channel_id=1, source_target_pairs={{0,192},{16,208},{32,224},{48,240},{64,128},{80,144},{96,160},{112... | collective-permute-start | bytes 196616 | tf_op jit(solution)/shard_map/ppermute | solution.py:340
  39.9 5.2 %collective-permute-done.16.refs_14_ = f32[128,128]{1,0:T(8,128)S(1)} collective-permute-done((f32[128,128]{1,0:T(8,128)S(1)}, f32[128,128]{1,0:T(8,128)S(1)}, u32[]{:S(2)}, u32[]{:S(2)}) %collective-permute-start.16) | collective-permute-done | bytes 65568 | tf_op jit(solution)/shard_map/ppermute | solution.py:340
  45.2 1.9 %collective-permute-start.4 = (f32[136,128]{1,0:T(8,128)S(1)}, f32[136,128]{1,0:T(8,128)S(1)}, u32[]{:S(2)}, u32[]{:S(2)}) collective-permute-start(f32[136,128]{1,0:T(8,128)S(1)} %get-tuple-element.36), channel_id=1, source_target_pairs={{0,96},{16,112},{32,64},{48,80},{64,32},{80,48},{96,0},{112,16},{1... | collective-permute-start | bytes 208904 | tf_op jit(solution)/shard_map/ppermute | solution.py:340
  49.7 3.5 %collective-permute-start.7 = (f32[136,128]{1,0:T(8,128)S(1)}, f32[136,128]{1,0:T(8,128)S(1)}, u32[]{:S(2)}, u32[]{:S(2)}) collective-permute-start(f32[136,128]{1,0:T(8,128)S(1)} %get-tuple-element.39), channel_id=1, source_target_pairs={{0,192},{16,208},{32,224},{48,240},{64,128},{80,144},{96,160},{112... | collective-permute-start | bytes 208904 | tf_op jit(solution)/shard_map/ppermute | solution.py:340
  53.2 3.1 %collective-permute-start.8 = (f32[136,128]{1,0:T(8,128)S(1)}, f32[136,128]{1,0:T(8,128)S(1)}, u32[]{:S(2)}, u32[]{:S(2)}) collective-permute-start(f32[136,128]{1,0:T(8,128)S(1)} %get-tuple-element.40), channel_id=1, source_target_pairs={{0,224},{16,240},{32,192},{48,208},{64,160},{80,176},{96,128},{112... | collective-permute-start | bytes 208904 | tf_op jit(solution)/shard_map/ppermute | solution.py:340
  56.2 2.4 %collective-permute-done.6.refs_6_ = f32[136,128]{1,0:T(8,128)S(1)} collective-permute-done((f32[136,128]{1,0:T(8,128)S(1)}, f32[136,128]{1,0:T(8,128)S(1)}, u32[]{:S(2)}, u32[]{:S(2)}) %collective-permute-start.6) | collective-permute-done | bytes 69664 | tf_op jit(solution)/shard_map/ppermute | solution.py:340
  58.7 2.0 %collective-permute-done.7.refs_7_ = f32[136,128]{1,0:T(8,128)S(1)} collective-permute-done((f32[136,128]{1,0:T(8,128)S(1)}, f32[136,128]{1,0:T(8,128)S(1)}, u32[]{:S(2)}, u32[]{:S(2)}) %collective-permute-start.7) | collective-permute-done | bytes 69664 | tf_op jit(solution)/shard_map/ppermute | solution.py:340
  60.7 4.7 %collective-permute-done.8.refs_8_ = f32[136,128]{1,0:T(8,128)S(1)} collective-permute-done((f32[136,128]{1,0:T(8,128)S(1)}, f32[136,128]{1,0:T(8,128)S(1)}, u32[]{:S(2)}, u32[]{:S(2)}) %collective-permute-start.8) | collective-permute-done | bytes 69664 | tf_op jit(solution)/shard_map/ppermute | solution.py:340
  70.9 4.4 %collective-permute-done.19 = f32[2,208,128]{2,1,0:T(8,128)S(1)} collective-permute-done((f32[2,208,128]{2,1,0:T(8,128)S(1)}, f32[2,208,128]{2,1,0:T(8,128)S(1)}, u32[]{:S(2)}, u32[]{:S(2)}) %collective-permute-start.19) | collective-permute-done | bytes 213024 | tf_op jit(solution)/shard_map/ppermute | solution.py:340
  75.6 3.2 %collective-permute-start.24 = (f32[2,208,128]{2,1,0:T(8,128)S(1)}, f32[2,208,128]{2,1,0:T(8,128)S(1)}, u32[]{:S(2)}, u32[]{:S(2)}) collective-permute-start(f32[2,208,128]{2,1,0:T(8,128)S(1)} %add.105.refs_3_), channel_id=1, source_target_pairs={{32,0},{48,16},{64,32},{80,48},{96,64},{112,80},{128,96},{144,112}... | collective-permute-start | bytes 638984 | tf_op jit(solution)/shard_map/ppermute | solution.py:368
  79.0 3.2 %collective-permute-start.22 = (f32[2,208,128]{2,1,0:T(8,128)S(1)}, f32[2,208,128]{2,1,0:T(8,128)S(1)}, u32[]{:S(2)}, u32[]{:S(2)}) collective-permute-start(f32[2,208,128]{2,1,0:T(8,128)S(1)} %add.104.refs_2_), channel_id=1, source_target_pairs={{32,0},{48,16},{64,32},{80,48},{96,64},{112,80},{128,96},{144,112}... | collective-permute-start | bytes 638984 | tf_op jit(solution)/shard_map/ppermute | solution.py:368
  83.1 3.5 %collective-permute-start.25 = (f32[2,208,128]{2,1,0:T(8,128)S(1)}, f32[2,208,128]{2,1,0:T(8,128)S(1)}, u32[]{:S(2)}, u32[]{:S(2)}) collective-permute-start(f32[2,208,128]{2,1,0:T(8,128)S(1)} %collective-permute-done.24.refs_7_), channel_id=1, source_target_pairs={{32,0},{48,16},{64,32},{80,48},{96,64},{112,80},{128,96},{144,112}... | collective-permute-start | bytes 638984 | tf_op jit(solution)/shard_map/ppermute | solution.py:368
  86.6 1.8 %collective-permute-done.10.refs_4_ = f32[2,208,128]{2,1,0:T(8,128)S(1)} collective-permute-done((f32[2,208,128]{2,1,0:T(8,128)S(1)}, f32[2,208,128]{2,1,0:T(8,128)S(1)}, u32[]{:S(2)}, u32[]{:S(2)}) %collective-permute-start.10) | collective-permute-done | bytes 213024 | tf_op jit(solution)/shard_map/ppermute | solution.py:367
  88.4 3.2 %collective-permute-start.23 = (f32[2,208,128]{2,1,0:T(8,128)S(1)}, f32[2,208,128]{2,1,0:T(8,128)S(1)}, u32[]{:S(2)}, u32[]{:S(2)}) collective-permute-start(f32[2,208,128]{2,1,0:T(8,128)S(1)} %collective-permute-done.22.refs_6_), channel_id=1, source_target_pairs={{32,0},{48,16},{64,32},{80,48},{96,64},{112,80},{128,96},{144,112}... | collective-permute-start | bytes 638984 | tf_op jit(solution)/shard_map/ppermute | solution.py:368
  92.7 2.5 %fill.4.refs_6_ = f32[32,512,128]{2,1,0:T(8,128)} custom-call(s32[6]{0:T(128)S(1)} %stack.89.refs_0_, bf16[512,256]{1,0:T(8,128)(2,1)S(1)} %copy-done, f32[2,208,128]{2,1,0:T(8,128)S(1)} %add.104.refs_2_, f32[2,208,128]{2,1,0:T(8,128)S(1)} %add.105.refs_3_, f32[2,208,128]{2,1,0:T(8,128)S(1)} %collective-permute-done.10.refs_4_, ...), custom_call_target="tpu_custom_call" | custom-call | flops 1207959552 | bytes 4423680 | tf_op jit(solution)/shard_map/fill/pallas_call | solution.py:310
  96.3 1.6 %collective-permute-start.27 = (f32[2,208,128]{2,1,0:T(8,128)S(1)}, f32[2,208,128]{2,1,0:T(8,128)S(1)}, u32[]{:S(2)}, u32[]{:S(2)}) collective-permute-start(f32[2,208,128]{2,1,0:T(8,128)S(1)} %collective-permute-done.21.refs_3_), channel_id=1, source_target_pairs={{0,32},{16,48},{32,64},{48,80},{64,96},{80,112},{96,128},{112,144}... | collective-permute-start | bytes 638984 | tf_op jit(solution)/shard_map/ppermute | solution.py:367
  97.8 1.7 %collective-permute-start.28 = (f32[2,208,128]{2,1,0:T(8,128)S(1)}, f32[2,208,128]{2,1,0:T(8,128)S(1)}, u32[]{:S(2)}, u32[]{:S(2)}) collective-permute-start(f32[2,208,128]{2,1,0:T(8,128)S(1)} %collective-permute-done.23.refs_4_), channel_id=1, source_target_pairs={{32,0},{48,16},{64,32},{80,48},{96,64},{112,80},{128,96},{144,112}... | collective-permute-start | bytes 638984 | tf_op jit(solution)/shard_map/ppermute | solution.py:368
  99.5 2.0 %collective-permute-start.29 = (f32[2,208,128]{2,1,0:T(8,128)S(1)}, f32[2,208,128]{2,1,0:T(8,128)S(1)}, u32[]{:S(2)}, u32[]{:S(2)}) collective-permute-start(f32[2,208,128]{2,1,0:T(8,128)S(1)} %collective-permute-done.25.refs_5_), channel_id=1, source_target_pairs={{32,0},{48,16},{64,32},{80,48},{96,64},{112,80},{128,96},{144,112}... | collective-permute-start | bytes 638984 | tf_op jit(solution)/shard_map/ppermute | solution.py:368
  101.6 2.1 %fill.5.refs_6_ = f32[32,512,128]{2,1,0:T(8,128)} custom-call(s32[4]{0:T(128)S(1)} %pad_add_fusion.1.refs_0_, bf16[512,256]{1,0:T(8,128)(2,1)S(1)} %copy-done.1, f32[2,208,128]{2,1,0:T(8,128)S(1)} %collective-permute-done.11.refs_2_, f32[2,208,128]{2,1,0:T(8,128)S(1)} %collective-permute-done.21.refs_3_, ...), custom_call_target="tpu_custom_call", output_to_operand_aliasing={{}: (6, {})} | custom-call | flops 805306368 | bytes 2949120 | tf_op jit(solution)/shard_map/fill/pallas_call | solution.py:310
  103.8 1.9 %collective-permute-done.26.refs_2_ = f32[2,208,128]{2,1,0:T(8,128)S(1)} collective-permute-done((f32[2,208,128]{2,1,0:T(8,128)S(1)}, f32[2,208,128]{2,1,0:T(8,128)S(1)}, u32[]{:S(2)}, u32[]{:S(2)}) %collective-permute-start.26) | collective-permute-done | bytes 213024 | tf_op jit(solution)/shard_map/ppermute | solution.py:367
  105.7 2.4 %collective-permute-done.27.refs_3_ = f32[2,208,128]{2,1,0:T(8,128)S(1)} collective-permute-done((f32[2,208,128]{2,1,0:T(8,128)S(1)}, f32[2,208,128]{2,1,0:T(8,128)S(1)}, u32[]{:S(2)}, u32[]{:S(2)}) %collective-permute-start.27) | collective-permute-done | bytes 213024 | tf_op jit(solution)/shard_map/ppermute | solution.py:367
  108.4 1.7 %collective-permute-start.30 = (f32[2,208,128]{2,1,0:T(8,128)S(1)}, f32[2,208,128]{2,1,0:T(8,128)S(1)}, u32[]{:S(2)}, u32[]{:S(2)}) collective-permute-start(f32[2,208,128]{2,1,0:T(8,128)S(1)} %collective-permute-done.26.refs_2_), channel_id=1, source_target_pairs={{0,32},{16,48},{32,64},{48,80},{64,96},{80,112},{96,128},{112,144}... | collective-permute-start | bytes 638984 | tf_op jit(solution)/shard_map/ppermute | solution.py:379
  111.8 2.1 %fill.6.refs_4_ = f32[32,512,128]{2,1,0:T(8,128)} custom-call(s32[4]{0:T(128)S(1)} %pad_add_fusion.2.refs_0_, bf16[512,256]{1,0:T(8,128)(2,1)S(1)} %copy-done.1, f32[2,208,128]{2,1,0:T(8,128)S(1)} %collective-permute-done.26.refs_2_, f32[2,208,128]{2,1,0:T(8,128)S(1)} %collective-permute-done.27.refs_3_, ...), custom_call_target="tpu_custom_call", output_to_operand_aliasing={{}: (6, {})} | custom-call | flops 805306368 | bytes 2949120 | tf_op jit(solution)/shard_map/fill/pallas_call | solution.py:310
  116.0 1.8 %fill.7 = f32[32,512,128]{2,1,0:T(8,128)} custom-call(s32[2]{0:T(128)S(1)} %pad_add_fusion.refs_0_, bf16[512,256]{1,0:T(8,128)(2,1)S(1)} %copy-done.1, f32[2,208,128]{2,1,0:T(8,128)S(1)} %collective-permute-done.30.refs_2_, f32[2,208,128]{2,1,0:T(8,128)S(1)} %collective-permute-done.31.refs_3_, ...), custom_call_target="tpu_custom_call", output_to_operand_aliasing={{}: (4, {})} | custom-call | flops 402653184 | bytes 1474560 | tf_op jit(solution)/shard_map/fill/pallas_call | solution.py:310
  (59 shorter events, 19.6 us)
Async XLA Ops:
  1.7 6.5 %collective-permute-start.1 = (f32[4,64,128]{2,1,0:T(8,128)S(1)}, f32[4,64,128]{2,1,0:T(8,128)S(1)}, u32[]{:S(2)}, u32[]{:S(2)}) collective-permute-start(f32[4,64,128]{2,1,0:T(8,128)S(1)} %get-tuple-element.62), channel_id=1, source_target_pairs={{1,0},{2,1},{3,2},{4,3},{5,4},{6,5},{7,6},{8,7},{9,8},{10,9},{11,1... | collective-permute-start | bytes 393224 | tf_op jit(solution)/shard_map/ppermute | solution.py:345
  3.9 6.3 %collective-permute-start = (f32[4,64,128]{2,1,0:T(8,128)S(1)}, f32[4,64,128]{2,1,0:T(8,128)S(1)}, u32[]{:S(2)}, u32[]{:S(2)}) collective-permute-start(f32[4,64,128]{2,1,0:T(8,128)S(1)} %get-tuple-element.63), channel_id=1, source_target_pairs={{0,1},{1,2},{2,3},{3,4},{4,5},{5,6},{6,7},{7,8},{8,9},{9,10},{10,1... | collective-permute-start | bytes 393224 | tf_op jit(solution)/shard_map/ppermute | solution.py:344
  20.8 12.1 %collective-permute-start.12 = (f32[128,128]{1,0:T(8,128)S(1)}, f32[128,128]{1,0:T(8,128)S(1)}, u32[]{:S(2)}, u32[]{:S(2)}) collective-permute-start(f32[128,128]{1,0:T(8,128)S(1)} %get-tuple-element.42), channel_id=1, source_target_pairs={{0,32},{16,48},{32,0},{48,16},{64,96},{80,112},{96,64},{112,80},{1... | collective-permute-start | bytes 196616 | tf_op jit(solution)/shard_map/ppermute | solution.py:340
  23.0 12.2 %collective-permute-start.13 = (f32[128,128]{1,0:T(8,128)S(1)}, f32[128,128]{1,0:T(8,128)S(1)}, u32[]{:S(2)}, u32[]{:S(2)}) collective-permute-start(f32[128,128]{1,0:T(8,128)S(1)} %get-tuple-element.43), channel_id=1, source_target_pairs={{0,64},{16,80},{32,96},{48,112},{64,0},{80,16},{96,32},{112,48},{1... | collective-permute-start | bytes 196616 | tf_op jit(solution)/shard_map/ppermute | solution.py:340
  26.3 8.9 %collective-permute-start.14 = (f32[128,128]{1,0:T(8,128)S(1)}, f32[128,128]{1,0:T(8,128)S(1)}, u32[]{:S(2)}, u32[]{:S(2)}) collective-permute-start(f32[128,128]{1,0:T(8,128)S(1)} %get-tuple-element.44), channel_id=1, source_target_pairs={{0,96},{16,112},{32,64},{48,80},{64,32},{80,48},{96,0},{112,16},{1... | collective-permute-start | bytes 196616 | tf_op jit(solution)/shard_map/ppermute | solution.py:340
  26.3 13.6 %collective-permute-start.15 = (f32[128,128]{1,0:T(8,128)S(1)}, f32[128,128]{1,0:T(8,128)S(1)}, u32[]{:S(2)}, u32[]{:S(2)}) collective-permute-start(f32[128,128]{1,0:T(8,128)S(1)} %get-tuple-element.45), channel_id=1, source_target_pairs={{0,128},{16,144},{32,160},{48,176},{64,192},{80,208},{96,224},{112... | collective-permute-start | bytes 196616 | tf_op jit(solution)/shard_map/ppermute | solution.py:340
  32.9 16.8 %collective-permute-start.2 = (f32[136,128]{1,0:T(8,128)S(1)}, f32[136,128]{1,0:T(8,128)S(1)}, u32[]{:S(2)}, u32[]{:S(2)}) collective-permute-start(f32[136,128]{1,0:T(8,128)S(1)} %get-tuple-element.34), channel_id=1, source_target_pairs={{0,32},{16,48},{32,0},{48,16},{64,96},{80,112},{96,64},{112,80},{1... | collective-permute-start | bytes 208904 | tf_op jit(solution)/shard_map/ppermute | solution.py:340
  32.9 20.3 %collective-permute-start.3 = (f32[136,128]{1,0:T(8,128)S(1)}, f32[136,128]{1,0:T(8,128)S(1)}, u32[]{:S(2)}, u32[]{:S(2)}) collective-permute-start(f32[136,128]{1,0:T(8,128)S(1)} %get-tuple-element.35), channel_id=1, source_target_pairs={{0,64},{16,80},{32,96},{48,112},{64,0},{80,16},{96,32},{112,48},{1... | collective-permute-start | bytes 208904 | tf_op jit(solution)/shard_map/ppermute | solution.py:340
  35.2 10.0 %collective-permute-start.16 = (f32[128,128]{1,0:T(8,128)S(1)}, f32[128,128]{1,0:T(8,128)S(1)}, u32[]{:S(2)}, u32[]{:S(2)}) collective-permute-start(f32[128,128]{1,0:T(8,128)S(1)} %get-tuple-element.46), channel_id=1, source_target_pairs={{0,160},{16,176},{32,128},{48,144},{64,224},{80,240},{96,192},{112... | collective-permute-start | bytes 196616 | tf_op jit(solution)/shard_map/ppermute | solution.py:340
  35.2 11.9 %collective-permute-start.17 = (f32[128,128]{1,0:T(8,128)S(1)}, f32[128,128]{1,0:T(8,128)S(1)}, u32[]{:S(2)}, u32[]{:S(2)}) collective-permute-start(f32[128,128]{1,0:T(8,128)S(1)} %get-tuple-element.47), channel_id=1, source_target_pairs={{0,192},{16,208},{32,224},{48,240},{64,128},{80,144},{96,160},{112... | collective-permute-start | bytes 196616 | tf_op jit(solution)/shard_map/ppermute | solution.py:340
  39.9 8.7 %collective-permute-start.18 = (f32[128,128]{1,0:T(8,128)S(1)}, f32[128,128]{1,0:T(8,128)S(1)}, u32[]{:S(2)}, u32[]{:S(2)}) collective-permute-start(f32[128,128]{1,0:T(8,128)S(1)} %get-tuple-element.48), channel_id=1, source_target_pairs={{0,224},{16,240},{32,192},{48,208},{64,160},{80,176},{96,128},{112... | collective-permute-start | bytes 196616 | tf_op jit(solution)/shard_map/ppermute | solution.py:340
  45.2 11.1 %collective-permute-start.4 = (f32[136,128]{1,0:T(8,128)S(1)}, f32[136,128]{1,0:T(8,128)S(1)}, u32[]{:S(2)}, u32[]{:S(2)}) collective-permute-start(f32[136,128]{1,0:T(8,128)S(1)} %get-tuple-element.36), channel_id=1, source_target_pairs={{0,96},{16,112},{32,64},{48,80},{64,32},{80,48},{96,0},{112,16},{1... | collective-permute-start | bytes 208904 | tf_op jit(solution)/shard_map/ppermute | solution.py:340
  47.1 9.2 %collective-permute-start.5 = (f32[136,128]{1,0:T(8,128)S(1)}, f32[136,128]{1,0:T(8,128)S(1)}, u32[]{:S(2)}, u32[]{:S(2)}) collective-permute-start(f32[136,128]{1,0:T(8,128)S(1)} %get-tuple-element.37), channel_id=1, source_target_pairs={{0,128},{16,144},{32,160},{48,176},{64,192},{80,208},{96,224},{112... | collective-permute-start | bytes 208904 | tf_op jit(solution)/shard_map/ppermute | solution.py:340
  48.6 10.1 %collective-permute-start.6 = (f32[136,128]{1,0:T(8,128)S(1)}, f32[136,128]{1,0:T(8,128)S(1)}, u32[]{:S(2)}, u32[]{:S(2)}) collective-permute-start(f32[136,128]{1,0:T(8,128)S(1)} %get-tuple-element.38), channel_id=1, source_target_pairs={{0,160},{16,176},{32,128},{48,144},{64,224},{80,240},{96,192},{112... | collective-permute-start | bytes 208904 | tf_op jit(solution)/shard_map/ppermute | solution.py:340
  49.7 11.0 %collective-permute-start.7 = (f32[136,128]{1,0:T(8,128)S(1)}, f32[136,128]{1,0:T(8,128)S(1)}, u32[]{:S(2)}, u32[]{:S(2)}) collective-permute-start(f32[136,128]{1,0:T(8,128)S(1)} %get-tuple-element.39), channel_id=1, source_target_pairs={{0,192},{16,208},{32,224},{48,240},{64,128},{80,144},{96,160},{112... | collective-permute-start | bytes 208904 | tf_op jit(solution)/shard_map/ppermute | solution.py:340
  53.2 12.2 %collective-permute-start.8 = (f32[136,128]{1,0:T(8,128)S(1)}, f32[136,128]{1,0:T(8,128)S(1)}, u32[]{:S(2)}, u32[]{:S(2)}) collective-permute-start(f32[136,128]{1,0:T(8,128)S(1)} %get-tuple-element.40), channel_id=1, source_target_pairs={{0,224},{16,240},{32,192},{48,208},{64,160},{80,176},{96,128},{112... | collective-permute-start | bytes 208904 | tf_op jit(solution)/shard_map/ppermute | solution.py:340
  67.0 8.2 %collective-permute-start.19 = (f32[2,208,128]{2,1,0:T(8,128)S(1)}, f32[2,208,128]{2,1,0:T(8,128)S(1)}, u32[]{:S(2)}, u32[]{:S(2)}) collective-permute-start(f32[2,208,128]{2,1,0:T(8,128)S(1)} %combine.3), channel_id=1, source_target_pairs={{0,16},{16,0},{32,48},{48,32},{64,80},{80,64},{96,112},{112,96},{1... | collective-permute-start | bytes 638984 | tf_op jit(solution)/shard_map/ppermute | solution.py:340
  69.9 9.0 %collective-permute-start.9 = (f32[2,208,128]{2,1,0:T(8,128)S(1)}, f32[2,208,128]{2,1,0:T(8,128)S(1)}, u32[]{:S(2)}, u32[]{:S(2)}) collective-permute-start(f32[2,208,128]{2,1,0:T(8,128)S(1)} %combine.2), channel_id=1, source_target_pairs={{0,16},{16,0},{32,48},{48,32},{64,80},{80,64},{96,112},{112,96},{1... | collective-permute-start | bytes 638984 | tf_op jit(solution)/shard_map/ppermute | solution.py:340
  75.3 7.8 %collective-permute-start.20 = (f32[2,208,128]{2,1,0:T(8,128)S(1)}, f32[2,208,128]{2,1,0:T(8,128)S(1)}, u32[]{:S(2)}, u32[]{:S(2)}) collective-permute-start(f32[2,208,128]{2,1,0:T(8,128)S(1)} %add.105.refs_3_), channel_id=1, source_target_pairs={{0,32},{16,48},{32,64},{48,80},{64,96},{80,112},{96,128},{112,144}... | collective-permute-start | bytes 638984 | tf_op jit(solution)/shard_map/ppermute | solution.py:367
  75.6 7.5 %collective-permute-start.24 = (f32[2,208,128]{2,1,0:T(8,128)S(1)}, f32[2,208,128]{2,1,0:T(8,128)S(1)}, u32[]{:S(2)}, u32[]{:S(2)}) collective-permute-start(f32[2,208,128]{2,1,0:T(8,128)S(1)} %add.105.refs_3_), channel_id=1, source_target_pairs={{32,0},{48,16},{64,32},{80,48},{96,64},{112,80},{128,96},{144,112}... | collective-permute-start | bytes 638984 | tf_op jit(solution)/shard_map/ppermute | solution.py:368
  78.9 9.5 %collective-permute-start.10 = (f32[2,208,128]{2,1,0:T(8,128)S(1)}, f32[2,208,128]{2,1,0:T(8,128)S(1)}, u32[]{:S(2)}, u32[]{:S(2)}) collective-permute-start(f32[2,208,128]{2,1,0:T(8,128)S(1)} %add.104.refs_2_), channel_id=1, source_target_pairs={{0,32},{16,48},{32,64},{48,80},{64,96},{80,112},{96,128},{112,144}... | collective-permute-start | bytes 638984 | tf_op jit(solution)/shard_map/ppermute | solution.py:367
  79.0 9.4 %collective-permute-start.22 = (f32[2,208,128]{2,1,0:T(8,128)S(1)}, f32[2,208,128]{2,1,0:T(8,128)S(1)}, u32[]{:S(2)}, u32[]{:S(2)}) collective-permute-start(f32[2,208,128]{2,1,0:T(8,128)S(1)} %add.104.refs_2_), channel_id=1, source_target_pairs={{32,0},{48,16},{64,32},{80,48},{96,64},{112,80},{128,96},{144,112}... | collective-permute-start | bytes 638984 | tf_op jit(solution)/shard_map/ppermute | solution.py:368
  83.1 12.1 %collective-permute-start.21 = (f32[2,208,128]{2,1,0:T(8,128)S(1)}, f32[2,208,128]{2,1,0:T(8,128)S(1)}, u32[]{:S(2)}, u32[]{:S(2)}) collective-permute-start(f32[2,208,128]{2,1,0:T(8,128)S(1)} %collective-permute-done.20.refs_5_), channel_id=1, source_target_pairs={{0,32},{16,48},{32,64},{48,80},{64,96},{80,112},{96,128},{112,144}... | collective-permute-start | bytes 638984 | tf_op jit(solution)/shard_map/ppermute | solution.py:367
  83.1 12.1 %collective-permute-start.25 = (f32[2,208,128]{2,1,0:T(8,128)S(1)}, f32[2,208,128]{2,1,0:T(8,128)S(1)}, u32[]{:S(2)}, u32[]{:S(2)}) collective-permute-start(f32[2,208,128]{2,1,0:T(8,128)S(1)} %collective-permute-done.24.refs_7_), channel_id=1, source_target_pairs={{32,0},{48,16},{64,32},{80,48},{96,64},{112,80},{128,96},{144,112}... | collective-permute-start | bytes 638984 | tf_op jit(solution)/shard_map/ppermute | solution.py:368
  88.4 7.9 %collective-permute-start.11 = (f32[2,208,128]{2,1,0:T(8,128)S(1)}, f32[2,208,128]{2,1,0:T(8,128)S(1)}, u32[]{:S(2)}, u32[]{:S(2)}) collective-permute-start(f32[2,208,128]{2,1,0:T(8,128)S(1)} %collective-permute-done.10.refs_4_), channel_id=1, source_target_pairs={{0,32},{16,48},{32,64},{48,80},{64,96},{80,112},{96,128},{112,144}... | collective-permute-start | bytes 638984 | tf_op jit(solution)/shard_map/ppermute | solution.py:367
  88.4 7.9 %collective-permute-start.23 = (f32[2,208,128]{2,1,0:T(8,128)S(1)}, f32[2,208,128]{2,1,0:T(8,128)S(1)}, u32[]{:S(2)}, u32[]{:S(2)}) collective-permute-start(f32[2,208,128]{2,1,0:T(8,128)S(1)} %collective-permute-done.22.refs_6_), channel_id=1, source_target_pairs={{32,0},{48,16},{64,32},{80,48},{96,64},{112,80},{128,96},{144,112}... | collective-permute-start | bytes 638984 | tf_op jit(solution)/shard_map/ppermute | solution.py:368
  96.3 9.4 %collective-permute-start.26 = (f32[2,208,128]{2,1,0:T(8,128)S(1)}, f32[2,208,128]{2,1,0:T(8,128)S(1)}, u32[]{:S(2)}, u32[]{:S(2)}) collective-permute-start(f32[2,208,128]{2,1,0:T(8,128)S(1)} %collective-permute-done.11.refs_2_), channel_id=1, source_target_pairs={{0,32},{16,48},{32,64},{48,80},{64,96},{80,112},{96,128},{112,144}... | collective-permute-start | bytes 638984 | tf_op jit(solution)/shard_map/ppermute | solution.py:367
  96.3 11.8 %collective-permute-start.27 = (f32[2,208,128]{2,1,0:T(8,128)S(1)}, f32[2,208,128]{2,1,0:T(8,128)S(1)}, u32[]{:S(2)}, u32[]{:S(2)}) collective-permute-start(f32[2,208,128]{2,1,0:T(8,128)S(1)} %collective-permute-done.21.refs_3_), channel_id=1, source_target_pairs={{0,32},{16,48},{32,64},{48,80},{64,96},{80,112},{96,128},{112,144}... | collective-permute-start | bytes 638984 | tf_op jit(solution)/shard_map/ppermute | solution.py:367
  97.8 10.2 %collective-permute-start.28 = (f32[2,208,128]{2,1,0:T(8,128)S(1)}, f32[2,208,128]{2,1,0:T(8,128)S(1)}, u32[]{:S(2)}, u32[]{:S(2)}) collective-permute-start(f32[2,208,128]{2,1,0:T(8,128)S(1)} %collective-permute-done.23.refs_4_), channel_id=1, source_target_pairs={{32,0},{48,16},{64,32},{80,48},{96,64},{112,80},{128,96},{144,112}... | collective-permute-start | bytes 638984 | tf_op jit(solution)/shard_map/ppermute | solution.py:368
  99.5 8.9 %collective-permute-start.29 = (f32[2,208,128]{2,1,0:T(8,128)S(1)}, f32[2,208,128]{2,1,0:T(8,128)S(1)}, u32[]{:S(2)}, u32[]{:S(2)}) collective-permute-start(f32[2,208,128]{2,1,0:T(8,128)S(1)} %collective-permute-done.25.refs_5_), channel_id=1, source_target_pairs={{32,0},{48,16},{64,32},{80,48},{96,64},{112,80},{128,96},{144,112}... | collective-permute-start | bytes 638984 | tf_op jit(solution)/shard_map/ppermute | solution.py:368
  108.4 7.1 %collective-permute-start.30 = (f32[2,208,128]{2,1,0:T(8,128)S(1)}, f32[2,208,128]{2,1,0:T(8,128)S(1)}, u32[]{:S(2)}, u32[]{:S(2)}) collective-permute-start(f32[2,208,128]{2,1,0:T(8,128)S(1)} %collective-permute-done.26.refs_2_), channel_id=1, source_target_pairs={{0,32},{16,48},{32,64},{48,80},{64,96},{80,112},{96,128},{112,144}... | collective-permute-start | bytes 638984 | tf_op jit(solution)/shard_map/ppermute | solution.py:379
  110.2 5.8 %collective-permute-start.31 = (f32[2,208,128]{2,1,0:T(8,128)S(1)}, f32[2,208,128]{2,1,0:T(8,128)S(1)}, u32[]{:S(2)}, u32[]{:S(2)}) collective-permute-start(f32[2,208,128]{2,1,0:T(8,128)S(1)} %collective-permute-done.29.refs_5_), channel_id=1, source_target_pairs={{32,0},{48,16},{64,32},{80,48},{96,64},{112,80},{128,96},{144,112}... | collective-permute-start | bytes 638984 | tf_op jit(solution)/shard_map/ppermute | solution.py:379
  (5 other events, 105.4 us)

commit v3 on v2

v3 whole, which is shorter than its diff:
```python
import itertools

import jax
import jax.numpy as jnp
import numpy as np
from jax import lax
from jax.experimental import pallas as pl
from jax.experimental.pallas import tpu as pltpu
from jax.sharding import PartitionSpec as P

STEPS = 4
MLEN = 8
FINEST = 3
LEVEL_SUM = 6
ZLEN = 8
QUARTERS = 4
ORDER = (2, 1, 3)
INNER_LIMIT = 24 * 2**20
OUTER_LIMIT = 24 * 2**20


def rank_of(coordinate):
    if coordinate % 4 == 0:
        return 1
    return 2 if coordinate % 2 == 0 else 3


def union_points():
    points = []
    for first in (0, 4, 2, 6, 1, 3, 5, 7):
        for second, third in itertools.product(range(MLEN), repeat=2):
            if rank_of(first) + rank_of(second) + rank_of(third) <= LEVEL_SUM:
                points.append((first, second, third))
    return np.array(points, np.int32)


POINTS = union_points()
COUNT = len(POINTS)
SUB = 64
META = 8
TRIPLES = ((1, 2), (1, 3), (2, 1), (2, 2), (2, 3), (3, 1), (3, 2))
GROUPS = (((0, 48), (0,)), ((48, 96), (4,)), ((96, 160), (2, 6)), ((160, 208), (1, 3, 5, 7)))


def nodal_matrix(length_dim):
    matrix = np.eye(length_dim)
    stride = length_dim // 2
    while stride >= 1:
        for position in range(stride, length_dim, 2 * stride):
            matrix[position] = matrix[position] + 0.5 * matrix[position - stride]
            if position + stride < length_dim:
                matrix[position] = matrix[position] + 0.5 * matrix[position + stride]
        stride = stride // 2
    return matrix


def fill_matrix():
    nodal = nodal_matrix(MLEN)
    square = MLEN**2
    matrix = np.zeros((MLEN, MLEN, MLEN, COUNT))
    for column, (first, second, third) in enumerate(POINTS):
        matrix[first, :, :, column] = np.outer(nodal[:, second], nodal[:, third])
    matrix = matrix.reshape(MLEN, square, COUNT)
    packed = np.zeros((MLEN * square, 256))
    begin = 0
    for (low, high), members in GROUPS:
        block = matrix[list(members), :, low:high].reshape(-1, high - low)
        packed[begin : begin + len(block), : 3 * (high - low)] = np.tile(block, (1, 3))
        begin += len(block)
    return packed

def placing_table():
    tables = []
    for first, second in TRIPLES:
        level = (first, second, LEVEL_SUM - first - second)
        length = [2**v for v in level]
        surplus = np.ones((1, 1))
        for n in length:
            surplus = np.kron(surplus, np.round(2.0 * np.linalg.inv(nodal_matrix(n))) / 2.0)
        target = np.zeros((COUNT, SUB))
        for column, coords in enumerate(itertools.product(*[range(n) for n in length])):
            point = [c * (MLEN // n) for c, n in zip(coords, length)]
            target[np.all(POINTS == point, axis=1), column] = 1.0
        tables.append(np.tile(target @ surplus, (1, 3)))
    return np.stack(tables)


def split_three(values):
    high = values.astype(jnp.bfloat16)
    rest = values - high.astype(jnp.float32)
    middle = rest.astype(jnp.bfloat16)
    low = (rest - middle.astype(jnp.float32)).astype(jnp.bfloat16)
    return high, middle, low


class Stencil:
    def __init__(self, points, facts_ref, coef_ref):
        self.points, self.coef_ref = points, coef_ref
        levels = [facts_ref[dim].astype(jnp.int32) for dim in range(3)]
        spread = [facts_ref[4 + dim] for dim in range(5)]
        drift = [0.5 * facts_ref[9 + dim] for dim in range(5)]
        place = lax.broadcasted_iota(jnp.int32, (points, 128), 0)
        lane = lax.broadcasted_iota(jnp.int32, (8, 128), 1)
        sublane = lax.broadcasted_iota(jnp.int32, (META, 128), 0)
        offsets = [levels[1] + levels[2], levels[2], jnp.int32(0)]
        self.strides = []
        self.centre_rate = 1.0 - 2.0 * spread[0] - 2.0 * spread[4]
        for dim in range(3):
            length = jnp.left_shift(jnp.int32(1), levels[dim])
            coord = jnp.bitwise_and(jnp.right_shift(place, offsets[dim]), length - 1)
            rise, fall = spread[dim + 1] + drift[dim + 1], spread[dim + 1] - drift[dim + 1]
            coef_ref[2 * dim] = jnp.where(coord < length - 1, rise, 0.0)
            coef_ref[2 * dim + 1] = jnp.where(coord > 0, fall, 0.0)
            self.strides.append(jnp.left_shift(jnp.int32(1), offsets[dim]))
            self.centre_rate = self.centre_rate - 2.0 * spread[dim + 1]
        self.row_up, self.row_down = spread[0] + drift[0], spread[0] - drift[0]
        self.lane_up = jnp.where(lane < 127, spread[4] + drift[4], 0.0)
        self.lane_down = jnp.where(lane > 0, spread[4] - drift[4], 0.0)
        triple = (3 * levels[0] + levels[1] - 5).astype(jnp.float32)
        self.head = jnp.where(sublane == 0, triple, facts_ref[3])

    def advance(self, source, target, spans, locate, mask):
        points = self.points

        def tile(tile_index, carry):
            base = pl.multiple_of(tile_index * 8, 8)
            coefs = [self.coef_ref[i, pl.ds(base, 8), :] for i in range(6)]

            def at(row):
                return source[pl.ds(pl.multiple_of(row * points + base, 8), 8), :]

            for low, high in spans:
                below, centre = at(low - 1), at(low)
                for row in range(low, high):
                    above = at(row + 1)
                    offset = row * points + base
                    total = centre * self.centre_rate + above * self.row_up + below * self.row_down
                    total = total + pltpu.roll(centre, 127, 1) * self.lane_up
                    total = total + pltpu.roll(centre, 1, 1) * self.lane_down
                    for dim in range(3):
                        stride = self.strides[dim]
                        total = total + source[pl.ds(offset + stride, 8), :] * coefs[2 * dim]
                        total = total + source[pl.ds(offset - stride, 8), :] * coefs[2 * dim + 1]
                    total = mask(row, total)
                    target[pl.ds(pl.multiple_of(locate(row) + base, 8), 8), :] = total
                    below, centre = centre, above
            return carry

        lax.fori_loop(0, points // 8, tile, 0, unroll=4)


def shifted_place():
    columns = lax.axis_size("grid") // ZLEN
    core = jnp.bitwise_and(lax.axis_index("dom"), 1)
    return jnp.bitwise_and(lax.axis_index("grid") // columns - core + ZLEN, ZLEN - 1)


def inner_kernel(rows, points, facts_ref, start_ref, stepped_ref, *rest):
    parts = rest[:QUARTERS]
    first, second, final, coef_ref, load_sem, part_sem, store_sem = rest[QUARTERS:]
    share = (rows - 2 * STEPS) // QUARTERS
    size = share * points
    block = size + META
    load = pltpu.make_async_copy(start_ref, first, load_sem)
    load.start()
    quarter = jnp.right_shift(shifted_place(), 1)
    stencil = Stencil(points, facts_ref, coef_ref)
    for index in range(QUARTERS):
        final[index * block + size : (index + 1) * block, :] = stencil.head
    load.wait()

    def located(row):
        group, inner = divmod(row - STEPS, share)
        return group * block + inner * points

    same = lambda row: row * points
    keep = lambda row, value: value
    buffers = [first, second, first, second, final]
    for step in range(1, STEPS + 1):
        place = located if step == STEPS else same
        stencil.advance(buffers[step - 1], buffers[step], [(step, rows - step)], place, keep)

    copies = []
    for index, part in enumerate(parts):
        begin = pl.multiple_of(jnp.bitwise_xor(quarter, index) * block, 8)
        copies.append(
            pltpu.make_async_copy(final.at[pl.ds(begin, block)], part, part_sem.at[index])
        )
    for index in range(QUARTERS):
        copies.append(
            pltpu.make_async_copy(
                final.at[pl.ds(index * block, size)],
                stepped_ref.at[pl.ds(STEPS * points + index * size, size)],
                store_sem.at[index],
            )
        )
    for copy in copies:
        copy.start()
    for copy in copies:
        copy.wait()


def outer_kernel(rows, points, facts_ref, start_ref, before_ref, after_ref, _, stepped_ref, *rest):
    parts = rest[:QUARTERS]
    first, second, final, coef_ref, load_sem, part_sem, store_sem = rest[QUARTERS:]
    halo, near = STEPS * points, 2 * STEPS * points
    sides = [
        (before_ref, 0, halo),
        (start_ref.at[pl.ds(0, near)], halo, near),
        (start_ref.at[pl.ds(rows * points - near, near)], halo + near, near),
        (after_ref, halo + 2 * near, halo),
    ]
    loads = [
        pltpu.make_async_copy(source, first.at[pl.ds(begin, size)], load_sem.at[i])
        for i, (source, begin, size) in enumerate(sides)
    ]
    for load in loads:
        load.start()
    quarter = jnp.right_shift(shifted_place(), 1)
    dom = lax.axis_index("dom")
    keep_low = (dom > 0).astype(jnp.float32)
    keep_high = (dom < lax.axis_size("dom") - 1).astype(jnp.float32)
    stencil = Stencil(points, facts_ref, coef_ref)
    for load in loads:
        load.wait()

    strip = 3 * STEPS

    def mask(row, value):
        if row < STEPS:
            return value * keep_low
        if row >= 2 * strip - STEPS:
            return value * keep_high
        return value

    def located(row):
        side, inner = divmod(row, strip)
        return (2 * (inner - STEPS) + side) * points

    same = lambda row: row * points
    buffers = [first, second, first, second, final]
    for step in range(1, STEPS + 1):
        place = located if step == STEPS else same
        spans = [(step, strip - step), (strip + step, 2 * strip - step)]
        stencil.advance(buffers[step - 1], buffers[step], spans, place, mask)

    copies = []
    for index, part in enumerate(parts):
        begin = pl.multiple_of(jnp.bitwise_xor(quarter, index) * (2 * points), 8)
        copies.append(
            pltpu.make_async_copy(final.at[pl.ds(begin, 2 * points)], part, part_sem.at[index])
        )
    for index in range(2 * QUARTERS):
        row = index // 2 + index % 2 * (rows - STEPS)
        copies.append(
            pltpu.make_async_copy(
                final.at[pl.ds(index * points, points)],
                stepped_ref.at[pl.ds(row * points, points)],
                store_sem.at[index],
            )
        )
    for copy in copies:
        copy.start()
    for copy in copies:
        copy.wait()


def step_call(kernel, name, facts, inputs, olds, rows, points, tall, wide, part, limit):
    lanes = inputs[0].shape[-1]
    anywhere = pl.BlockSpec(memory_space=pl.ANY)
    buffer = pltpu.VMEM((tall * points, lanes), jnp.float32)
    return pl.pallas_call(
        lambda *refs: kernel(rows, points, *refs),
        out_shape=[jax.ShapeDtypeStruct((rows * points, lanes), jnp.float32)]
        + [jax.ShapeDtypeStruct((part, lanes), jnp.float32)] * QUARTERS,
        in_specs=[pl.BlockSpec(memory_space=pltpu.SMEM)] + [anywhere] * (len(inputs) + len(olds)),
        out_specs=[anywhere] * (1 + QUARTERS),
        input_output_aliases={1 + len(inputs): 0} if olds else {},
        scratch_shapes=[
            buffer,
            buffer,
            pltpu.VMEM((wide, lanes), jnp.float32),
            pltpu.VMEM((6, points, lanes), jnp.float32),
            pltpu.SemaphoreType.DMA((4,)) if olds else pltpu.SemaphoreType.DMA,
            pltpu.SemaphoreType.DMA((QUARTERS,)),
            pltpu.SemaphoreType.DMA((2 * QUARTERS,)),
        ],
        compiler_params=pltpu.CompilerParams(vmem_limit_bytes=limit),
        cost_estimate=pl.CostEstimate(
            flops=25 * STEPS * tall * points * lanes, bytes_accessed=12 * tall * points * lanes,
            transcendentals=0,
        ),
        name=name,
    )(facts, *inputs, *olds)


def inner_steps(facts, start):
    rows, points, lanes = start.shape
    part = (rows - 2 * STEPS) // QUARTERS * points + META
    inputs = [start.reshape(-1, lanes)]
    return step_call(
        inner_kernel, "inner_steps", facts, inputs, [], rows, points, rows, QUARTERS * part, part,
        INNER_LIMIT,
    )


def outer_steps(facts, start, before, after, stepped):
    rows, points, lanes = start.shape
    inputs = [v.reshape(-1, lanes) for v in (start, before, after)]
    return step_call(
        outer_kernel, "outer_steps", facts, inputs, [stepped], rows, points, 6 * STEPS,
        2 * QUARTERS * points, 2 * points, OUTER_LIMIT,
    )


def combine_kernel(grids, edge, table_ref, *refs):
    inner, outer = refs[:QUARTERS], refs[QUARTERS:-2]
    half = inner[0].shape[0] // 2 // SUB * SUB
    lanes = inner[0].shape[1]
    mine = jnp.bitwise_and(shifted_place(), 1)
    total = None
    for index in range(QUARTERS):
        head = inner[index]
        triple = jnp.max(head[2 * half : 2 * half + 1, :]).astype(jnp.int32)
        scale = jnp.max(head[2 * half + 1 : 2 * half + 2, :]) / grids
        columns = []
        for member in (1 - mine, mine):
            begin = pl.multiple_of(member * half, SUB)
            if edge:
                columns.append(head[pl.ds(begin + 2 * SUB, SUB), :])
                columns.append(outer[index][pl.ds(pl.multiple_of(member * SUB, SUB), SUB), :])
            else:
                columns.append(head[pl.ds(begin, SUB), :])
                columns.append(head[pl.ds(begin + SUB, SUB), :])
        wide = jnp.concatenate(columns, axis=1) * scale
        stack = jnp.concatenate(split_three(wide), axis=0)
        matrix = table_ref[jnp.clip(triple, 0, len(TRIPLES) - 1)]
        term = jnp.dot(matrix, stack, preferred_element_type=jnp.float32)
        total = term if total is None else total + term
    for side, out_ref in enumerate(refs[-2:]):
        for row in range(2):
            begin = (2 * side + row) * lanes
            out_ref[row] = total[:, begin : begin + lanes]


def combine(table, inner, outer, grids):
    lanes = inner[0].shape[1]
    shape = jax.ShapeDtypeStruct((2, COUNT, lanes), jnp.float32)
    return pl.pallas_call(
        lambda *refs: combine_kernel(grids, bool(outer), *refs),
        out_shape=[shape, shape],
        compiler_params=pltpu.CompilerParams(vmem_limit_bytes=24 * 2**20),
        cost_estimate=pl.CostEstimate(
            flops=2 * QUARTERS * 3 * SUB * COUNT * 4 * lanes, bytes_accessed=2**20, transcendentals=0
        ),
        name="combine",
    )(table, *inner, *outer)


def fill_kernel(chunks, width, with_base, where_ref, matrix_ref, *refs):
    sources = refs[:chunks]
    out_ref, scratch, sems = refs[chunks + with_base :]
    square = MLEN**2
    copies = []
    for index, source in enumerate(sources):
        lanes = source.shape[2]
        parts = split_three(jnp.concatenate([source[row] for row in range(width)], axis=1))
        level = {}
        begin = 0
        for (low, high), members in GROUPS:
            block = matrix_ref[begin : begin + square * len(members), : 3 * (high - low)]
            stack = jnp.concatenate([part[low:high] for part in parts], axis=0)
            result = jnp.dot(block, stack, preferred_element_type=jnp.float32)
            for k, member in enumerate(members):
                level[member] = result[k * square : (k + 1) * square]
            begin += square * len(members)
        nodal = dict(level)
        nodal[4] = level[4] + 0.5 * nodal[0]
        nodal[2] = level[2] + 0.5 * (nodal[0] + nodal[4])
        nodal[6] = level[6] + 0.5 * nodal[4]
        for odd in (1, 3, 5):
            nodal[odd] = level[odd] + 0.5 * (nodal[odd - 1] + nodal[odd + 1])
        nodal[7] = level[7] + 0.5 * nodal[6]
        for row in range(width):
            for c in range(MLEN):
                scratch[index * width + row, c * square : (c + 1) * square, :] = nodal[c][
                    :, row * lanes : (row + 1) * lanes
                ]
        for row in range(width):
            copy = pltpu.make_async_copy(
                scratch.at[index * width + row],
                out_ref.at[where_ref[index * width + row]],
                sems.at[index * width + row],
            )
            copy.start()
            copies.append(copy)
    for copy in copies:
        copy.wait()


def fill(where, matrix, sources, rows, base):
    width, _, lanes = sources[0].shape
    chunks = len(sources)
    with_base = 0 if base is None else 1
    args = [where, matrix, *sources] + ([base] if with_base else [])
    anywhere = pl.BlockSpec(memory_space=pl.ANY)
    vector = pl.BlockSpec(memory_space=pltpu.VMEM)
    return pl.pallas_call(
        lambda *refs: fill_kernel(chunks, width, with_base, *refs),
        out_shape=jax.ShapeDtypeStruct((rows, MLEN**3, lanes), jnp.float32),
        in_specs=[pl.BlockSpec(memory_space=pltpu.SMEM)] + [vector] * (1 + chunks) + [anywhere] * with_base,
        out_specs=anywhere,
        input_output_aliases={2 + chunks: 0} if with_base else {},
        scratch_shapes=[
            pltpu.VMEM((chunks * width, MLEN**3, lanes), jnp.float32),
            pltpu.SemaphoreType.DMA((chunks * width,)),
        ],
        compiler_params=pltpu.CompilerParams(vmem_limit_bytes=24 * 2**20),
        cost_estimate=pl.CostEstimate(
            flops=6 * chunks * width * matrix.size * lanes,
            bytes_accessed=4 * chunks * width * (MLEN**3 + COUNT) * lanes,
            transcendentals=0,
        ),
        name="fill",
    )(*args)


def per_device(initial, diffusion, drift, levels, weights):
    values = initial[0]
    rows, points, _ = values.shape
    dom_size = lax.axis_size("dom")
    grid_size = lax.axis_size("grid")
    columns = grid_size // ZLEN
    place = shifted_place()

    def swap(v, bits):
        pairs = []
        for grid in range(grid_size):
            z, y = divmod(grid, columns)
            for dom in range(dom_size):
                core = dom % 2
                partner = (((z - core) % ZLEN ^ bits) + core) % ZLEN * columns + y
                pairs.append((grid * dom_size + dom, partner * dom_size + dom))
        return lax.ppermute(v, ("grid", "dom"), pairs)

    across = lambda v: lax.ppermute(v, "grid", [(i, i ^ 1) for i in range(grid_size)])

    up = [(i, i + 1) for i in range(dom_size - 1)]
    down = [(j, i) for i, j in up]
    before = lax.ppermute(values[rows - STEPS :], "dom", up)
    after = lax.ppermute(values[:STEPS], "dom", down)
    numbers = [levels[0].astype(jnp.float32), weights.astype(jnp.float32), diffusion[0], drift[0]]
    facts = jnp.concatenate(numbers)
    stepped, *inner = inner_steps(facts, values)
    inner = [inner[0]] + [swap(inner[k], 2 * k) for k in ORDER]
    stepped, *outer = outer_steps(facts, values, before, after, stepped)
    held = lax.optimization_barrier((*inner, *outer))
    inner, outer = held[:QUARTERS], held[QUARTERS:]
    outer = [outer[0]] + [swap(outer[k], 2 * k) for k in ORDER]
    stepped = stepped.reshape(rows, points, -1)

    table = jnp.asarray(placing_table(), jnp.bfloat16)
    sums = []
    for pieces in ([], outer):
        theirs, mine = combine(table, inner, pieces, grid_size)
        partial = mine + swap(theirs, 1)
        sums.append(partial + across(partial))

    plus = [(i, (i + columns) % grid_size) for i in range(grid_size)]
    minus = [(j, i) for i, j in plus]
    matrix = jnp.asarray(fill_matrix(), jnp.bfloat16)

    def spots(source, edge):
        source = jnp.bitwise_and(source + ZLEN, ZLEN - 1)
        begin = STEPS + 3 * source
        if not edge:
            return [begin, begin + 1]
        side = jnp.bitwise_and(source, 1) * (rows - STEPS)
        return [begin + 2, side + jnp.right_shift(source, 1)]

    ups, downs = list(sums), list(sums)
    chunks = list(sums)
    where = spots(place, 0) + spots(place, 1)
    for hop in range(1, ZLEN // 2):
        for s in range(2):
            next_up = lax.ppermute(ups[s], "grid", plus)
            next_down = lax.ppermute(downs[s], "grid", minus)
            ups[s], downs[s] = next_up, next_down
            chunks += [next_up, next_down]
            where += spots(place - hop, s) + spots(place + hop, s)
    last = [lax.ppermute(ups[0], "grid", plus), lax.ppermute(downs[1], "grid", minus)]
    combined = fill(jnp.stack(where), matrix, chunks, rows, None)
    last, combined = lax.optimization_barrier((last, combined))
    spot = spots(place + ZLEN // 2, 0) + spots(place + ZLEN // 2, 1)
    combined = fill(jnp.stack(spot), matrix, last, rows, combined)
    return stepped[None], combined.reshape(rows, MLEN, MLEN, MLEN, -1)


def solution(mesh):
    in_specs = (
        P("grid", "dom", None, None),
        P("grid", None),
        P("grid", None),
        P("grid", None),
        P("grid"),
    )
    out_specs = (P("grid", "dom", None, None), P("dom", None, None, None, None))
    return jax.shard_map(
        per_device, mesh=mesh, in_specs=in_specs, out_specs=out_specs, check_vma=False
    )
```

time: 120 us -> 101 us (0.84); the launches traced: 118 us -> 101 us
  starting transfers between devices: 58.8 us -> 45.2 us
  local copies, waits for them, and re-layouts: 6.27 us -> 3.59 us
  Pallas kernels: 19 us -> 17.6 us
    ppermute x28 -> x22, starting transfers between devices: 51.3 us -> 37.6 us  [the longest x8 17.6 us: swap(): return lax.ppermute(v, ('grid', 'dom'), pairs)]
    pallas_call x4 -> x2, Pallas kernels: 8.55 us -> 5.77 us  [fill(): pl.pallas_call(lambda *refs: fill_kernel(chunks, width, with_base, *refs)...]
    ppermute x1, waiting for transfers between devices: 1.97 us -> 3.79 us  [per_device(): before = lax.ppermute(values[rows - STEPS:], 'dom', up)]
    ppermute x1, starting transfers between devices: 1.75 us -> 0.01 us  [per_device(): lax.ppermute(ups[0], 'grid', plus)]
    ppermute x1, starting transfers between devices: 1.49 us -> 3.23 us  [per_device(): lax.ppermute(downs[1], 'grid', minus)]
    ppermute x1, waiting for transfers between devices: 1.52 us -> 0.01 us  [per_device(): lax.ppermute(ups[0], 'grid', plus)]
    pallas_call x3 -> x4, Pallas kernels: 10.4 us -> 11.9 us  [the longest x2 10.8 us: step_call(): pl.pallas_call(lambda *refs: kernel(rows, points, *refs), out_shape=[jax....]
    unnamed x10 -> x8, local copies, waits for them, and re-layouts: 4.42 us -> 3.47 us
  transfers between devices with their start and end apart: 32 -> 26, of which waited for: 15 -> 15; matrix products, arithmetic and copies ran while one was open for 2% -> 0% of each run, Pallas kernels for 6% -> 9%
where the time goes in v3:
time: 101 us
  starting transfers between devices  45.2 us (45%)
  waiting for transfers between devices  31 us (31%)
  Pallas kernels  17.6 us (17%)
  local copies, waits for them, and re-layouts  3.59 us (4%)
  other arithmetic  1.6 us (2%)
  between operations  1.57 us (2%)
    ppermute x8, starting transfers between devices, swap(): return lax.ppermute(v, ('grid', 'dom'), pairs)  17.6 us
    ppermute x6, starting transfers between devices, per_device(): next_down = lax.ppermute(downs[s], 'grid', minus)  13.4 us
    pallas_call x2, Pallas kernels, step_call(): pl.pallas_call(lambda *refs: kernel(rows, points, *refs), out_shape=[jax....  10.8 us
    ppermute x8, waiting for transfers between devices, swap(): return lax.ppermute(v, ('grid', 'dom'), pairs)  10.8 us
    ppermute x6, waiting for transfers between devices, per_device(): next_down = lax.ppermute(downs[s], 'grid', minus)  10.3 us
    pallas_call x2, Pallas kernels, fill(): pl.pallas_call(lambda *refs: fill_kernel(chunks, width, with_base, *refs)...  5.77 us
    ppermute x1, waiting for transfers between devices, per_device(): before = lax.ppermute(values[rows - STEPS:], 'dom', up)  3.79 us
    ppermute x6, starting transfers between devices, per_device(): next_up = lax.ppermute(ups[s], 'grid', plus)  3.67 us
  transfers between devices with their start and end apart: 26, of which 15 were waited for; matrix products, arithmetic and copies ran while one was open for 0% of the time, Pallas kernels for 9%

profile of v3, /device:TPU:6, one launch (start us, length us, event | category | flops | bytes accessed | tf_op | source)
XLA Modules:
  0.0 100.5 jit_solution(8562934902029901006)
XLA Ops:
  3.9 6.4 %inner_steps.1 = (f32[2048,128]{1,0:T(8,128)}, f32[392,128]{1,0:T(8,128)S(1)}, f32[392,128]{1,0:T(8,128)S(1)}, f32[392,128]{1,0:T(8,128)S(1)}, f32[392,128]{1,0:T(8,128)S(1)}) custom-call(f32[14]{0:T(128)S(1)} %pad_maximum_fusion.refs_0_, f32[2048,128]{1,0:T(8,128)S(1)} %bitcast.45), custom_call_target="tpu_custom_call" | custom-call | flops 26214400 | bytes 3145728 | tf_op jit(solution)/shard_map/inner_steps/pallas_call | solution.py:272
  10.4 7.2 %collective-permute-start.2 = (f32[392,128]{1,0:T(8,128)S(1)}, f32[392,128]{1,0:T(8,128)S(1)}, u32[]{:S(2)}, u32[]{:S(2)}) collective-permute-start(f32[392,128]{1,0:T(8,128)S(1)} %get-tuple-element.30), channel_id=1, source_target_pairs={{0,128},{1,129},{2,130},{3,131},{4,132},{5,133},{6,134},{7,135},{8... | collective-permute-start | bytes 602120 | tf_op jit(solution)/shard_map/ppermute | solution.py:444
  17.6 1.5 %collective-permute-start.3 = (f32[392,128]{1,0:T(8,128)S(1)}, f32[392,128]{1,0:T(8,128)S(1)}, u32[]{:S(2)}, u32[]{:S(2)}) collective-permute-start(f32[392,128]{1,0:T(8,128)S(1)} %get-tuple-element.31), channel_id=1, source_target_pairs={{0,64},{1,193},{2,66},{3,195},{4,68},{5,197},{6,70},{7,199},{8,72}... | collective-permute-start | bytes 602120 | tf_op jit(solution)/shard_map/ppermute | solution.py:444
  19.1 1.9 %collective-permute-start.1 = (f32[4,64,128]{2,1,0:T(8,128)S(1)}, f32[4,64,128]{2,1,0:T(8,128)S(1)}, u32[]{:S(2)}, u32[]{:S(2)}) collective-permute-start(f32[4,64,128]{2,1,0:T(8,128)S(1)} %get-tuple-element.52), channel_id=1, source_target_pairs={{1,0},{2,1},{3,2},{4,3},{5,4},{6,5},{7,6},{8,7},{9,8},{10,9},{11,1... | collective-permute-start | bytes 393224 | tf_op jit(solution)/shard_map/ppermute | solution.py:451
  21.1 2.4 %collective-permute-start = (f32[4,64,128]{2,1,0:T(8,128)S(1)}, f32[4,64,128]{2,1,0:T(8,128)S(1)}, u32[]{:S(2)}, u32[]{:S(2)}) collective-permute-start(f32[4,64,128]{2,1,0:T(8,128)S(1)} %get-tuple-element.53), channel_id=1, source_target_pairs={{0,1},{1,2},{2,3},{3,4},{4,5},{5,6},{6,7},{7,8},{8,9},{9,10},{10,1... | collective-permute-start | bytes 393224 | tf_op jit(solution)/shard_map/ppermute | solution.py:450
  23.6 3.8 %collective-permute-done = f32[4,64,128]{2,1,0:T(8,128)S(1)} collective-permute-done((f32[4,64,128]{2,1,0:T(8,128)S(1)}, f32[4,64,128]{2,1,0:T(8,128)S(1)}, u32[]{:S(2)}, u32[]{:S(2)}) %collective-permute-start) | collective-permute-done | bytes 131104 | tf_op jit(solution)/shard_map/ppermute | solution.py:450
  27.4 4.4 %outer_steps.1 = (f32[2048,128]{1,0:T(8,128)}, f32[128,128]{1,0:T(8,128)S(1)}, f32[128,128]{1,0:T(8,128)S(1)}, f32[128,128]{1,0:T(8,128)S(1)}, f32[128,128]{1,0:T(8,128)S(1)}) custom-call(f32[14]{0:T(128)S(1)} %pad_maximum_fusion.refs_0_, f32[2048,128]{1,0:T(8,128)S(1)} %bitcast.46, f32[256,128]{1,0:T(8,128)S(1)} %bitcast.48, ...), custom_call_target="tpu_custom_call", output_to_operand_aliasing={{0}: (4, {})} | custom-call | flops 19660800 | bytes 2359296 | tf_op jit(solution)/shard_map/outer_steps/pallas_call | solution.py:272
  31.8 4.3 %collective-permute-done.3.refs_3_ = f32[392,128]{1,0:T(8,128)S(1)} collective-permute-done((f32[392,128]{1,0:T(8,128)S(1)}, f32[392,128]{1,0:T(8,128)S(1)}, u32[]{:S(2)}, u32[]{:S(2)}) %collective-permute-start.3) | collective-permute-done | bytes 200736 | tf_op jit(solution)/shard_map/ppermute | solution.py:444
  36.1 1.8 %collective-permute-start.11 = (f32[128,128]{1,0:T(8,128)S(1)}, f32[128,128]{1,0:T(8,128)S(1)}, u32[]{:S(2)}, u32[]{:S(2)}) collective-permute-start(f32[128,128]{1,0:T(8,128)S(1)} %get-tuple-element.44), channel_id=1, source_target_pairs={{0,128},{1,129},{2,130},{3,131},{4,132},{5,133},{6,134},{7,135},{8... | collective-permute-start | bytes 196616 | tf_op jit(solution)/shard_map/ppermute | solution.py:444
  37.9 3.6 %collective-permute-start.12 = (f32[128,128]{1,0:T(8,128)S(1)}, f32[128,128]{1,0:T(8,128)S(1)}, u32[]{:S(2)}, u32[]{:S(2)}) collective-permute-start(f32[128,128]{1,0:T(8,128)S(1)} %get-tuple-element.45), channel_id=1, source_target_pairs={{0,64},{1,193},{2,66},{3,195},{4,68},{5,197},{6,70},{7,199},{8,72}... | collective-permute-start | bytes 196616 | tf_op jit(solution)/shard_map/ppermute | solution.py:444
  44.8 2.5 %collective-permute-done.12.refs_7_ = f32[128,128]{1,0:T(8,128)S(1)} collective-permute-done((f32[128,128]{1,0:T(8,128)S(1)}, f32[128,128]{1,0:T(8,128)S(1)}, u32[]{:S(2)}, u32[]{:S(2)}) %collective-permute-start.12) | collective-permute-done | bytes 65568 | tf_op jit(solution)/shard_map/ppermute | solution.py:444
  47.3 1.3 %collective-permute-done.13.refs_8_ = f32[128,128]{1,0:T(8,128)S(1)} collective-permute-done((f32[128,128]{1,0:T(8,128)S(1)}, f32[128,128]{1,0:T(8,128)S(1)}, u32[]{:S(2)}, u32[]{:S(2)}) %collective-permute-start.13) | collective-permute-done | bytes 65568 | tf_op jit(solution)/shard_map/ppermute | solution.py:444
  50.2 1.9 %collective-permute-start.14 = (f32[2,208,128]{2,1,0:T(8,128)S(1)}, f32[2,208,128]{2,1,0:T(8,128)S(1)}, u32[]{:S(2)}, u32[]{:S(2)}) collective-permute-start(f32[2,208,128]{2,1,0:T(8,128)S(1)} %get-tuple-element.48), channel_id=1, source_target_pairs={{0,32},{1,225},{2,34},{3,227},{4,36},{5,229},{6,38},{7,231},{8,40}... | collective-permute-start | bytes 638984 | tf_op jit(solution)/shard_map/ppermute | solution.py:444
  52.1 1.4 %collective-permute-start.6 = (f32[2,208,128]{2,1,0:T(8,128)S(1)}, f32[2,208,128]{2,1,0:T(8,128)S(1)}, u32[]{:S(2)}, u32[]{:S(2)}) collective-permute-start(f32[2,208,128]{2,1,0:T(8,128)S(1)} %add.215), channel_id=1, source_target_pairs={{0,16},{16,0},{32,48},{48,32},{64,80},{80,64},{96,112},{112,96},{1... | collective-permute-start | bytes 638984 | tf_op jit(solution)/shard_map/ppermute | solution.py:446
  53.6 2.6 %collective-permute-done.14 = f32[2,208,128]{2,1,0:T(8,128)S(1)} collective-permute-done((f32[2,208,128]{2,1,0:T(8,128)S(1)}, f32[2,208,128]{2,1,0:T(8,128)S(1)}, u32[]{:S(2)}, u32[]{:S(2)}) %collective-permute-start.14) | collective-permute-done | bytes 213024 | tf_op jit(solution)/shard_map/ppermute | solution.py:444
  56.2 1.5 %collective-permute-start.15 = (f32[2,208,128]{2,1,0:T(8,128)S(1)}, f32[2,208,128]{2,1,0:T(8,128)S(1)}, u32[]{:S(2)}, u32[]{:S(2)}) collective-permute-start(f32[2,208,128]{2,1,0:T(8,128)S(1)} %add.217), channel_id=1, source_target_pairs={{0,16},{16,0},{32,48},{48,32},{64,80},{80,64},{96,112},{112,96},{1... | collective-permute-start | bytes 638984 | tf_op jit(solution)/shard_map/ppermute | solution.py:446
  58.3 1.6 %collective-permute-start.7 = (f32[2,208,128]{2,1,0:T(8,128)S(1)}, f32[2,208,128]{2,1,0:T(8,128)S(1)}, u32[]{:S(2)}, u32[]{:S(2)}) collective-permute-start(f32[2,208,128]{2,1,0:T(8,128)S(1)} %add.216.refs_2_), channel_id=1, source_target_pairs={{0,32},{16,48},{32,64},{48,80},{64,96},{80,112},{96,128},{112,144}... | collective-permute-start | bytes 638984 | tf_op jit(solution)/shard_map/ppermute | solution.py:486
  59.9 2.7 %collective-permute-done.15 = f32[2,208,128]{2,1,0:T(8,128)S(1)} collective-permute-done((f32[2,208,128]{2,1,0:T(8,128)S(1)}, f32[2,208,128]{2,1,0:T(8,128)S(1)}, u32[]{:S(2)}, u32[]{:S(2)}) %collective-permute-start.15) | collective-permute-done | bytes 213024 | tf_op jit(solution)/shard_map/ppermute | solution.py:446
  62.7 1.5 %collective-permute-start.16 = (f32[2,208,128]{2,1,0:T(8,128)S(1)}, f32[2,208,128]{2,1,0:T(8,128)S(1)}, u32[]{:S(2)}, u32[]{:S(2)}) collective-permute-start(f32[2,208,128]{2,1,0:T(8,128)S(1)} %add.218.refs_3_), channel_id=1, source_target_pairs={{32,0},{48,16},{64,32},{80,48},{96,64},{112,80},{128,96},{144,112}... | collective-permute-start | bytes 638984 | tf_op jit(solution)/shard_map/ppermute | solution.py:487
  66.8 4.1 %collective-permute-done.16.refs_7_ = f32[2,208,128]{2,1,0:T(8,128)S(1)} collective-permute-done((f32[2,208,128]{2,1,0:T(8,128)S(1)}, f32[2,208,128]{2,1,0:T(8,128)S(1)}, u32[]{:S(2)}, u32[]{:S(2)}) %collective-permute-start.16) | collective-permute-done | bytes 213024 | tf_op jit(solution)/shard_map/ppermute | solution.py:487
  70.9 2.6 %collective-permute-start.17 = (f32[2,208,128]{2,1,0:T(8,128)S(1)}, f32[2,208,128]{2,1,0:T(8,128)S(1)}, u32[]{:S(2)}, u32[]{:S(2)}) collective-permute-start(f32[2,208,128]{2,1,0:T(8,128)S(1)} %collective-permute-done.16.refs_7_), channel_id=1, source_target_pairs={{32,0},{48,16},{64,32},{80,48},{96,64},{112,80},{128,96},{144,112}... | collective-permute-start | bytes 638984 | tf_op jit(solution)/shard_map/ppermute | solution.py:487
  73.5 2.0 %collective-permute-done.20.refs_5_ = f32[2,208,128]{2,1,0:T(8,128)S(1)} collective-permute-done((f32[2,208,128]{2,1,0:T(8,128)S(1)}, f32[2,208,128]{2,1,0:T(8,128)S(1)}, u32[]{:S(2)}, u32[]{:S(2)}) %collective-permute-start.20) | collective-permute-done | bytes 213024 | tf_op jit(solution)/shard_map/ppermute | solution.py:487
  75.5 2.6 %collective-permute-start.22 = (f32[2,208,128]{2,1,0:T(8,128)S(1)}, f32[2,208,128]{2,1,0:T(8,128)S(1)}, u32[]{:S(2)}, u32[]{:S(2)}) collective-permute-start(f32[2,208,128]{2,1,0:T(8,128)S(1)} %collective-permute-done.20.refs_5_), channel_id=1, source_target_pairs={{32,0},{48,16},{64,32},{80,48},{96,64},{112,80},{128,96},{144,112}... | collective-permute-start | bytes 638984 | tf_op jit(solution)/shard_map/ppermute | solution.py:487
  78.4 1.6 %collective-permute-done.17.refs_11_ = f32[2,208,128]{2,1,0:T(8,128)S(1)} collective-permute-done((f32[2,208,128]{2,1,0:T(8,128)S(1)}, f32[2,208,128]{2,1,0:T(8,128)S(1)}, u32[]{:S(2)}, u32[]{:S(2)}) %collective-permute-start.17) | collective-permute-done | bytes 213024 | tf_op jit(solution)/shard_map/ppermute | solution.py:487
  80.1 2.9 %collective-permute-start.18 = (f32[2,208,128]{2,1,0:T(8,128)S(1)}, f32[2,208,128]{2,1,0:T(8,128)S(1)}, u32[]{:S(2)}, u32[]{:S(2)}) collective-permute-start(f32[2,208,128]{2,1,0:T(8,128)S(1)} %collective-permute-done.17.refs_11_), channel_id=1, source_target_pairs={{32,0},{48,16},{64,32},{80,48},{96,64},{112,80},{128,96},{144,112}... | collective-permute-start | bytes 638984 | tf_op jit(solution)/shard_map/ppermute | solution.py:487
  82.9 1.7 %collective-permute-done.22.refs_9_ = f32[2,208,128]{2,1,0:T(8,128)S(1)} collective-permute-done((f32[2,208,128]{2,1,0:T(8,128)S(1)}, f32[2,208,128]{2,1,0:T(8,128)S(1)}, u32[]{:S(2)}, u32[]{:S(2)}) %collective-permute-start.22) | collective-permute-done | bytes 213024 | tf_op jit(solution)/shard_map/ppermute | solution.py:487
  84.6 2.9 %collective-permute-start.24 = (f32[2,208,128]{2,1,0:T(8,128)S(1)}, f32[2,208,128]{2,1,0:T(8,128)S(1)}, u32[]{:S(2)}, u32[]{:S(2)}) collective-permute-start(f32[2,208,128]{2,1,0:T(8,128)S(1)} %collective-permute-done.22.refs_9_), channel_id=1, source_target_pairs={{32,0},{48,16},{64,32},{80,48},{96,64},{112,80},{128,96},{144,112}... | collective-permute-start | bytes 638984 | tf_op jit(solution)/shard_map/ppermute | solution.py:487
  87.7 1.5 %collective-permute-done.9.refs_12_ = f32[2,208,128]{2,1,0:T(8,128)S(1)} collective-permute-done((f32[2,208,128]{2,1,0:T(8,128)S(1)}, f32[2,208,128]{2,1,0:T(8,128)S(1)}, u32[]{:S(2)}, u32[]{:S(2)}) %collective-permute-start.9) | collective-permute-done | bytes 213024 | tf_op jit(solution)/shard_map/ppermute | solution.py:486
  89.2 3.2 %collective-permute-start.19 = (f32[2,208,128]{2,1,0:T(8,128)S(1)}, f32[2,208,128]{2,1,0:T(8,128)S(1)}, u32[]{:S(2)}, u32[]{:S(2)}) collective-permute-start(f32[2,208,128]{2,1,0:T(8,128)S(1)} %collective-permute-done.18.refs_15_), channel_id=1, source_target_pairs={{32,0},{48,16},{64,32},{80,48},{96,64},{112,80},{128,96},{144,112}... | collective-permute-start | bytes 638984 | tf_op jit(solution)/shard_map/ppermute | solution.py:491
  93.3 1.3 %collective-permute-done.25.refs_14_ = f32[2,208,128]{2,1,0:T(8,128)S(1)} collective-permute-done((f32[2,208,128]{2,1,0:T(8,128)S(1)}, f32[2,208,128]{2,1,0:T(8,128)S(1)}, u32[]{:S(2)}, u32[]{:S(2)}) %collective-permute-start.25) | collective-permute-done | bytes 213024 | tf_op jit(solution)/shard_map/ppermute | solution.py:486
  94.6 4.0 %fill.2.refs_4_ = f32[32,512,128]{2,1,0:T(8,128)} custom-call(s32[28]{0:T(128)S(1)} %stack.135.refs_0_, bf16[512,256]{1,0:T(8,128)(2,1)S(1)} %copy-done.3, f32[2,208,128]{2,1,0:T(8,128)S(1)} %add.216.refs_2_, f32[2,208,128]{2,1,0:T(8,128)S(1)} %add.218.refs_3_, f32[2,208,128]{2,1,0:T(8,128)S(1)} %collective-permute-done.7.refs_4_, ...), custom_call_target="tpu_custom_call" | custom-call | flops 2818572288 | bytes 10321920 | tf_op jit(solution)/shard_map/fill/pallas_call | solution.py:408
  98.6 1.8 %fill.3 = f32[32,512,128]{2,1,0:T(8,128)} custom-call(s32[4]{0:T(128)S(1)} %pad_add_fusion.refs_0_, bf16[512,256]{1,0:T(8,128)(2,1)S(1)} %copy-done.3, f32[2,208,128]{2,1,0:T(8,128)S(1)} %collective-permute-done.10.refs_2_, f32[2,208,128]{2,1,0:T(8,128)S(1)} %collective-permute-done.19.refs_3_, ...), custom_call_target="tpu_custom_call", output_to_operand_aliasing={{}: (4, {})} | custom-call | flops 402653184 | bytes 1474560 | tf_op jit(solution)/shard_map/fill/pallas_call | solution.py:408
  (43 shorter events, 12.4 us)
Async XLA Ops:
  2.7 1.2 %copy-start = (f32[1,32,64,128]{3,2,1,0:T(8,128)S(1)}, f32[1,32,64,128]{3,2,1,0:T(8,128)}, u32[]{:S(2)}) copy-start(f32[1,32,64,128]{3,2,1,0:T(8,128)} %param.7) | copy-start | bytes 3145732
  3.9 90.7 %copy-start.3 = (bf16[512,256]{1,0:T(8,128)(2,1)S(1)}, bf16[512,256]{1,0:T(8,128)(2,1)}, u32[]{:S(2)}) copy-start(bf16[512,256]{1,0:T(8,128)(2,1)} %constant.69.clone.refs_1_) | copy-start | bytes 786436
  10.4 21.4 %collective-permute-start.2 = (f32[392,128]{1,0:T(8,128)S(1)}, f32[392,128]{1,0:T(8,128)S(1)}, u32[]{:S(2)}, u32[]{:S(2)}) collective-permute-start(f32[392,128]{1,0:T(8,128)S(1)} %get-tuple-element.30), channel_id=1, source_target_pairs={{0,128},{1,129},{2,130},{3,131},{4,132},{5,133},{6,134},{7,135},{8... | collective-permute-start | bytes 602120 | tf_op jit(solution)/shard_map/ppermute | solution.py:444
  17.6 18.5 %collective-permute-start.3 = (f32[392,128]{1,0:T(8,128)S(1)}, f32[392,128]{1,0:T(8,128)S(1)}, u32[]{:S(2)}, u32[]{:S(2)}) collective-permute-start(f32[392,128]{1,0:T(8,128)S(1)} %get-tuple-element.31), channel_id=1, source_target_pairs={{0,64},{1,193},{2,66},{3,195},{4,68},{5,197},{6,70},{7,199},{8,72}... | collective-permute-start | bytes 602120 | tf_op jit(solution)/shard_map/ppermute | solution.py:444
  19.1 17.0 %collective-permute-start.4 = (f32[392,128]{1,0:T(8,128)S(1)}, f32[392,128]{1,0:T(8,128)S(1)}, u32[]{:S(2)}, u32[]{:S(2)}) collective-permute-start(f32[392,128]{1,0:T(8,128)S(1)} %get-tuple-element.32), channel_id=1, source_target_pairs={{0,192},{1,65},{2,194},{3,67},{4,196},{5,69},{6,198},{7,71},{8,200... | collective-permute-start | bytes 602120 | tf_op jit(solution)/shard_map/ppermute | solution.py:444
  19.1 4.4 %collective-permute-start.1 = (f32[4,64,128]{2,1,0:T(8,128)S(1)}, f32[4,64,128]{2,1,0:T(8,128)S(1)}, u32[]{:S(2)}, u32[]{:S(2)}) collective-permute-start(f32[4,64,128]{2,1,0:T(8,128)S(1)} %get-tuple-element.52), channel_id=1, source_target_pairs={{1,0},{2,1},{3,2},{4,3},{5,4},{6,5},{7,6},{8,7},{9,8},{10,9},{11,1... | collective-permute-start | bytes 393224 | tf_op jit(solution)/shard_map/ppermute | solution.py:451
  21.1 6.3 %collective-permute-start = (f32[4,64,128]{2,1,0:T(8,128)S(1)}, f32[4,64,128]{2,1,0:T(8,128)S(1)}, u32[]{:S(2)}, u32[]{:S(2)}) collective-permute-start(f32[4,64,128]{2,1,0:T(8,128)S(1)} %get-tuple-element.53), channel_id=1, source_target_pairs={{0,1},{1,2},{2,3},{3,4},{4,5},{5,6},{6,7},{7,8},{8,9},{9,10},{10,1... | collective-permute-start | bytes 393224 | tf_op jit(solution)/shard_map/ppermute | solution.py:450
  36.1 8.7 %collective-permute-start.11 = (f32[128,128]{1,0:T(8,128)S(1)}, f32[128,128]{1,0:T(8,128)S(1)}, u32[]{:S(2)}, u32[]{:S(2)}) collective-permute-start(f32[128,128]{1,0:T(8,128)S(1)} %get-tuple-element.44), channel_id=1, source_target_pairs={{0,128},{1,129},{2,130},{3,131},{4,132},{5,133},{6,134},{7,135},{8... | collective-permute-start | bytes 196616 | tf_op jit(solution)/shard_map/ppermute | solution.py:444
  37.9 9.4 %collective-permute-start.12 = (f32[128,128]{1,0:T(8,128)S(1)}, f32[128,128]{1,0:T(8,128)S(1)}, u32[]{:S(2)}, u32[]{:S(2)}) collective-permute-start(f32[128,128]{1,0:T(8,128)S(1)} %get-tuple-element.45), channel_id=1, source_target_pairs={{0,64},{1,193},{2,66},{3,195},{4,68},{5,197},{6,70},{7,199},{8,72}... | collective-permute-start | bytes 196616 | tf_op jit(solution)/shard_map/ppermute | solution.py:444
  41.5 7.1 %collective-permute-start.13 = (f32[128,128]{1,0:T(8,128)S(1)}, f32[128,128]{1,0:T(8,128)S(1)}, u32[]{:S(2)}, u32[]{:S(2)}) collective-permute-start(f32[128,128]{1,0:T(8,128)S(1)} %get-tuple-element.46), channel_id=1, source_target_pairs={{0,192},{1,65},{2,194},{3,67},{4,196},{5,69},{6,198},{7,71},{8,200... | collective-permute-start | bytes 196616 | tf_op jit(solution)/shard_map/ppermute | solution.py:444
  42.6 1.1 %copy-start.1 = (bf16[7,208,192]{2,1,0:T(8,128)(2,1)S(1)}, bf16[7,208,192]{2,1,0:T(8,128)(2,1)}, u32[]{:S(2)}) copy-start(bf16[7,208,192]{2,1,0:T(8,128)(2,1)} %constant.68.clone.refs_0_) | copy-start | bytes 1677316
  44.2 7.9 %collective-permute-start.5 = (f32[2,208,128]{2,1,0:T(8,128)S(1)}, f32[2,208,128]{2,1,0:T(8,128)S(1)}, u32[]{:S(2)}, u32[]{:S(2)}) collective-permute-start(f32[2,208,128]{2,1,0:T(8,128)S(1)} %get-tuple-element.42), channel_id=1, source_target_pairs={{0,32},{1,225},{2,34},{3,227},{4,36},{5,229},{6,38},{7,231},{8,40}... | collective-permute-start | bytes 638984 | tf_op jit(solution)/shard_map/ppermute | solution.py:444
  48.6 1.1 %copy-start.2 = (bf16[7,208,192]{2,1,0:T(8,128)(2,1)S(1)}, bf16[7,208,192]{2,1,0:T(8,128)(2,1)}, u32[]{:S(2)}) copy-start(bf16[7,208,192]{2,1,0:T(8,128)(2,1)} %constant.68.clone.refs_0_) | copy-start | bytes 1677316
  50.2 5.9 %collective-permute-start.14 = (f32[2,208,128]{2,1,0:T(8,128)S(1)}, f32[2,208,128]{2,1,0:T(8,128)S(1)}, u32[]{:S(2)}, u32[]{:S(2)}) collective-permute-start(f32[2,208,128]{2,1,0:T(8,128)S(1)} %get-tuple-element.48), channel_id=1, source_target_pairs={{0,32},{1,225},{2,34},{3,227},{4,36},{5,229},{6,38},{7,231},{8,40}... | collective-permute-start | bytes 638984 | tf_op jit(solution)/shard_map/ppermute | solution.py:444
  52.1 6.1 %collective-permute-start.6 = (f32[2,208,128]{2,1,0:T(8,128)S(1)}, f32[2,208,128]{2,1,0:T(8,128)S(1)}, u32[]{:S(2)}, u32[]{:S(2)}) collective-permute-start(f32[2,208,128]{2,1,0:T(8,128)S(1)} %add.215), channel_id=1, source_target_pairs={{0,16},{16,0},{32,48},{48,32},{64,80},{80,64},{96,112},{112,96},{1... | collective-permute-start | bytes 638984 | tf_op jit(solution)/shard_map/ppermute | solution.py:446
  56.2 6.4 %collective-permute-start.15 = (f32[2,208,128]{2,1,0:T(8,128)S(1)}, f32[2,208,128]{2,1,0:T(8,128)S(1)}, u32[]{:S(2)}, u32[]{:S(2)}) collective-permute-start(f32[2,208,128]{2,1,0:T(8,128)S(1)} %add.217), channel_id=1, source_target_pairs={{0,16},{16,0},{32,48},{48,32},{64,80},{80,64},{96,112},{112,96},{1... | collective-permute-start | bytes 638984 | tf_op jit(solution)/shard_map/ppermute | solution.py:446
  58.3 7.9 %collective-permute-start.7 = (f32[2,208,128]{2,1,0:T(8,128)S(1)}, f32[2,208,128]{2,1,0:T(8,128)S(1)}, u32[]{:S(2)}, u32[]{:S(2)}) collective-permute-start(f32[2,208,128]{2,1,0:T(8,128)S(1)} %add.216.refs_2_), channel_id=1, source_target_pairs={{0,32},{16,48},{32,64},{48,80},{64,96},{80,112},{96,128},{112,144}... | collective-permute-start | bytes 638984 | tf_op jit(solution)/shard_map/ppermute | solution.py:486
  62.7 8.3 %collective-permute-start.16 = (f32[2,208,128]{2,1,0:T(8,128)S(1)}, f32[2,208,128]{2,1,0:T(8,128)S(1)}, u32[]{:S(2)}, u32[]{:S(2)}) collective-permute-start(f32[2,208,128]{2,1,0:T(8,128)S(1)} %add.218.refs_3_), channel_id=1, source_target_pairs={{32,0},{48,16},{64,32},{80,48},{96,64},{112,80},{128,96},{144,112}... | collective-permute-start | bytes 638984 | tf_op jit(solution)/shard_map/ppermute | solution.py:487
  64.1 11.4 %collective-permute-start.20 = (f32[2,208,128]{2,1,0:T(8,128)S(1)}, f32[2,208,128]{2,1,0:T(8,128)S(1)}, u32[]{:S(2)}, u32[]{:S(2)}) collective-permute-start(f32[2,208,128]{2,1,0:T(8,128)S(1)} %add.216.refs_2_), channel_id=1, source_target_pairs={{32,0},{48,16},{64,32},{80,48},{96,64},{112,80},{128,96},{144,112}... | collective-permute-start | bytes 638984 | tf_op jit(solution)/shard_map/ppermute | solution.py:487
  65.1 13.0 %collective-permute-start.21 = (f32[2,208,128]{2,1,0:T(8,128)S(1)}, f32[2,208,128]{2,1,0:T(8,128)S(1)}, u32[]{:S(2)}, u32[]{:S(2)}) collective-permute-start(f32[2,208,128]{2,1,0:T(8,128)S(1)} %add.218.refs_3_), channel_id=1, source_target_pairs={{0,32},{16,48},{32,64},{48,80},{64,96},{80,112},{96,128},{112,144}... | collective-permute-start | bytes 638984 | tf_op jit(solution)/shard_map/ppermute | solution.py:486
  66.2 11.9 %collective-permute-start.8 = (f32[2,208,128]{2,1,0:T(8,128)S(1)}, f32[2,208,128]{2,1,0:T(8,128)S(1)}, u32[]{:S(2)}, u32[]{:S(2)}) collective-permute-start(f32[2,208,128]{2,1,0:T(8,128)S(1)} %collective-permute-done.7.refs_4_), channel_id=1, source_target_pairs={{0,32},{16,48},{32,64},{48,80},{64,96},{80,112},{96,128},{112,144}... | collective-permute-start | bytes 638984 | tf_op jit(solution)/shard_map/ppermute | solution.py:486
  70.9 9.1 %collective-permute-start.17 = (f32[2,208,128]{2,1,0:T(8,128)S(1)}, f32[2,208,128]{2,1,0:T(8,128)S(1)}, u32[]{:S(2)}, u32[]{:S(2)}) collective-permute-start(f32[2,208,128]{2,1,0:T(8,128)S(1)} %collective-permute-done.16.refs_7_), channel_id=1, source_target_pairs={{32,0},{48,16},{64,32},{80,48},{96,64},{112,80},{128,96},{144,112}... | collective-permute-start | bytes 638984 | tf_op jit(solution)/shard_map/ppermute | solution.py:487
  75.5 9.1 %collective-permute-start.22 = (f32[2,208,128]{2,1,0:T(8,128)S(1)}, f32[2,208,128]{2,1,0:T(8,128)S(1)}, u32[]{:S(2)}, u32[]{:S(2)}) collective-permute-start(f32[2,208,128]{2,1,0:T(8,128)S(1)} %collective-permute-done.20.refs_5_), channel_id=1, source_target_pairs={{32,0},{48,16},{64,32},{80,48},{96,64},{112,80},{128,96},{144,112}... | collective-permute-start | bytes 638984 | tf_op jit(solution)/shard_map/ppermute | solution.py:487
  78.1 9.4 %collective-permute-start.23 = (f32[2,208,128]{2,1,0:T(8,128)S(1)}, f32[2,208,128]{2,1,0:T(8,128)S(1)}, u32[]{:S(2)}, u32[]{:S(2)}) collective-permute-start(f32[2,208,128]{2,1,0:T(8,128)S(1)} %collective-permute-done.21.refs_6_), channel_id=1, source_target_pairs={{0,32},{16,48},{32,64},{48,80},{64,96},{80,112},{96,128},{112,144}... | collective-permute-start | bytes 638984 | tf_op jit(solution)/shard_map/ppermute | solution.py:486
  78.1 11.1 %collective-permute-start.9 = (f32[2,208,128]{2,1,0:T(8,128)S(1)}, f32[2,208,128]{2,1,0:T(8,128)S(1)}, u32[]{:S(2)}, u32[]{:S(2)}) collective-permute-start(f32[2,208,128]{2,1,0:T(8,128)S(1)} %collective-permute-done.8.refs_8_), channel_id=1, source_target_pairs={{0,32},{16,48},{32,64},{48,80},{64,96},{80,112},{96,128},{112,144}... | collective-permute-start | bytes 638984 | tf_op jit(solution)/shard_map/ppermute | solution.py:486
  80.1 9.1 %collective-permute-start.18 = (f32[2,208,128]{2,1,0:T(8,128)S(1)}, f32[2,208,128]{2,1,0:T(8,128)S(1)}, u32[]{:S(2)}, u32[]{:S(2)}) collective-permute-start(f32[2,208,128]{2,1,0:T(8,128)S(1)} %collective-permute-done.17.refs_11_), channel_id=1, source_target_pairs={{32,0},{48,16},{64,32},{80,48},{96,64},{112,80},{128,96},{144,112}... | collective-permute-start | bytes 638984 | tf_op jit(solution)/shard_map/ppermute | solution.py:487
  84.6 8.7 %collective-permute-start.24 = (f32[2,208,128]{2,1,0:T(8,128)S(1)}, f32[2,208,128]{2,1,0:T(8,128)S(1)}, u32[]{:S(2)}, u32[]{:S(2)}) collective-permute-start(f32[2,208,128]{2,1,0:T(8,128)S(1)} %collective-permute-done.22.refs_9_), channel_id=1, source_target_pairs={{32,0},{48,16},{64,32},{80,48},{96,64},{112,80},{128,96},{144,112}... | collective-permute-start | bytes 638984 | tf_op jit(solution)/shard_map/ppermute | solution.py:487
  87.5 7.1 %collective-permute-start.25 = (f32[2,208,128]{2,1,0:T(8,128)S(1)}, f32[2,208,128]{2,1,0:T(8,128)S(1)}, u32[]{:S(2)}, u32[]{:S(2)}) collective-permute-start(f32[2,208,128]{2,1,0:T(8,128)S(1)} %collective-permute-done.23.refs_10_), channel_id=1, source_target_pairs={{0,32},{16,48},{32,64},{48,80},{64,96},{80,112},{96,128},{112,144}... | collective-permute-start | bytes 638984 | tf_op jit(solution)/shard_map/ppermute | solution.py:486
  89.2 9.4 %collective-permute-start.10 = (f32[2,208,128]{2,1,0:T(8,128)S(1)}, f32[2,208,128]{2,1,0:T(8,128)S(1)}, u32[]{:S(2)}, u32[]{:S(2)}) collective-permute-start(f32[2,208,128]{2,1,0:T(8,128)S(1)} %collective-permute-done.9.refs_12_), channel_id=1, source_target_pairs={{0,32},{16,48},{32,64},{48,80},{64,96},{80,112},{96,128},{112,144}... | collective-permute-start | bytes 638984 | tf_op jit(solution)/shard_map/ppermute | solution.py:491
  89.2 9.4 %collective-permute-start.19 = (f32[2,208,128]{2,1,0:T(8,128)S(1)}, f32[2,208,128]{2,1,0:T(8,128)S(1)}, u32[]{:S(2)}, u32[]{:S(2)}) collective-permute-start(f32[2,208,128]{2,1,0:T(8,128)S(1)} %collective-permute-done.18.refs_15_), channel_id=1, source_target_pairs={{32,0},{48,16},{64,32},{80,48},{96,64},{112,80},{128,96},{144,112}... | collective-permute-start | bytes 638984 | tf_op jit(solution)/shard_map/ppermute | solution.py:491

commit v4 on v3

--- a/solution.py
+++ b/solution.py
@@ -314,7 +314,8 @@
 
 
 def combine_kernel(grids, edge, table_ref, *refs):
-    inner, outer = refs[:QUARTERS], refs[QUARTERS:-2]
+    inner, outer = refs[:QUARTERS], refs[QUARTERS:-2] if edge else []
+    outs = refs[-2:] if edge else refs[QUARTERS : QUARTERS + 2]
     half = inner[0].shape[0] // 2 // SUB * SUB
     lanes = inner[0].shape[1]
     mine = jnp.bitwise_and(shifted_place(), 1)
@@ -334,10 +335,14 @@
                 columns.append(head[pl.ds(begin + SUB, SUB), :])
         wide = jnp.concatenate(columns, axis=1) * scale
         stack = jnp.concatenate(split_three(wide), axis=0)
-        matrix = table_ref[jnp.clip(triple, 0, len(TRIPLES) - 1)]
+        if edge:
+            matrix = table_ref[index]
+        else:
+            matrix = table_ref[jnp.clip(triple, 0, len(TRIPLES) - 1)]
+            refs[-1][index] = matrix
         term = jnp.dot(matrix, stack, preferred_element_type=jnp.float32)
         total = term if total is None else total + term
-    for side, out_ref in enumerate(refs[-2:]):
+    for side, out_ref in enumerate(outs):
         for row in range(2):
             begin = (2 * side + row) * lanes
             out_ref[row] = total[:, begin : begin + lanes]
@@ -346,9 +351,10 @@
 def combine(table, inner, outer, grids):
     lanes = inner[0].shape[1]
     shape = jax.ShapeDtypeStruct((2, COUNT, lanes), jnp.float32)
+    chosen = jax.ShapeDtypeStruct((QUARTERS, *table.shape[1:]), table.dtype)
     return pl.pallas_call(
         lambda *refs: combine_kernel(grids, bool(outer), *refs),
-        out_shape=[shape, shape],
+        out_shape=[shape, shape] + ([] if outer else [chosen]),
         compiler_params=pltpu.CompilerParams(vmem_limit_bytes=24 * 2**20),
         cost_estimate=pl.CostEstimate(
             flops=2 * QUARTERS * 3 * SUB * COUNT * 4 * lanes, bytes_accessed=2**20, transcendentals=0
@@ -433,13 +439,13 @@
     columns = grid_size // ZLEN
     place = shifted_place()
 
-    def swap(v, bits):
+    def swap(v, bits, offset=0):
         pairs = []
         for grid in range(grid_size):
             z, y = divmod(grid, columns)
             for dom in range(dom_size):
-                core = dom % 2
-                partner = (((z - core) % ZLEN ^ bits) + core) % ZLEN * columns + y
+                origin = dom % 2 + offset
+                partner = (((z - origin) % ZLEN ^ bits) + origin) % ZLEN * columns + y
                 pairs.append((grid * dom_size + dom, partner * dom_size + dom))
         return lax.ppermute(v, ("grid", "dom"), pairs)
 
@@ -454,20 +460,18 @@
     stepped, *inner = inner_steps(facts, values)
     inner = [inner[0]] + [swap(inner[k], 2 * k) for k in ORDER]
     stepped, *outer = outer_steps(facts, values, before, after, stepped)
-    held = lax.optimization_barrier((*inner, *outer))
-    inner, outer = held[:QUARTERS], held[QUARTERS:]
     outer = [outer[0]] + [swap(outer[k], 2 * k) for k in ORDER]
     stepped = stepped.reshape(rows, points, -1)
 
     table = jnp.asarray(placing_table(), jnp.bfloat16)
     sums = []
     for pieces in ([], outer):
-        theirs, mine = combine(table, inner, pieces, grid_size)
+        theirs, mine, *rest = combine(table, inner, pieces, grid_size)
+        table = rest[0] if rest else None
         partial = mine + swap(theirs, 1)
         sums.append(partial + across(partial))
 
-    plus = [(i, (i + columns) % grid_size) for i in range(grid_size)]
-    minus = [(j, i) for i, j in plus]
+    ring_sign = 1 - 2 * jnp.bitwise_and(place, 1)
     matrix = jnp.asarray(fill_matrix(), jnp.bfloat16)
 
     def spots(source, edge):
@@ -483,12 +487,12 @@
     where = spots(place, 0) + spots(place, 1)
     for hop in range(1, ZLEN // 2):
         for s in range(2):
-            next_up = lax.ppermute(ups[s], "grid", plus)
-            next_down = lax.ppermute(downs[s], "grid", minus)
+            next_up = swap(downs[s], 1)
+            next_down = swap(ups[s], 1, 1)
             ups[s], downs[s] = next_up, next_down
             chunks += [next_up, next_down]
-            where += spots(place - hop, s) + spots(place + hop, s)
-    last = [lax.ppermute(ups[0], "grid", plus), lax.ppermute(downs[1], "grid", minus)]
+            where += spots(place + hop * ring_sign, s) + spots(place - hop * ring_sign, s)
+    last = [swap(downs[0], 1), swap(ups[1], 1, 1)]
     combined = fill(jnp.stack(where), matrix, chunks, rows, None)
     last, combined = lax.optimization_barrier((last, combined))
     spot = spots(place + ZLEN // 2, 0) + spots(place + ZLEN // 2, 1)

time: 101 us -> 98.5 us (0.975)
  starting transfers between devices: 45.2 us -> 40.1 us
  waiting for transfers between devices: 31 us -> 33.4 us
  local copies, waits for them, and re-layouts: 3.59 us -> 2.47 us
    ppermute x14 -> x0, starting transfers between devices: 20.3 us -> none  [the longest x6 13.4 us: per_device(): next_down = lax.ppermute(downs[s], 'grid', minus)]
    ppermute x8 -> x22, starting transfers between devices: 17.6 us -> 33.1 us  [swap(): return lax.ppermute(v, ('grid', 'dom'), pairs)]
    ppermute x8 -> x22, waiting for transfers between devices: 10.8 us -> 24.6 us  [swap(): return lax.ppermute(v, ('grid', 'dom'), pairs)]
    ppermute x14 -> x0, waiting for transfers between devices: 13 us -> none  [the longest x6 10.3 us: per_device(): next_down = lax.ppermute(downs[s], 'grid', minus)]
    ppermute x2, waiting for transfers between devices: 3.29 us -> 5 us  [per_device(): lax.ppermute(v, 'grid', [(i, i ^ 1) for i in range(grid_size)])]
    unnamed x8 -> x6, local copies, waits for them, and re-layouts: 3.47 us -> 2.35 us
  transfers between devices with their start and end apart: 26 -> 26, of which waited for: 15 -> 14; matrix products, arithmetic and copies ran while one was open for 0% -> 0% of each run, Pallas kernels for 9% -> 10%
where the time goes in v4:
time: 98.5 us; the launch traced here: 97 us
  starting transfers between devices  40.1 us (41%)
  waiting for transfers between devices  33.4 us (34%)
  Pallas kernels  17.9 us (18%)
  local copies, waits for them, and re-layouts  2.47 us (3%)
  other arithmetic  1.59 us (2%)
  between operations  1.56 us (2%)
    ppermute x22, starting transfers between devices, swap(): return lax.ppermute(v, ('grid', 'dom'), pairs)  33.1 us
    ppermute x22, waiting for transfers between devices, swap(): return lax.ppermute(v, ('grid', 'dom'), pairs)  24.6 us
    pallas_call x2, Pallas kernels, step_call(): pl.pallas_call(lambda *refs: kernel(rows, points, *refs), out_shape=[jax....  11.1 us
    pallas_call x2, Pallas kernels, fill(): pl.pallas_call(lambda *refs: fill_kernel(chunks, width, with_base, *refs)...  5.77 us
    ppermute x2, waiting for transfers between devices, per_device(): lax.ppermute(v, 'grid', [(i, i ^ 1) for i in range(grid_size)])  5 us
    ppermute x1, waiting for transfers between devices, per_device(): before = lax.ppermute(values[rows - STEPS:], 'dom', up)  3.79 us
    ppermute x2, starting transfers between devices, per_device(): lax.ppermute(v, 'grid', [(i, i ^ 1) for i in range(grid_size)])  2.65 us
    ppermute x1, starting transfers between devices, per_device(): before = lax.ppermute(values[rows - STEPS:], 'dom', up)  2.41 us
  transfers between devices with their start and end apart: 26, of which 14 were waited for; matrix products, arithmetic and copies ran while one was open for 0% of the time, Pallas kernels for 10%

profile of v4, /device:TPU:6, one launch (start us, length us, event | category | flops | bytes accessed | tf_op | source)
XLA Modules:
  0.0 97.0 jit_solution(6355842888344493115)
XLA Ops:
  2.7 1.2 %copy-done = f32[1,32,64,128]{3,2,1,0:T(8,128)S(1)} copy-done((f32[1,32,64,128]{3,2,1,0:T(8,128)S(1)}, f32[1,32,64,128]{3,2,1,0:T(8,128)}, u32[]{:S(2)}) %copy-start) | copy-done | bytes 1048600
  3.9 6.6 %inner_steps.1 = (f32[2048,128]{1,0:T(8,128)}, f32[392,128]{1,0:T(8,128)S(1)}, f32[392,128]{1,0:T(8,128)S(1)}, f32[392,128]{1,0:T(8,128)S(1)}, f32[392,128]{1,0:T(8,128)S(1)}) custom-call(f32[14]{0:T(128)S(1)} %pad_maximum_fusion.refs_0_, f32[2048,128]{1,0:T(8,128)S(1)} %bitcast.45), custom_call_target="tpu_custom_call" | custom-call | flops 26214400 | bytes 3145728 | tf_op jit(solution)/shard_map/inner_steps/pallas_call | solution.py:272
  10.5 7.3 %collective-permute-start.2 = (f32[392,128]{1,0:T(8,128)S(1)}, f32[392,128]{1,0:T(8,128)S(1)}, u32[]{:S(2)}, u32[]{:S(2)}) collective-permute-start(f32[392,128]{1,0:T(8,128)S(1)} %get-tuple-element.23), channel_id=1, source_target_pairs={{0,128},{1,129},{2,130},{3,131},{4,132},{5,133},{6,134},{7,135},{8... | collective-permute-start | bytes 602120 | tf_op jit(solution)/shard_map/ppermute | solution.py:450
  17.8 1.3 %collective-permute-start.3 = (f32[392,128]{1,0:T(8,128)S(1)}, f32[392,128]{1,0:T(8,128)S(1)}, u32[]{:S(2)}, u32[]{:S(2)}) collective-permute-start(f32[392,128]{1,0:T(8,128)S(1)} %get-tuple-element.24), channel_id=1, source_target_pairs={{0,64},{1,193},{2,66},{3,195},{4,68},{5,197},{6,70},{7,199},{8,72}... | collective-permute-start | bytes 602120 | tf_op jit(solution)/shard_map/ppermute | solution.py:450
  19.1 1.9 %collective-permute-start.1 = (f32[4,64,128]{2,1,0:T(8,128)S(1)}, f32[4,64,128]{2,1,0:T(8,128)S(1)}, u32[]{:S(2)}, u32[]{:S(2)}) collective-permute-start(f32[4,64,128]{2,1,0:T(8,128)S(1)} %get-tuple-element.38), channel_id=1, source_target_pairs={{1,0},{2,1},{3,2},{4,3},{5,4},{6,5},{7,6},{8,7},{9,8},{10,9},{11,1... | collective-permute-start | bytes 393224 | tf_op jit(solution)/shard_map/ppermute | solution.py:457
  21.0 2.4 %collective-permute-start = (f32[4,64,128]{2,1,0:T(8,128)S(1)}, f32[4,64,128]{2,1,0:T(8,128)S(1)}, u32[]{:S(2)}, u32[]{:S(2)}) collective-permute-start(f32[4,64,128]{2,1,0:T(8,128)S(1)} %get-tuple-element.39), channel_id=1, source_target_pairs={{0,1},{1,2},{2,3},{3,4},{4,5},{5,6},{6,7},{7,8},{8,9},{9,10},{10,1... | collective-permute-start | bytes 393224 | tf_op jit(solution)/shard_map/ppermute | solution.py:456
  23.5 3.8 %collective-permute-done = f32[4,64,128]{2,1,0:T(8,128)S(1)} collective-permute-done((f32[4,64,128]{2,1,0:T(8,128)S(1)}, f32[4,64,128]{2,1,0:T(8,128)S(1)}, u32[]{:S(2)}, u32[]{:S(2)}) %collective-permute-start) | collective-permute-done | bytes 131104 | tf_op jit(solution)/shard_map/ppermute | solution.py:456
  27.3 4.5 %outer_steps.1 = (f32[2048,128]{1,0:T(8,128)}, f32[128,128]{1,0:T(8,128)S(1)}, f32[128,128]{1,0:T(8,128)S(1)}, f32[128,128]{1,0:T(8,128)S(1)}, f32[128,128]{1,0:T(8,128)S(1)}) custom-call(f32[14]{0:T(128)S(1)} %pad_maximum_fusion.refs_0_, f32[2048,128]{1,0:T(8,128)S(1)} %bitcast.46, f32[256,128]{1,0:T(8,128)S(1)} %bitcast.48, ...), custom_call_target="tpu_custom_call", output_to_operand_aliasing={{0}: (4, {})} | custom-call | flops 19660800 | bytes 2359296 | tf_op jit(solution)/shard_map/outer_steps/pallas_call | solution.py:272
  31.8 5.3 %collective-permute-start.11 = (f32[128,128]{1,0:T(8,128)S(1)}, f32[128,128]{1,0:T(8,128)S(1)}, u32[]{:S(2)}, u32[]{:S(2)}) collective-permute-start(f32[128,128]{1,0:T(8,128)S(1)} %get-tuple-element.30), channel_id=1, source_target_pairs={{0,128},{1,129},{2,130},{3,131},{4,132},{5,133},{6,134},{7,135},{8... | collective-permute-start | bytes 196616 | tf_op jit(solution)/shard_map/ppermute | solution.py:450
  41.0 4.3 %collective-permute-done.12.refs_7_ = f32[128,128]{1,0:T(8,128)S(1)} collective-permute-done((f32[128,128]{1,0:T(8,128)S(1)}, f32[128,128]{1,0:T(8,128)S(1)}, u32[]{:S(2)}, u32[]{:S(2)}) %collective-permute-start.12) | collective-permute-done | bytes 65568 | tf_op jit(solution)/shard_map/ppermute | solution.py:450
  45.9 2.4 %collective-permute-start.14 = (f32[2,208,128]{2,1,0:T(8,128)S(1)}, f32[2,208,128]{2,1,0:T(8,128)S(1)}, u32[]{:S(2)}, u32[]{:S(2)}) collective-permute-start(f32[2,208,128]{2,1,0:T(8,128)S(1)} %get-tuple-element.34), channel_id=1, source_target_pairs={{0,32},{1,225},{2,34},{3,227},{4,36},{5,229},{6,38},{7,231},{8,40}... | collective-permute-start | bytes 638984 | tf_op jit(solution)/shard_map/ppermute | solution.py:450
  48.3 1.3 %collective-permute-start.6 = (f32[2,208,128]{2,1,0:T(8,128)S(1)}, f32[2,208,128]{2,1,0:T(8,128)S(1)}, u32[]{:S(2)}, u32[]{:S(2)}) collective-permute-start(f32[2,208,128]{2,1,0:T(8,128)S(1)} %add.206), channel_id=1, source_target_pairs={{0,16},{16,0},{32,48},{48,32},{64,80},{80,64},{96,112},{112,96},{1... | collective-permute-start | bytes 638984 | tf_op jit(solution)/shard_map/ppermute | solution.py:452
  49.6 2.5 %collective-permute-done.14 = f32[2,208,128]{2,1,0:T(8,128)S(1)} collective-permute-done((f32[2,208,128]{2,1,0:T(8,128)S(1)}, f32[2,208,128]{2,1,0:T(8,128)S(1)}, u32[]{:S(2)}, u32[]{:S(2)}) %collective-permute-start.14) | collective-permute-done | bytes 213024 | tf_op jit(solution)/shard_map/ppermute | solution.py:450
  52.1 1.3 %collective-permute-start.15 = (f32[2,208,128]{2,1,0:T(8,128)S(1)}, f32[2,208,128]{2,1,0:T(8,128)S(1)}, u32[]{:S(2)}, u32[]{:S(2)}) collective-permute-start(f32[2,208,128]{2,1,0:T(8,128)S(1)} %add.208), channel_id=1, source_target_pairs={{0,16},{16,0},{32,48},{48,32},{64,80},{80,64},{96,112},{112,96},{1... | collective-permute-start | bytes 638984 | tf_op jit(solution)/shard_map/ppermute | solution.py:452
  53.5 3.0 %collective-permute-done.6 = f32[2,208,128]{2,1,0:T(8,128)S(1)} collective-permute-done((f32[2,208,128]{2,1,0:T(8,128)S(1)}, f32[2,208,128]{2,1,0:T(8,128)S(1)}, u32[]{:S(2)}, u32[]{:S(2)}) %collective-permute-start.6) | collective-permute-done | bytes 213024 | tf_op jit(solution)/shard_map/ppermute | solution.py:452
  56.5 1.8 %collective-permute-start.7 = (f32[2,208,128]{2,1,0:T(8,128)S(1)}, f32[2,208,128]{2,1,0:T(8,128)S(1)}, u32[]{:S(2)}, u32[]{:S(2)}) collective-permute-start(f32[2,208,128]{2,1,0:T(8,128)S(1)} %add.207.refs_2_), channel_id=1, source_target_pairs={{0,224},{1,33},{2,226},{3,35},{4,228},{5,37},{6,230},{7,39},{8,232... | collective-permute-start | bytes 638984 | tf_op jit(solution)/shard_map/ppermute | solution.py:450
  58.3 2.0 %collective-permute-done.15 = f32[2,208,128]{2,1,0:T(8,128)S(1)} collective-permute-done((f32[2,208,128]{2,1,0:T(8,128)S(1)}, f32[2,208,128]{2,1,0:T(8,128)S(1)}, u32[]{:S(2)}, u32[]{:S(2)}) %collective-permute-start.15) | collective-permute-done | bytes 213024 | tf_op jit(solution)/shard_map/ppermute | solution.py:452
  60.7 1.7 %collective-permute-start.20 = (f32[2,208,128]{2,1,0:T(8,128)S(1)}, f32[2,208,128]{2,1,0:T(8,128)S(1)}, u32[]{:S(2)}, u32[]{:S(2)}) collective-permute-start(f32[2,208,128]{2,1,0:T(8,128)S(1)} %add.207.refs_2_), channel_id=1, source_target_pairs={{0,32},{1,225},{2,34},{3,227},{4,36},{5,229},{6,38},{7,231},{8,40}... | collective-permute-start | bytes 638984 | tf_op jit(solution)/shard_map/ppermute | solution.py:450
  62.4 2.2 %collective-permute-start.21 = (f32[2,208,128]{2,1,0:T(8,128)S(1)}, f32[2,208,128]{2,1,0:T(8,128)S(1)}, u32[]{:S(2)}, u32[]{:S(2)}) collective-permute-start(f32[2,208,128]{2,1,0:T(8,128)S(1)} %add.209.refs_3_), channel_id=1, source_target_pairs={{0,224},{1,33},{2,226},{3,35},{4,228},{5,37},{6,230},{7,39},{8,232... | collective-permute-start | bytes 638984 | tf_op jit(solution)/shard_map/ppermute | solution.py:450
  64.6 2.9 %collective-permute-done.16.refs_6_ = f32[2,208,128]{2,1,0:T(8,128)S(1)} collective-permute-done((f32[2,208,128]{2,1,0:T(8,128)S(1)}, f32[2,208,128]{2,1,0:T(8,128)S(1)}, u32[]{:S(2)}, u32[]{:S(2)}) %collective-permute-start.16) | collective-permute-done | bytes 213024 | tf_op jit(solution)/shard_map/ppermute | solution.py:450
  67.5 1.6 %collective-permute-start.17 = (f32[2,208,128]{2,1,0:T(8,128)S(1)}, f32[2,208,128]{2,1,0:T(8,128)S(1)}, u32[]{:S(2)}, u32[]{:S(2)}) collective-permute-start(f32[2,208,128]{2,1,0:T(8,128)S(1)} %collective-permute-done.16.refs_6_), channel_id=1, source_target_pairs={{0,224},{1,33},{2,226},{3,35},{4,228},{5,37},{6,230},{7,39},{8,232... | collective-permute-start | bytes 638984 | tf_op jit(solution)/shard_map/ppermute | solution.py:450
  69.1 3.0 %collective-permute-done.20.refs_4_ = f32[2,208,128]{2,1,0:T(8,128)S(1)} collective-permute-done((f32[2,208,128]{2,1,0:T(8,128)S(1)}, f32[2,208,128]{2,1,0:T(8,128)S(1)}, u32[]{:S(2)}, u32[]{:S(2)}) %collective-permute-start.20) | collective-permute-done | bytes 213024 | tf_op jit(solution)/shard_map/ppermute | solution.py:450
  72.1 1.6 %collective-permute-start.22 = (f32[2,208,128]{2,1,0:T(8,128)S(1)}, f32[2,208,128]{2,1,0:T(8,128)S(1)}, u32[]{:S(2)}, u32[]{:S(2)}) collective-permute-start(f32[2,208,128]{2,1,0:T(8,128)S(1)} %collective-permute-done.20.refs_4_), channel_id=1, source_target_pairs={{0,224},{1,33},{2,226},{3,35},{4,228},{5,37},{6,230},{7,39},{8,232... | collective-permute-start | bytes 638984 | tf_op jit(solution)/shard_map/ppermute | solution.py:450
  73.7 2.9 %collective-permute-done.8.refs_8_ = f32[2,208,128]{2,1,0:T(8,128)S(1)} collective-permute-done((f32[2,208,128]{2,1,0:T(8,128)S(1)}, f32[2,208,128]{2,1,0:T(8,128)S(1)}, u32[]{:S(2)}, u32[]{:S(2)}) %collective-permute-start.8) | collective-permute-done | bytes 213024 | tf_op jit(solution)/shard_map/ppermute | solution.py:450
  76.6 1.6 %collective-permute-start.9 = (f32[2,208,128]{2,1,0:T(8,128)S(1)}, f32[2,208,128]{2,1,0:T(8,128)S(1)}, u32[]{:S(2)}, u32[]{:S(2)}) collective-permute-start(f32[2,208,128]{2,1,0:T(8,128)S(1)} %collective-permute-done.8.refs_8_), channel_id=1, source_target_pairs={{0,224},{1,33},{2,226},{3,35},{4,228},{5,37},{6,230},{7,39},{8,232... | collective-permute-start | bytes 638984 | tf_op jit(solution)/shard_map/ppermute | solution.py:450
  78.2 3.1 %collective-permute-done.22.refs_9_ = f32[2,208,128]{2,1,0:T(8,128)S(1)} collective-permute-done((f32[2,208,128]{2,1,0:T(8,128)S(1)}, f32[2,208,128]{2,1,0:T(8,128)S(1)}, u32[]{:S(2)}, u32[]{:S(2)}) %collective-permute-start.22) | collective-permute-done | bytes 213024 | tf_op jit(solution)/shard_map/ppermute | solution.py:450
  81.9 1.6 %collective-permute-start.25 = (f32[2,208,128]{2,1,0:T(8,128)S(1)}, f32[2,208,128]{2,1,0:T(8,128)S(1)}, u32[]{:S(2)}, u32[]{:S(2)}) collective-permute-start(f32[2,208,128]{2,1,0:T(8,128)S(1)} %collective-permute-done.23.refs_10_), channel_id=1, source_target_pairs={{0,224},{1,33},{2,226},{3,35},{4,228},{5,37},{6,230},{7,39},{8,232... | collective-permute-start | bytes 638984 | tf_op jit(solution)/shard_map/ppermute | solution.py:450
  83.7 2.3 %collective-permute-done.9.refs_13_ = f32[2,208,128]{2,1,0:T(8,128)S(1)} collective-permute-done((f32[2,208,128]{2,1,0:T(8,128)S(1)}, f32[2,208,128]{2,1,0:T(8,128)S(1)}, u32[]{:S(2)}, u32[]{:S(2)}) %collective-permute-start.9) | collective-permute-done | bytes 213024 | tf_op jit(solution)/shard_map/ppermute | solution.py:450
  86.0 2.0 %collective-permute-start.19 = (f32[2,208,128]{2,1,0:T(8,128)S(1)}, f32[2,208,128]{2,1,0:T(8,128)S(1)}, u32[]{:S(2)}, u32[]{:S(2)}) collective-permute-start(f32[2,208,128]{2,1,0:T(8,128)S(1)} %collective-permute-done.18.refs_14_), channel_id=1, source_target_pairs={{0,224},{1,33},{2,226},{3,35},{4,228},{5,37},{6,230},{7,39},{8,232... | collective-permute-start | bytes 638984 | tf_op jit(solution)/shard_map/ppermute | solution.py:450
  88.1 2.2 %collective-permute-done.24.refs_12_ = f32[2,208,128]{2,1,0:T(8,128)S(1)} collective-permute-done((f32[2,208,128]{2,1,0:T(8,128)S(1)}, f32[2,208,128]{2,1,0:T(8,128)S(1)}, u32[]{:S(2)}, u32[]{:S(2)}) %collective-permute-start.24) | collective-permute-done | bytes 213024 | tf_op jit(solution)/shard_map/ppermute | solution.py:450
  91.1 4.0 %fill.2.refs_4_ = f32[32,512,128]{2,1,0:T(8,128)} custom-call(s32[28]{0:T(128)S(1)} %stack.135.refs_0_, bf16[512,256]{1,0:T(8,128)(2,1)S(1)} %copy-done.1, f32[2,208,128]{2,1,0:T(8,128)S(1)} %add.207.refs_2_, f32[2,208,128]{2,1,0:T(8,128)S(1)} %add.209.refs_3_, f32[2,208,128]{2,1,0:T(8,128)S(1)} %collective-permute-done.20.refs_4_, ...), custom_call_target="tpu_custom_call" | custom-call | flops 2818572288 | bytes 10321920 | tf_op jit(solution)/shard_map/fill/pallas_call | solution.py:414
  95.1 1.8 %fill.3 = f32[32,512,128]{2,1,0:T(8,128)} custom-call(s32[4]{0:T(128)S(1)} %pad_add_fusion.refs_0_, bf16[512,256]{1,0:T(8,128)(2,1)S(1)} %copy-done.1, f32[2,208,128]{2,1,0:T(8,128)S(1)} %collective-permute-done.10.refs_2_, f32[2,208,128]{2,1,0:T(8,128)S(1)} %collective-permute-done.19.refs_3_, ...), custom_call_target="tpu_custom_call", output_to_operand_aliasing={{}: (4, {})} | custom-call | flops 402653184 | bytes 1474560 | tf_op jit(solution)/shard_map/fill/pallas_call | solution.py:414
  (41 shorter events, 8.0 us)
Async XLA Ops:
  2.7 1.2 %copy-start = (f32[1,32,64,128]{3,2,1,0:T(8,128)S(1)}, f32[1,32,64,128]{3,2,1,0:T(8,128)}, u32[]{:S(2)}) copy-start(f32[1,32,64,128]{3,2,1,0:T(8,128)} %param.7) | copy-start | bytes 3145732
  3.9 87.2 %copy-start.1 = (bf16[512,256]{1,0:T(8,128)(2,1)S(1)}, bf16[512,256]{1,0:T(8,128)(2,1)}, u32[]{:S(2)}) copy-start(bf16[512,256]{1,0:T(8,128)(2,1)} %constant.58.clone.refs_1_) | copy-start | bytes 786436
  10.5 27.7 %collective-permute-start.2 = (f32[392,128]{1,0:T(8,128)S(1)}, f32[392,128]{1,0:T(8,128)S(1)}, u32[]{:S(2)}, u32[]{:S(2)}) collective-permute-start(f32[392,128]{1,0:T(8,128)S(1)} %get-tuple-element.23), channel_id=1, source_target_pairs={{0,128},{1,129},{2,130},{3,131},{4,132},{5,133},{6,134},{7,135},{8... | collective-permute-start | bytes 602120 | tf_op jit(solution)/shard_map/ppermute | solution.py:450
  17.8 20.5 %collective-permute-start.3 = (f32[392,128]{1,0:T(8,128)S(1)}, f32[392,128]{1,0:T(8,128)S(1)}, u32[]{:S(2)}, u32[]{:S(2)}) collective-permute-start(f32[392,128]{1,0:T(8,128)S(1)} %get-tuple-element.24), channel_id=1, source_target_pairs={{0,64},{1,193},{2,66},{3,195},{4,68},{5,197},{6,70},{7,199},{8,72}... | collective-permute-start | bytes 602120 | tf_op jit(solution)/shard_map/ppermute | solution.py:450
  19.1 19.3 %collective-permute-start.4 = (f32[392,128]{1,0:T(8,128)S(1)}, f32[392,128]{1,0:T(8,128)S(1)}, u32[]{:S(2)}, u32[]{:S(2)}) collective-permute-start(f32[392,128]{1,0:T(8,128)S(1)} %get-tuple-element.25), channel_id=1, source_target_pairs={{0,192},{1,65},{2,194},{3,67},{4,196},{5,69},{6,198},{7,71},{8,200... | collective-permute-start | bytes 602120 | tf_op jit(solution)/shard_map/ppermute | solution.py:450
  19.1 4.4 %collective-permute-start.1 = (f32[4,64,128]{2,1,0:T(8,128)S(1)}, f32[4,64,128]{2,1,0:T(8,128)S(1)}, u32[]{:S(2)}, u32[]{:S(2)}) collective-permute-start(f32[4,64,128]{2,1,0:T(8,128)S(1)} %get-tuple-element.38), channel_id=1, source_target_pairs={{1,0},{2,1},{3,2},{4,3},{5,4},{6,5},{7,6},{8,7},{9,8},{10,9},{11,1... | collective-permute-start | bytes 393224 | tf_op jit(solution)/shard_map/ppermute | solution.py:457
  21.0 6.3 %collective-permute-start = (f32[4,64,128]{2,1,0:T(8,128)S(1)}, f32[4,64,128]{2,1,0:T(8,128)S(1)}, u32[]{:S(2)}, u32[]{:S(2)}) collective-permute-start(f32[4,64,128]{2,1,0:T(8,128)S(1)} %get-tuple-element.39), channel_id=1, source_target_pairs={{0,1},{1,2},{2,3},{3,4},{4,5},{5,6},{6,7},{7,8},{8,9},{9,10},{10,1... | collective-permute-start | bytes 393224 | tf_op jit(solution)/shard_map/ppermute | solution.py:456
  31.8 9.3 %collective-permute-start.11 = (f32[128,128]{1,0:T(8,128)S(1)}, f32[128,128]{1,0:T(8,128)S(1)}, u32[]{:S(2)}, u32[]{:S(2)}) collective-permute-start(f32[128,128]{1,0:T(8,128)S(1)} %get-tuple-element.30), channel_id=1, source_target_pairs={{0,128},{1,129},{2,130},{3,131},{4,132},{5,133},{6,134},{7,135},{8... | collective-permute-start | bytes 196616 | tf_op jit(solution)/shard_map/ppermute | solution.py:450
  37.1 8.3 %collective-permute-start.12 = (f32[128,128]{1,0:T(8,128)S(1)}, f32[128,128]{1,0:T(8,128)S(1)}, u32[]{:S(2)}, u32[]{:S(2)}) collective-permute-start(f32[128,128]{1,0:T(8,128)S(1)} %get-tuple-element.31), channel_id=1, source_target_pairs={{0,64},{1,193},{2,66},{3,195},{4,68},{5,197},{6,70},{7,199},{8,72}... | collective-permute-start | bytes 196616 | tf_op jit(solution)/shard_map/ppermute | solution.py:450
  38.3 7.1 %collective-permute-start.13 = (f32[128,128]{1,0:T(8,128)S(1)}, f32[128,128]{1,0:T(8,128)S(1)}, u32[]{:S(2)}, u32[]{:S(2)}) collective-permute-start(f32[128,128]{1,0:T(8,128)S(1)} %get-tuple-element.32), channel_id=1, source_target_pairs={{0,192},{1,65},{2,194},{3,67},{4,196},{5,69},{6,198},{7,71},{8,200... | collective-permute-start | bytes 196616 | tf_op jit(solution)/shard_map/ppermute | solution.py:450
  38.4 1.1 %copy-start.2 = (bf16[7,208,192]{2,1,0:T(8,128)(2,1)S(1)}, bf16[7,208,192]{2,1,0:T(8,128)(2,1)}, u32[]{:S(2)}) copy-start(bf16[7,208,192]{2,1,0:T(8,128)(2,1)} %constant.57.clone.refs_0_) | copy-start | bytes 1677316
  40.0 8.3 %collective-permute-start.5 = (f32[2,208,128]{2,1,0:T(8,128)S(1)}, f32[2,208,128]{2,1,0:T(8,128)S(1)}, u32[]{:S(2)}, u32[]{:S(2)}) collective-permute-start(f32[2,208,128]{2,1,0:T(8,128)S(1)} %get-tuple-element.27), channel_id=1, source_target_pairs={{0,32},{1,225},{2,34},{3,227},{4,36},{5,229},{6,38},{7,231},{8,40}... | collective-permute-start | bytes 638984 | tf_op jit(solution)/shard_map/ppermute | solution.py:450
  45.9 6.2 %collective-permute-start.14 = (f32[2,208,128]{2,1,0:T(8,128)S(1)}, f32[2,208,128]{2,1,0:T(8,128)S(1)}, u32[]{:S(2)}, u32[]{:S(2)}) collective-permute-start(f32[2,208,128]{2,1,0:T(8,128)S(1)} %get-tuple-element.34), channel_id=1, source_target_pairs={{0,32},{1,225},{2,34},{3,227},{4,36},{5,229},{6,38},{7,231},{8,40}... | collective-permute-start | bytes 638984 | tf_op jit(solution)/shard_map/ppermute | solution.py:450
  48.3 8.2 %collective-permute-start.6 = (f32[2,208,128]{2,1,0:T(8,128)S(1)}, f32[2,208,128]{2,1,0:T(8,128)S(1)}, u32[]{:S(2)}, u32[]{:S(2)}) collective-permute-start(f32[2,208,128]{2,1,0:T(8,128)S(1)} %add.206), channel_id=1, source_target_pairs={{0,16},{16,0},{32,48},{48,32},{64,80},{80,64},{96,112},{112,96},{1... | collective-permute-start | bytes 638984 | tf_op jit(solution)/shard_map/ppermute | solution.py:452
  52.1 8.1 %collective-permute-start.15 = (f32[2,208,128]{2,1,0:T(8,128)S(1)}, f32[2,208,128]{2,1,0:T(8,128)S(1)}, u32[]{:S(2)}, u32[]{:S(2)}) collective-permute-start(f32[2,208,128]{2,1,0:T(8,128)S(1)} %add.208), channel_id=1, source_target_pairs={{0,16},{16,0},{32,48},{48,32},{64,80},{80,64},{96,112},{112,96},{1... | collective-permute-start | bytes 638984 | tf_op jit(solution)/shard_map/ppermute | solution.py:452
  56.5 8.1 %collective-permute-start.7 = (f32[2,208,128]{2,1,0:T(8,128)S(1)}, f32[2,208,128]{2,1,0:T(8,128)S(1)}, u32[]{:S(2)}, u32[]{:S(2)}) collective-permute-start(f32[2,208,128]{2,1,0:T(8,128)S(1)} %add.207.refs_2_), channel_id=1, source_target_pairs={{0,224},{1,33},{2,226},{3,35},{4,228},{5,37},{6,230},{7,39},{8,232... | collective-permute-start | bytes 638984 | tf_op jit(solution)/shard_map/ppermute | solution.py:450
  60.3 7.2 %collective-permute-start.16 = (f32[2,208,128]{2,1,0:T(8,128)S(1)}, f32[2,208,128]{2,1,0:T(8,128)S(1)}, u32[]{:S(2)}, u32[]{:S(2)}) collective-permute-start(f32[2,208,128]{2,1,0:T(8,128)S(1)} %add.209.refs_3_), channel_id=1, source_target_pairs={{0,32},{1,225},{2,34},{3,227},{4,36},{5,229},{6,38},{7,231},{8,40}... | collective-permute-start | bytes 638984 | tf_op jit(solution)/shard_map/ppermute | solution.py:450
  60.7 11.4 %collective-permute-start.20 = (f32[2,208,128]{2,1,0:T(8,128)S(1)}, f32[2,208,128]{2,1,0:T(8,128)S(1)}, u32[]{:S(2)}, u32[]{:S(2)}) collective-permute-start(f32[2,208,128]{2,1,0:T(8,128)S(1)} %add.207.refs_2_), channel_id=1, source_target_pairs={{0,32},{1,225},{2,34},{3,227},{4,36},{5,229},{6,38},{7,231},{8,40}... | collective-permute-start | bytes 638984 | tf_op jit(solution)/shard_map/ppermute | solution.py:450
  62.4 11.3 %collective-permute-start.21 = (f32[2,208,128]{2,1,0:T(8,128)S(1)}, f32[2,208,128]{2,1,0:T(8,128)S(1)}, u32[]{:S(2)}, u32[]{:S(2)}) collective-permute-start(f32[2,208,128]{2,1,0:T(8,128)S(1)} %add.209.refs_3_), channel_id=1, source_target_pairs={{0,224},{1,33},{2,226},{3,35},{4,228},{5,37},{6,230},{7,39},{8,232... | collective-permute-start | bytes 638984 | tf_op jit(solution)/shard_map/ppermute | solution.py:450
  64.6 12.0 %collective-permute-start.8 = (f32[2,208,128]{2,1,0:T(8,128)S(1)}, f32[2,208,128]{2,1,0:T(8,128)S(1)}, u32[]{:S(2)}, u32[]{:S(2)}) collective-permute-start(f32[2,208,128]{2,1,0:T(8,128)S(1)} %collective-permute-done.7.refs_5_), channel_id=1, source_target_pairs={{0,32},{1,225},{2,34},{3,227},{4,36},{5,229},{6,38},{7,231},{8,40}... | collective-permute-start | bytes 638984 | tf_op jit(solution)/shard_map/ppermute | solution.py:450
  67.5 10.7 %collective-permute-start.17 = (f32[2,208,128]{2,1,0:T(8,128)S(1)}, f32[2,208,128]{2,1,0:T(8,128)S(1)}, u32[]{:S(2)}, u32[]{:S(2)}) collective-permute-start(f32[2,208,128]{2,1,0:T(8,128)S(1)} %collective-permute-done.16.refs_6_), channel_id=1, source_target_pairs={{0,224},{1,33},{2,226},{3,35},{4,228},{5,37},{6,230},{7,39},{8,232... | collective-permute-start | bytes 638984 | tf_op jit(solution)/shard_map/ppermute | solution.py:450
  72.1 9.3 %collective-permute-start.22 = (f32[2,208,128]{2,1,0:T(8,128)S(1)}, f32[2,208,128]{2,1,0:T(8,128)S(1)}, u32[]{:S(2)}, u32[]{:S(2)}) collective-permute-start(f32[2,208,128]{2,1,0:T(8,128)S(1)} %collective-permute-done.20.refs_4_), channel_id=1, source_target_pairs={{0,224},{1,33},{2,226},{3,35},{4,228},{5,37},{6,230},{7,39},{8,232... | collective-permute-start | bytes 638984 | tf_op jit(solution)/shard_map/ppermute | solution.py:450
  73.7 8.2 %collective-permute-start.23 = (f32[2,208,128]{2,1,0:T(8,128)S(1)}, f32[2,208,128]{2,1,0:T(8,128)S(1)}, u32[]{:S(2)}, u32[]{:S(2)}) collective-permute-start(f32[2,208,128]{2,1,0:T(8,128)S(1)} %collective-permute-done.21.refs_7_), channel_id=1, source_target_pairs={{0,32},{1,225},{2,34},{3,227},{4,36},{5,229},{6,38},{7,231},{8,40}... | collective-permute-start | bytes 638984 | tf_op jit(solution)/shard_map/ppermute | solution.py:450
  76.6 9.4 %collective-permute-start.9 = (f32[2,208,128]{2,1,0:T(8,128)S(1)}, f32[2,208,128]{2,1,0:T(8,128)S(1)}, u32[]{:S(2)}, u32[]{:S(2)}) collective-permute-start(f32[2,208,128]{2,1,0:T(8,128)S(1)} %collective-permute-done.8.refs_8_), channel_id=1, source_target_pairs={{0,224},{1,33},{2,226},{3,35},{4,228},{5,37},{6,230},{7,39},{8,232... | collective-permute-start | bytes 638984 | tf_op jit(solution)/shard_map/ppermute | solution.py:450
  78.2 7.8 %collective-permute-start.18 = (f32[2,208,128]{2,1,0:T(8,128)S(1)}, f32[2,208,128]{2,1,0:T(8,128)S(1)}, u32[]{:S(2)}, u32[]{:S(2)}) collective-permute-start(f32[2,208,128]{2,1,0:T(8,128)S(1)} %collective-permute-done.17.refs_11_), channel_id=1, source_target_pairs={{0,32},{1,225},{2,34},{3,227},{4,36},{5,229},{6,38},{7,231},{8,40}... | collective-permute-start | bytes 638984 | tf_op jit(solution)/shard_map/ppermute | solution.py:450
  81.3 9.0 %collective-permute-start.24 = (f32[2,208,128]{2,1,0:T(8,128)S(1)}, f32[2,208,128]{2,1,0:T(8,128)S(1)}, u32[]{:S(2)}, u32[]{:S(2)}) collective-permute-start(f32[2,208,128]{2,1,0:T(8,128)S(1)} %collective-permute-done.22.refs_9_), channel_id=1, source_target_pairs={{0,32},{1,225},{2,34},{3,227},{4,36},{5,229},{6,38},{7,231},{8,40}... | collective-permute-start | bytes 638984 | tf_op jit(solution)/shard_map/ppermute | solution.py:450
  81.9 9.2 %collective-permute-start.25 = (f32[2,208,128]{2,1,0:T(8,128)S(1)}, f32[2,208,128]{2,1,0:T(8,128)S(1)}, u32[]{:S(2)}, u32[]{:S(2)}) collective-permute-start(f32[2,208,128]{2,1,0:T(8,128)S(1)} %collective-permute-done.23.refs_10_), channel_id=1, source_target_pairs={{0,224},{1,33},{2,226},{3,35},{4,228},{5,37},{6,230},{7,39},{8,232... | collective-permute-start | bytes 638984 | tf_op jit(solution)/shard_map/ppermute | solution.py:450
  86.0 9.0 %collective-permute-start.10 = (f32[2,208,128]{2,1,0:T(8,128)S(1)}, f32[2,208,128]{2,1,0:T(8,128)S(1)}, u32[]{:S(2)}, u32[]{:S(2)}) collective-permute-start(f32[2,208,128]{2,1,0:T(8,128)S(1)} %collective-permute-done.9.refs_13_), channel_id=1, source_target_pairs={{0,32},{1,225},{2,34},{3,227},{4,36},{5,229},{6,38},{7,231},{8,40}... | collective-permute-start | bytes 638984 | tf_op jit(solution)/shard_map/ppermute | solution.py:450
  86.0 9.0 %collective-permute-start.19 = (f32[2,208,128]{2,1,0:T(8,128)S(1)}, f32[2,208,128]{2,1,0:T(8,128)S(1)}, u32[]{:S(2)}, u32[]{:S(2)}) collective-permute-start(f32[2,208,128]{2,1,0:T(8,128)S(1)} %collective-permute-done.18.refs_14_), channel_id=1, source_target_pairs={{0,224},{1,33},{2,226},{3,35},{4,228},{5,37},{6,230},{7,39},{8,232... | collective-permute-start | bytes 638984 | tf_op jit(solution)/shard_map/ppermute | solution.py:450

commit v5 on v4

--- a/solution.py
+++ b/solution.py
@@ -156,8 +156,8 @@
 
 
 def inner_kernel(rows, points, facts_ref, start_ref, stepped_ref, *rest):
-    parts = rest[:QUARTERS]
-    first, second, final, coef_ref, load_sem, part_sem, store_sem = rest[QUARTERS:]
+    parts, edges = rest[:QUARTERS], rest[QUARTERS : QUARTERS + 3]
+    first, second, final, coef_ref, load_sem, part_sem, store_sem = rest[QUARTERS + 3 :]
     share = (rows - 2 * STEPS) // QUARTERS
     size = share * points
     block = size + META
@@ -168,6 +168,20 @@
     for index in range(QUARTERS):
         final[index * block + size : (index + 1) * block, :] = stencil.head
     load.wait()
+    odd = jnp.bitwise_and(lax.axis_index("dom"), 1)
+    halo, near, last = STEPS * points, 2 * STEPS * points, (rows - STEPS) * points
+    spans = [
+        (pl.multiple_of((1 - odd) * last, 8), halo, edges[0]),
+        (pl.multiple_of(odd * last, 8), halo, edges[1]),
+        (0, near, edges[2].at[pl.ds(0, near)]),
+        (rows * points - near, near, edges[2].at[pl.ds(near, near)]),
+    ]
+    passed = [
+        pltpu.make_async_copy(first.at[pl.ds(begin, size)], target, store_sem.at[QUARTERS + i])
+        for i, (begin, size, target) in enumerate(spans)
+    ]
+    for copy in passed:
+        copy.start()
 
     def located(row):
         group, inner = divmod(row - STEPS, share)
@@ -179,6 +193,9 @@
     for step in range(1, STEPS + 1):
         place = located if step == STEPS else same
         stencil.advance(buffers[step - 1], buffers[step], [(step, rows - step)], place, keep)
+        if step == 1:
+            for copy in passed:
+                copy.wait()
 
     copies = []
     for index, part in enumerate(parts):
@@ -200,15 +217,17 @@
         copy.wait()
 
 
-def outer_kernel(rows, points, facts_ref, start_ref, before_ref, after_ref, _, stepped_ref, *rest):
+def outer_kernel(rows, points, facts_ref, ends_ref, before_ref, after_ref, _, stepped_ref, *rest):
     parts = rest[:QUARTERS]
     first, second, final, coef_ref, load_sem, part_sem, store_sem = rest[QUARTERS:]
     halo, near = STEPS * points, 2 * STEPS * points
+    dom = lax.axis_index("dom")
+    near_side = pl.multiple_of((1 - jnp.bitwise_and(dom, 1)) * (halo + 2 * near), 8)
+    far_side = pl.multiple_of(jnp.bitwise_and(dom, 1) * (halo + 2 * near), 8)
     sides = [
-        (before_ref, 0, halo),
-        (start_ref.at[pl.ds(0, near)], halo, near),
-        (start_ref.at[pl.ds(rows * points - near, near)], halo + near, near),
-        (after_ref, halo + 2 * near, halo),
+        (before_ref, near_side, halo),
+        (ends_ref, halo, 2 * near),
+        (after_ref, far_side, halo),
     ]
     loads = [
         pltpu.make_async_copy(source, first.at[pl.ds(begin, size)], load_sem.at[i])
@@ -217,7 +236,6 @@
     for load in loads:
         load.start()
     quarter = jnp.right_shift(shifted_place(), 1)
-    dom = lax.axis_index("dom")
     keep_low = (dom > 0).astype(jnp.float32)
     keep_high = (dom < lax.axis_size("dom") - 1).astype(jnp.float32)
     stencil = Stencil(points, facts_ref, coef_ref)
@@ -265,16 +283,17 @@
         copy.wait()
 
 
-def step_call(kernel, name, facts, inputs, olds, rows, points, tall, wide, part, limit):
+def step_call(kernel, name, facts, inputs, olds, rows, points, tall, wide, part, extra, limit):
     lanes = inputs[0].shape[-1]
     anywhere = pl.BlockSpec(memory_space=pl.ANY)
     buffer = pltpu.VMEM((tall * points, lanes), jnp.float32)
     return pl.pallas_call(
         lambda *refs: kernel(rows, points, *refs),
         out_shape=[jax.ShapeDtypeStruct((rows * points, lanes), jnp.float32)]
-        + [jax.ShapeDtypeStruct((part, lanes), jnp.float32)] * QUARTERS,
+        + [jax.ShapeDtypeStruct((part, lanes), jnp.float32)] * QUARTERS
+        + [jax.ShapeDtypeStruct((size, lanes), jnp.float32) for size in extra],
         in_specs=[pl.BlockSpec(memory_space=pltpu.SMEM)] + [anywhere] * (len(inputs) + len(olds)),
-        out_specs=[anywhere] * (1 + QUARTERS),
+        out_specs=[anywhere] * (1 + QUARTERS + len(extra)),
         input_output_aliases={1 + len(inputs): 0} if olds else {},
         scratch_shapes=[
             buffer,
@@ -300,16 +319,15 @@
     inputs = [start.reshape(-1, lanes)]
     return step_call(
         inner_kernel, "inner_steps", facts, inputs, [], rows, points, rows, QUARTERS * part, part,
-        INNER_LIMIT,
+        [STEPS * points, STEPS * points, 4 * STEPS * points], INNER_LIMIT,
     )
 
 
-def outer_steps(facts, start, before, after, stepped):
-    rows, points, lanes = start.shape
-    inputs = [v.reshape(-1, lanes) for v in (start, before, after)]
+def outer_steps(facts, rows, points, ends, before, after, stepped):
+    inputs = [ends, before, after]
     return step_call(
         outer_kernel, "outer_steps", facts, inputs, [stepped], rows, points, 6 * STEPS,
-        2 * QUARTERS * points, 2 * points, OUTER_LIMIT,
+        2 * QUARTERS * points, 2 * points, [], OUTER_LIMIT,
     )
 
 
@@ -451,15 +469,15 @@
 
     across = lambda v: lax.ppermute(v, "grid", [(i, i ^ 1) for i in range(grid_size)])
 
-    up = [(i, i + 1) for i in range(dom_size - 1)]
-    down = [(j, i) for i, j in up]
-    before = lax.ppermute(values[rows - STEPS :], "dom", up)
-    after = lax.ppermute(values[:STEPS], "dom", down)
+    near = [(i, i ^ 1) for i in range(dom_size)]
+    far = [(i, i - 1 + 2 * (i % 2)) for i in range(1, dom_size - 1)]
     numbers = [levels[0].astype(jnp.float32), weights.astype(jnp.float32), diffusion[0], drift[0]]
     facts = jnp.concatenate(numbers)
-    stepped, *inner = inner_steps(facts, values)
+    stepped, *inner, before, after, ends = inner_steps(facts, values)
+    before = lax.ppermute(before, "dom", near)
+    after = lax.ppermute(after, "dom", far)
     inner = [inner[0]] + [swap(inner[k], 2 * k) for k in ORDER]
-    stepped, *outer = outer_steps(facts, values, before, after, stepped)
+    stepped, *outer = outer_steps(facts, rows, points, ends, before, after, stepped)
     outer = [outer[0]] + [swap(outer[k], 2 * k) for k in ORDER]
     stepped = stepped.reshape(rows, points, -1)
 

time: 98.5 us -> 95.7 us (0.972)
  starting transfers between devices: 40.1 us -> 33.4 us
  waiting for transfers between devices: 33.4 us -> 38 us
    ppermute x22, starting transfers between devices: 33.1 us -> 27.4 us  [swap(): return lax.ppermute(v, ('grid', 'dom'), pairs)]
    ppermute x22, waiting for transfers between devices: 24.6 us -> 28.9 us  [swap(): return lax.ppermute(v, ('grid', 'dom'), pairs)]
    ppermute x2, starting transfers between devices: 4.33 us -> 2.84 us  [the longest x1 2.84 us: per_device(): after = lax.ppermute(after, 'dom', far)]
  transfers between devices with their start and end apart: 26 -> 26, of which waited for: 14 -> 17; matrix products, arithmetic and copies ran while one was open for 0% -> 0% of each run, Pallas kernels for 10% -> 10%
where the time goes in v5:
time: 95.7 us; the launch traced here: 95.1 us
  waiting for transfers between devices  38 us (40%)
  starting transfers between devices  33.4 us (35%)
  Pallas kernels  18 us (19%)
  local copies, waits for them, and re-layouts  2.45 us (3%)
  between operations  1.62 us (2%)
  other arithmetic  1.59 us (2%)
    ppermute x22, waiting for transfers between devices, swap(): return lax.ppermute(v, ('grid', 'dom'), pairs)  28.9 us
    ppermute x22, starting transfers between devices, swap(): return lax.ppermute(v, ('grid', 'dom'), pairs)  27.4 us
    pallas_call x2, Pallas kernels, step_call(): pl.pallas_call(lambda *refs: kernel(rows, points, *refs), out_shape=[jax....  11.2 us
    pallas_call x2, Pallas kernels, fill(): pl.pallas_call(lambda *refs: fill_kernel(chunks, width, with_base, *refs)...  5.77 us
    ppermute x2, waiting for transfers between devices, per_device(): lax.ppermute(v, 'grid', [(i, i ^ 1) for i in range(grid_size)])  5.75 us
    ppermute x1, waiting for transfers between devices, per_device(): after = lax.ppermute(after, 'dom', far)  3.42 us
    ppermute x2, starting transfers between devices, per_device(): lax.ppermute(v, 'grid', [(i, i ^ 1) for i in range(grid_size)])  3.2 us
    ppermute x1, starting transfers between devices, per_device(): after = lax.ppermute(after, 'dom', far)  2.84 us
  transfers between devices with their start and end apart: 26, of which 17 were waited for; matrix products, arithmetic and copies ran while one was open for 0% of the time, Pallas kernels for 10%

profile of v5, /device:TPU:6, one launch (start us, length us, event | category | flops | bytes accessed | tf_op | source)
XLA Modules:
  0.0 95.1 jit_solution(17092691699910469699)
XLA Ops:
  2.7 1.2 %copy-done.1 = f32[1,32,64,128]{3,2,1,0:T(8,128)S(1)} copy-done((f32[1,32,64,128]{3,2,1,0:T(8,128)S(1)}, f32[1,32,64,128]{3,2,1,0:T(8,128)}, u32[]{:S(2)}) %copy-start.1) | copy-done | bytes 1048600
  4.0 6.8 %inner_steps.1 = (f32[2048,128]{1,0:T(8,128)}, f32[392,128]{1,0:T(8,128)S(1)}, f32[392,128]{1,0:T(8,128)S(1)}, f32[392,128]{1,0:T(8,128)S(1)}, f32[392,128]{1,0:...) custom-call(f32[14]{0:T(128)S(1)} %pad_maximum_fusion.refs_0_, ...), custom_call_target="tpu_custom_call" | custom-call | flops 26214400 | bytes 3145728 | tf_op jit(solution)/shard_map/inner_steps/pallas_call | solution.py:290
  10.8 7.1 %collective-permute-start.2 = (f32[392,128]{1,0:T(8,128)S(1)}, f32[392,128]{1,0:T(8,128)S(1)}, u32[]{:S(2)}, u32[]{:S(2)}) collective-permute-start(f32[392,128]{1,0:T(8,128)S(1)} %get-tuple-element.29), channel_id=1, source_target_pairs={{0,128},{1,129},{2,130},{3,131},{4,132},{5,133},{6,134},{7,135},{8... | collective-permute-start | bytes 602120 | tf_op jit(solution)/shard_map/ppermute | solution.py:468
  17.9 1.7 %collective-permute-start.3 = (f32[392,128]{1,0:T(8,128)S(1)}, f32[392,128]{1,0:T(8,128)S(1)}, u32[]{:S(2)}, u32[]{:S(2)}) collective-permute-start(f32[392,128]{1,0:T(8,128)S(1)} %get-tuple-element.30), channel_id=1, source_target_pairs={{0,64},{1,193},{2,66},{3,195},{4,68},{5,197},{6,70},{7,199},{8,72}... | collective-permute-start | bytes 602120 | tf_op jit(solution)/shard_map/ppermute | solution.py:468
  19.6 2.8 %collective-permute-start.1 = (f32[256,128]{1,0:T(8,128)S(1)}, f32[256,128]{1,0:T(8,128)S(1)}, u32[]{:S(2)}, u32[]{:S(2)}) collective-permute-start(f32[256,128]{1,0:T(8,128)S(1)} %get-tuple-element.25), channel_id=1, source_target_pairs={{1,2},{2,1},{3,4},{4,3},{5,6},{6,5},{7,8},{8,7},{9,10},{10,9},{11,... | collective-permute-start | bytes 393224 | tf_op jit(solution)/shard_map/ppermute | solution.py:478
  22.4 3.4 %collective-permute-done.1.refs_3_ = f32[256,128]{1,0:T(8,128)S(1)} collective-permute-done((f32[256,128]{1,0:T(8,128)S(1)}, f32[256,128]{1,0:T(8,128)S(1)}, u32[]{:S(2)}, u32[]{:S(2)}) %collective-permute-start.1) | collective-permute-done | bytes 131104 | tf_op jit(solution)/shard_map/ppermute | solution.py:478
  25.8 4.4 %outer_steps.1 = (f32[2048,128]{1,0:T(8,128)}, f32[128,128]{1,0:T(8,128)S(1)}, f32[128,128]{1,0:T(8,128)S(1)}, f32[128,128]{1,0:T(8,128)S(1)}, f32[128,128]{1,0:T(8,128)S(1)}) custom-call(f32[14]{0:T(128)S(1)} %pad_maximum_fusion.refs_0_, f32[1024,128]{1,0:T(8,128)S(1)} %get-tuple-element.23.refs_1_, ...), custom_call_target="tpu_custom_call", output_to_operand_aliasing={{0}: (4, {})} | custom-call | flops 19660800 | bytes 2359296 | tf_op jit(solution)/shard_map/outer_steps/pallas_call | solution.py:290
  30.2 4.8 %collective-permute-start.11 = (f32[128,128]{1,0:T(8,128)S(1)}, f32[128,128]{1,0:T(8,128)S(1)}, u32[]{:S(2)}, u32[]{:S(2)}) collective-permute-start(f32[128,128]{1,0:T(8,128)S(1)} %get-tuple-element.36), channel_id=1, source_target_pairs={{0,128},{1,129},{2,130},{3,131},{4,132},{5,133},{6,134},{7,135},{8... | collective-permute-start | bytes 196616 | tf_op jit(solution)/shard_map/ppermute | solution.py:468
  35.0 1.8 %collective-permute-start.12 = (f32[128,128]{1,0:T(8,128)S(1)}, f32[128,128]{1,0:T(8,128)S(1)}, u32[]{:S(2)}, u32[]{:S(2)}) collective-permute-start(f32[128,128]{1,0:T(8,128)S(1)} %get-tuple-element.37), channel_id=1, source_target_pairs={{0,64},{1,193},{2,66},{3,195},{4,68},{5,197},{6,70},{7,199},{8,72}... | collective-permute-start | bytes 196616 | tf_op jit(solution)/shard_map/ppermute | solution.py:468
  36.8 1.1 %copy-done.2 = bf16[7,208,192]{2,1,0:T(8,128)(2,1)S(1)} copy-done((bf16[7,208,192]{2,1,0:T(8,128)(2,1)S(1)}, bf16[7,208,192]{2,1,0:T(8,128)(2,1)}, u32[]{:S(2)}) %copy-start.2) | copy-done | bytes 559128
  38.5 1.3 %collective-permute-start.5 = (f32[2,208,128]{2,1,0:T(8,128)S(1)}, f32[2,208,128]{2,1,0:T(8,128)S(1)}, u32[]{:S(2)}, u32[]{:S(2)}) collective-permute-start(f32[2,208,128]{2,1,0:T(8,128)S(1)} %get-tuple-element.33), channel_id=1, source_target_pairs={{0,32},{1,225},{2,34},{3,227},{4,36},{5,229},{6,38},{7,231},{8,40}... | collective-permute-start | bytes 638984 | tf_op jit(solution)/shard_map/ppermute | solution.py:468
  39.8 1.1 %collective-permute-done.11.refs_6_ = f32[128,128]{1,0:T(8,128)S(1)} collective-permute-done((f32[128,128]{1,0:T(8,128)S(1)}, f32[128,128]{1,0:T(8,128)S(1)}, u32[]{:S(2)}, u32[]{:S(2)}) %collective-permute-start.11) | collective-permute-done | bytes 65568 | tf_op jit(solution)/shard_map/ppermute | solution.py:468
  41.1 3.5 %collective-permute-done.13.refs_8_ = f32[128,128]{1,0:T(8,128)S(1)} collective-permute-done((f32[128,128]{1,0:T(8,128)S(1)}, f32[128,128]{1,0:T(8,128)S(1)}, u32[]{:S(2)}, u32[]{:S(2)}) %collective-permute-start.13) | collective-permute-done | bytes 65568 | tf_op jit(solution)/shard_map/ppermute | solution.py:468
  46.6 1.6 %collective-permute-start.6 = (f32[2,208,128]{2,1,0:T(8,128)S(1)}, f32[2,208,128]{2,1,0:T(8,128)S(1)}, u32[]{:S(2)}, u32[]{:S(2)}) collective-permute-start(f32[2,208,128]{2,1,0:T(8,128)S(1)} %add.206), channel_id=1, source_target_pairs={{0,16},{16,0},{32,48},{48,32},{64,80},{80,64},{96,112},{112,96},{1... | collective-permute-start | bytes 638984 | tf_op jit(solution)/shard_map/ppermute | solution.py:470
  48.2 2.9 %collective-permute-done.14 = f32[2,208,128]{2,1,0:T(8,128)S(1)} collective-permute-done((f32[2,208,128]{2,1,0:T(8,128)S(1)}, f32[2,208,128]{2,1,0:T(8,128)S(1)}, u32[]{:S(2)}, u32[]{:S(2)}) %collective-permute-start.14) | collective-permute-done | bytes 213024 | tf_op jit(solution)/shard_map/ppermute | solution.py:468
  51.2 1.6 %collective-permute-start.15 = (f32[2,208,128]{2,1,0:T(8,128)S(1)}, f32[2,208,128]{2,1,0:T(8,128)S(1)}, u32[]{:S(2)}, u32[]{:S(2)}) collective-permute-start(f32[2,208,128]{2,1,0:T(8,128)S(1)} %add.208), channel_id=1, source_target_pairs={{0,16},{16,0},{32,48},{48,32},{64,80},{80,64},{96,112},{112,96},{1... | collective-permute-start | bytes 638984 | tf_op jit(solution)/shard_map/ppermute | solution.py:470
  52.7 0.8 collective-permute-done.6
  53.6 0.8 collective-permute-start.7
  54.4 4.9 %collective-permute-done.15 = f32[2,208,128]{2,1,0:T(8,128)S(1)} collective-permute-done((f32[2,208,128]{2,1,0:T(8,128)S(1)}, f32[2,208,128]{2,1,0:T(8,128)S(1)}, u32[]{:S(2)}, u32[]{:S(2)}) %collective-permute-start.15) | collective-permute-done | bytes 213024 | tf_op jit(solution)/shard_map/ppermute | solution.py:470
  59.4 0.8 collective-permute-start.16
  60.2 1.3 %collective-permute-start.20 = (f32[2,208,128]{2,1,0:T(8,128)S(1)}, f32[2,208,128]{2,1,0:T(8,128)S(1)}, u32[]{:S(2)}, u32[]{:S(2)}) collective-permute-start(f32[2,208,128]{2,1,0:T(8,128)S(1)} %add.207.refs_2_), channel_id=1, source_target_pairs={{0,32},{1,225},{2,34},{3,227},{4,36},{5,229},{6,38},{7,231},{8,40}... | collective-permute-start | bytes 638984 | tf_op jit(solution)/shard_map/ppermute | solution.py:468
  61.5 1.8 %collective-permute-start.8 = (f32[2,208,128]{2,1,0:T(8,128)S(1)}, f32[2,208,128]{2,1,0:T(8,128)S(1)}, u32[]{:S(2)}, u32[]{:S(2)}) collective-permute-start(f32[2,208,128]{2,1,0:T(8,128)S(1)} %collective-permute-done.7.refs_5_), channel_id=1, source_target_pairs={{0,32},{1,225},{2,34},{3,227},{4,36},{5,229},{6,38},{7,231},{8,40}... | collective-permute-start | bytes 638984 | tf_op jit(solution)/shard_map/ppermute | solution.py:468
  63.3 2.5 %collective-permute-done.16.refs_6_ = f32[2,208,128]{2,1,0:T(8,128)S(1)} collective-permute-done((f32[2,208,128]{2,1,0:T(8,128)S(1)}, f32[2,208,128]{2,1,0:T(8,128)S(1)}, u32[]{:S(2)}, u32[]{:S(2)}) %collective-permute-start.16) | collective-permute-done | bytes 213024 | tf_op jit(solution)/shard_map/ppermute | solution.py:468
  66.1 4.3 %collective-permute-done.20.refs_4_ = f32[2,208,128]{2,1,0:T(8,128)S(1)} collective-permute-done((f32[2,208,128]{2,1,0:T(8,128)S(1)}, f32[2,208,128]{2,1,0:T(8,128)S(1)}, u32[]{:S(2)}, u32[]{:S(2)}) %collective-permute-start.20) | collective-permute-done | bytes 213024 | tf_op jit(solution)/shard_map/ppermute | solution.py:468
  70.9 1.8 %collective-permute-start.23 = (f32[2,208,128]{2,1,0:T(8,128)S(1)}, f32[2,208,128]{2,1,0:T(8,128)S(1)}, u32[]{:S(2)}, u32[]{:S(2)}) collective-permute-start(f32[2,208,128]{2,1,0:T(8,128)S(1)} %collective-permute-done.21.refs_7_), channel_id=1, source_target_pairs={{0,32},{1,225},{2,34},{3,227},{4,36},{5,229},{6,38},{7,231},{8,40}... | collective-permute-start | bytes 638984 | tf_op jit(solution)/shard_map/ppermute | solution.py:468
  72.7 2.3 %collective-permute-done.8.refs_8_ = f32[2,208,128]{2,1,0:T(8,128)S(1)} collective-permute-done((f32[2,208,128]{2,1,0:T(8,128)S(1)}, f32[2,208,128]{2,1,0:T(8,128)S(1)}, u32[]{:S(2)}, u32[]{:S(2)}) %collective-permute-start.8) | collective-permute-done | bytes 213024 | tf_op jit(solution)/shard_map/ppermute | solution.py:468
  75.2 2.0 %collective-permute-start.18 = (f32[2,208,128]{2,1,0:T(8,128)S(1)}, f32[2,208,128]{2,1,0:T(8,128)S(1)}, u32[]{:S(2)}, u32[]{:S(2)}) collective-permute-start(f32[2,208,128]{2,1,0:T(8,128)S(1)} %collective-permute-done.17.refs_11_), channel_id=1, source_target_pairs={{0,32},{1,225},{2,34},{3,227},{4,36},{5,229},{6,38},{7,231},{8,40}... | collective-permute-start | bytes 638984 | tf_op jit(solution)/shard_map/ppermute | solution.py:468
  77.2 2.5 %collective-permute-done.22.refs_9_ = f32[2,208,128]{2,1,0:T(8,128)S(1)} collective-permute-done((f32[2,208,128]{2,1,0:T(8,128)S(1)}, f32[2,208,128]{2,1,0:T(8,128)S(1)}, u32[]{:S(2)}, u32[]{:S(2)}) %collective-permute-start.22) | collective-permute-done | bytes 213024 | tf_op jit(solution)/shard_map/ppermute | solution.py:468
  80.6 3.7 %collective-permute-done.9.refs_13_ = f32[2,208,128]{2,1,0:T(8,128)S(1)} collective-permute-done((f32[2,208,128]{2,1,0:T(8,128)S(1)}, f32[2,208,128]{2,1,0:T(8,128)S(1)}, u32[]{:S(2)}, u32[]{:S(2)}) %collective-permute-start.9) | collective-permute-done | bytes 213024 | tf_op jit(solution)/shard_map/ppermute | solution.py:468
  85.0 3.6 %collective-permute-done.24.refs_12_ = f32[2,208,128]{2,1,0:T(8,128)S(1)} collective-permute-done((f32[2,208,128]{2,1,0:T(8,128)S(1)}, f32[2,208,128]{2,1,0:T(8,128)S(1)}, u32[]{:S(2)}, u32[]{:S(2)}) %collective-permute-start.24) | collective-permute-done | bytes 213024 | tf_op jit(solution)/shard_map/ppermute | solution.py:468
  89.2 4.0 %fill.2.refs_4_ = f32[32,512,128]{2,1,0:T(8,128)} custom-call(s32[28]{0:T(128)S(1)} %stack.135.refs_0_, bf16[512,256]{1,0:T(8,128)(2,1)S(1)} %copy-done, f32[2,208,128]{2,1,0:T(8,128)S(1)} %add.207.refs_2_, f32[2,208,128]{2,1,0:T(8,128)S(1)} %add.209.refs_3_, f32[2,208,128]{2,1,0:T(8,128)S(1)} %collective-permute-done.20.refs_4_, ...), custom_call_target="tpu_custom_call" | custom-call | flops 2818572288 | bytes 10321920 | tf_op jit(solution)/shard_map/fill/pallas_call | solution.py:432
  93.2 1.8 %fill.3 = f32[32,512,128]{2,1,0:T(8,128)} custom-call(s32[4]{0:T(128)S(1)} %pad_add_fusion.refs_0_, bf16[512,256]{1,0:T(8,128)(2,1)S(1)} %copy-done, f32[2,208,128]{2,1,0:T(8,128)S(1)} %collective-permute-done.10.refs_2_, f32[2,208,128]{2,1,0:T(8,128)S(1)} %collective-permute-done.19.refs_3_, ...), custom_call_target="tpu_custom_call", output_to_operand_aliasing={{}: (4, {})} | custom-call | flops 402653184 | bytes 1474560 | tf_op jit(solution)/shard_map/fill/pallas_call | solution.py:432
  (40 shorter events, 7.2 us)
Async XLA Ops:
  0.6 88.5 %copy-start = (bf16[512,256]{1,0:T(8,128)(2,1)S(1)}, bf16[512,256]{1,0:T(8,128)(2,1)}, u32[]{:S(2)}) copy-start(bf16[512,256]{1,0:T(8,128)(2,1)} %constant.58.clone.refs_1_) | copy-start | bytes 786436
  2.7 1.2 %copy-start.1 = (f32[1,32,64,128]{3,2,1,0:T(8,128)S(1)}, f32[1,32,64,128]{3,2,1,0:T(8,128)}, u32[]{:S(2)}) copy-start(f32[1,32,64,128]{3,2,1,0:T(8,128)} %param.7) | copy-start | bytes 3145732
  10.8 26.0 %collective-permute-start.2 = (f32[392,128]{1,0:T(8,128)S(1)}, f32[392,128]{1,0:T(8,128)S(1)}, u32[]{:S(2)}, u32[]{:S(2)}) collective-permute-start(f32[392,128]{1,0:T(8,128)S(1)} %get-tuple-element.29), channel_id=1, source_target_pairs={{0,128},{1,129},{2,130},{3,131},{4,132},{5,133},{6,134},{7,135},{8... | collective-permute-start | bytes 602120 | tf_op jit(solution)/shard_map/ppermute | solution.py:468
  17.9 18.9 %collective-permute-start.3 = (f32[392,128]{1,0:T(8,128)S(1)}, f32[392,128]{1,0:T(8,128)S(1)}, u32[]{:S(2)}, u32[]{:S(2)}) collective-permute-start(f32[392,128]{1,0:T(8,128)S(1)} %get-tuple-element.30), channel_id=1, source_target_pairs={{0,64},{1,193},{2,66},{3,195},{4,68},{5,197},{6,70},{7,199},{8,72}... | collective-permute-start | bytes 602120 | tf_op jit(solution)/shard_map/ppermute | solution.py:468
  19.5 17.3 %collective-permute-start.4 = (f32[392,128]{1,0:T(8,128)S(1)}, f32[392,128]{1,0:T(8,128)S(1)}, u32[]{:S(2)}, u32[]{:S(2)}) collective-permute-start(f32[392,128]{1,0:T(8,128)S(1)} %get-tuple-element.31), channel_id=1, source_target_pairs={{0,192},{1,65},{2,194},{3,67},{4,196},{5,69},{6,198},{7,71},{8,200... | collective-permute-start | bytes 602120 | tf_op jit(solution)/shard_map/ppermute | solution.py:468
  19.6 2.9 %collective-permute-start = (f32[256,128]{1,0:T(8,128)S(1)}, f32[256,128]{1,0:T(8,128)S(1)}, u32[]{:S(2)}, u32[]{:S(2)}) collective-permute-start(f32[256,128]{1,0:T(8,128)S(1)} %get-tuple-element.24), channel_id=1, source_target_pairs={{0,1},{1,0},{2,3},{3,2},{4,5},{5,4},{6,7},{7,6},{8,9},{9,8},{10,11... | collective-permute-start | bytes 393224 | tf_op jit(solution)/shard_map/ppermute | solution.py:477
  19.6 6.3 %collective-permute-start.1 = (f32[256,128]{1,0:T(8,128)S(1)}, f32[256,128]{1,0:T(8,128)S(1)}, u32[]{:S(2)}, u32[]{:S(2)}) collective-permute-start(f32[256,128]{1,0:T(8,128)S(1)} %get-tuple-element.25), channel_id=1, source_target_pairs={{1,2},{2,1},{3,4},{4,3},{5,6},{6,5},{7,8},{8,7},{9,10},{10,9},{11,... | collective-permute-start | bytes 393224 | tf_op jit(solution)/shard_map/ppermute | solution.py:478
  30.2 10.7 %collective-permute-start.11 = (f32[128,128]{1,0:T(8,128)S(1)}, f32[128,128]{1,0:T(8,128)S(1)}, u32[]{:S(2)}, u32[]{:S(2)}) collective-permute-start(f32[128,128]{1,0:T(8,128)S(1)} %get-tuple-element.36), channel_id=1, source_target_pairs={{0,128},{1,129},{2,130},{3,131},{4,132},{5,133},{6,134},{7,135},{8... | collective-permute-start | bytes 196616 | tf_op jit(solution)/shard_map/ppermute | solution.py:468
  35.0 6.1 %collective-permute-start.12 = (f32[128,128]{1,0:T(8,128)S(1)}, f32[128,128]{1,0:T(8,128)S(1)}, u32[]{:S(2)}, u32[]{:S(2)}) collective-permute-start(f32[128,128]{1,0:T(8,128)S(1)} %get-tuple-element.37), channel_id=1, source_target_pairs={{0,64},{1,193},{2,66},{3,195},{4,68},{5,197},{6,70},{7,199},{8,72}... | collective-permute-start | bytes 196616 | tf_op jit(solution)/shard_map/ppermute | solution.py:468
  36.8 7.9 %collective-permute-start.13 = (f32[128,128]{1,0:T(8,128)S(1)}, f32[128,128]{1,0:T(8,128)S(1)}, u32[]{:S(2)}, u32[]{:S(2)}) collective-permute-start(f32[128,128]{1,0:T(8,128)S(1)} %get-tuple-element.38), channel_id=1, source_target_pairs={{0,192},{1,65},{2,194},{3,67},{4,196},{5,69},{6,198},{7,71},{8,200... | collective-permute-start | bytes 196616 | tf_op jit(solution)/shard_map/ppermute | solution.py:468
  36.8 1.1 %copy-start.2 = (bf16[7,208,192]{2,1,0:T(8,128)(2,1)S(1)}, bf16[7,208,192]{2,1,0:T(8,128)(2,1)}, u32[]{:S(2)}) copy-start(bf16[7,208,192]{2,1,0:T(8,128)(2,1)} %constant.57.clone.refs_0_) | copy-start | bytes 1677316
  38.5 8.0 %collective-permute-start.5 = (f32[2,208,128]{2,1,0:T(8,128)S(1)}, f32[2,208,128]{2,1,0:T(8,128)S(1)}, u32[]{:S(2)}, u32[]{:S(2)}) collective-permute-start(f32[2,208,128]{2,1,0:T(8,128)S(1)} %get-tuple-element.33), channel_id=1, source_target_pairs={{0,32},{1,225},{2,34},{3,227},{4,36},{5,229},{6,38},{7,231},{8,40}... | collective-permute-start | bytes 638984 | tf_op jit(solution)/shard_map/ppermute | solution.py:468
  45.2 5.9 %collective-permute-start.14 = (f32[2,208,128]{2,1,0:T(8,128)S(1)}, f32[2,208,128]{2,1,0:T(8,128)S(1)}, u32[]{:S(2)}, u32[]{:S(2)}) collective-permute-start(f32[2,208,128]{2,1,0:T(8,128)S(1)} %get-tuple-element.40), channel_id=1, source_target_pairs={{0,32},{1,225},{2,34},{3,227},{4,36},{5,229},{6,38},{7,231},{8,40}... | collective-permute-start | bytes 638984 | tf_op jit(solution)/shard_map/ppermute | solution.py:468
  46.6 7.0 %collective-permute-start.6 = (f32[2,208,128]{2,1,0:T(8,128)S(1)}, f32[2,208,128]{2,1,0:T(8,128)S(1)}, u32[]{:S(2)}, u32[]{:S(2)}) collective-permute-start(f32[2,208,128]{2,1,0:T(8,128)S(1)} %add.206), channel_id=1, source_target_pairs={{0,16},{16,0},{32,48},{48,32},{64,80},{80,64},{96,112},{112,96},{1... | collective-permute-start | bytes 638984 | tf_op jit(solution)/shard_map/ppermute | solution.py:470
  51.2 8.2 %collective-permute-start.15 = (f32[2,208,128]{2,1,0:T(8,128)S(1)}, f32[2,208,128]{2,1,0:T(8,128)S(1)}, u32[]{:S(2)}, u32[]{:S(2)}) collective-permute-start(f32[2,208,128]{2,1,0:T(8,128)S(1)} %add.208), channel_id=1, source_target_pairs={{0,16},{16,0},{32,48},{48,32},{64,80},{80,64},{96,112},{112,96},{1... | collective-permute-start | bytes 638984 | tf_op jit(solution)/shard_map/ppermute | solution.py:470
  53.6 7.9 %collective-permute-start.7 = (f32[2,208,128]{2,1,0:T(8,128)S(1)}, f32[2,208,128]{2,1,0:T(8,128)S(1)}, u32[]{:S(2)}, u32[]{:S(2)}) collective-permute-start(f32[2,208,128]{2,1,0:T(8,128)S(1)} %add.207.refs_2_), channel_id=1, source_target_pairs={{0,224},{1,33},{2,226},{3,35},{4,228},{5,37},{6,230},{7,39},{8,232... | collective-permute-start | bytes 638984 | tf_op jit(solution)/shard_map/ppermute | solution.py:468
  59.4 6.4 %collective-permute-start.16 = (f32[2,208,128]{2,1,0:T(8,128)S(1)}, f32[2,208,128]{2,1,0:T(8,128)S(1)}, u32[]{:S(2)}, u32[]{:S(2)}) collective-permute-start(f32[2,208,128]{2,1,0:T(8,128)S(1)} %add.209.refs_3_), channel_id=1, source_target_pairs={{0,32},{1,225},{2,34},{3,227},{4,36},{5,229},{6,38},{7,231},{8,40}... | collective-permute-start | bytes 638984 | tf_op jit(solution)/shard_map/ppermute | solution.py:468
  60.2 10.2 %collective-permute-start.20 = (f32[2,208,128]{2,1,0:T(8,128)S(1)}, f32[2,208,128]{2,1,0:T(8,128)S(1)}, u32[]{:S(2)}, u32[]{:S(2)}) collective-permute-start(f32[2,208,128]{2,1,0:T(8,128)S(1)} %add.207.refs_2_), channel_id=1, source_target_pairs={{0,32},{1,225},{2,34},{3,227},{4,36},{5,229},{6,38},{7,231},{8,40}... | collective-permute-start | bytes 638984 | tf_op jit(solution)/shard_map/ppermute | solution.py:468
  61.5 9.4 %collective-permute-start.21 = (f32[2,208,128]{2,1,0:T(8,128)S(1)}, f32[2,208,128]{2,1,0:T(8,128)S(1)}, u32[]{:S(2)}, u32[]{:S(2)}) collective-permute-start(f32[2,208,128]{2,1,0:T(8,128)S(1)} %add.209.refs_3_), channel_id=1, source_target_pairs={{0,224},{1,33},{2,226},{3,35},{4,228},{5,37},{6,230},{7,39},{8,232... | collective-permute-start | bytes 638984 | tf_op jit(solution)/shard_map/ppermute | solution.py:468
  61.5 13.4 %collective-permute-start.8 = (f32[2,208,128]{2,1,0:T(8,128)S(1)}, f32[2,208,128]{2,1,0:T(8,128)S(1)}, u32[]{:S(2)}, u32[]{:S(2)}) collective-permute-start(f32[2,208,128]{2,1,0:T(8,128)S(1)} %collective-permute-done.7.refs_5_), channel_id=1, source_target_pairs={{0,32},{1,225},{2,34},{3,227},{4,36},{5,229},{6,38},{7,231},{8,40}... | collective-permute-start | bytes 638984 | tf_op jit(solution)/shard_map/ppermute | solution.py:468
  65.8 9.4 %collective-permute-start.17 = (f32[2,208,128]{2,1,0:T(8,128)S(1)}, f32[2,208,128]{2,1,0:T(8,128)S(1)}, u32[]{:S(2)}, u32[]{:S(2)}) collective-permute-start(f32[2,208,128]{2,1,0:T(8,128)S(1)} %collective-permute-done.16.refs_6_), channel_id=1, source_target_pairs={{0,224},{1,33},{2,226},{3,35},{4,228},{5,37},{6,230},{7,39},{8,232... | collective-permute-start | bytes 638984 | tf_op jit(solution)/shard_map/ppermute | solution.py:468
  70.4 9.4 %collective-permute-start.22 = (f32[2,208,128]{2,1,0:T(8,128)S(1)}, f32[2,208,128]{2,1,0:T(8,128)S(1)}, u32[]{:S(2)}, u32[]{:S(2)}) collective-permute-start(f32[2,208,128]{2,1,0:T(8,128)S(1)} %collective-permute-done.20.refs_4_), channel_id=1, source_target_pairs={{0,224},{1,33},{2,226},{3,35},{4,228},{5,37},{6,230},{7,39},{8,232... | collective-permute-start | bytes 638984 | tf_op jit(solution)/shard_map/ppermute | solution.py:468
  70.9 8.9 %collective-permute-start.23 = (f32[2,208,128]{2,1,0:T(8,128)S(1)}, f32[2,208,128]{2,1,0:T(8,128)S(1)}, u32[]{:S(2)}, u32[]{:S(2)}) collective-permute-start(f32[2,208,128]{2,1,0:T(8,128)S(1)} %collective-permute-done.21.refs_7_), channel_id=1, source_target_pairs={{0,32},{1,225},{2,34},{3,227},{4,36},{5,229},{6,38},{7,231},{8,40}... | collective-permute-start | bytes 638984 | tf_op jit(solution)/shard_map/ppermute | solution.py:468
  74.9 9.4 %collective-permute-start.9 = (f32[2,208,128]{2,1,0:T(8,128)S(1)}, f32[2,208,128]{2,1,0:T(8,128)S(1)}, u32[]{:S(2)}, u32[]{:S(2)}) collective-permute-start(f32[2,208,128]{2,1,0:T(8,128)S(1)} %collective-permute-done.8.refs_8_), channel_id=1, source_target_pairs={{0,224},{1,33},{2,226},{3,35},{4,228},{5,37},{6,230},{7,39},{8,232... | collective-permute-start | bytes 638984 | tf_op jit(solution)/shard_map/ppermute | solution.py:468
  75.2 9.1 %collective-permute-start.18 = (f32[2,208,128]{2,1,0:T(8,128)S(1)}, f32[2,208,128]{2,1,0:T(8,128)S(1)}, u32[]{:S(2)}, u32[]{:S(2)}) collective-permute-start(f32[2,208,128]{2,1,0:T(8,128)S(1)} %collective-permute-done.17.refs_11_), channel_id=1, source_target_pairs={{0,32},{1,225},{2,34},{3,227},{4,36},{5,229},{6,38},{7,231},{8,40}... | collective-permute-start | bytes 638984 | tf_op jit(solution)/shard_map/ppermute | solution.py:468
  79.8 8.9 %collective-permute-start.24 = (f32[2,208,128]{2,1,0:T(8,128)S(1)}, f32[2,208,128]{2,1,0:T(8,128)S(1)}, u32[]{:S(2)}, u32[]{:S(2)}) collective-permute-start(f32[2,208,128]{2,1,0:T(8,128)S(1)} %collective-permute-done.22.refs_9_), channel_id=1, source_target_pairs={{0,32},{1,225},{2,34},{3,227},{4,36},{5,229},{6,38},{7,231},{8,40}... | collective-permute-start | bytes 638984 | tf_op jit(solution)/shard_map/ppermute | solution.py:468
  79.8 9.4 %collective-permute-start.25 = (f32[2,208,128]{2,1,0:T(8,128)S(1)}, f32[2,208,128]{2,1,0:T(8,128)S(1)}, u32[]{:S(2)}, u32[]{:S(2)}) collective-permute-start(f32[2,208,128]{2,1,0:T(8,128)S(1)} %collective-permute-done.23.refs_10_), channel_id=1, source_target_pairs={{0,224},{1,33},{2,226},{3,35},{4,228},{5,37},{6,230},{7,39},{8,232... | collective-permute-start | bytes 638984 | tf_op jit(solution)/shard_map/ppermute | solution.py:468
  84.3 8.8 %collective-permute-start.10 = (f32[2,208,128]{2,1,0:T(8,128)S(1)}, f32[2,208,128]{2,1,0:T(8,128)S(1)}, u32[]{:S(2)}, u32[]{:S(2)}) collective-permute-start(f32[2,208,128]{2,1,0:T(8,128)S(1)} %collective-permute-done.9.refs_13_), channel_id=1, source_target_pairs={{0,32},{1,225},{2,34},{3,227},{4,36},{5,229},{6,38},{7,231},{8,40}... | collective-permute-start | bytes 638984 | tf_op jit(solution)/shard_map/ppermute | solution.py:468
  84.3 8.9 %collective-permute-start.19 = (f32[2,208,128]{2,1,0:T(8,128)S(1)}, f32[2,208,128]{2,1,0:T(8,128)S(1)}, u32[]{:S(2)}, u32[]{:S(2)}) collective-permute-start(f32[2,208,128]{2,1,0:T(8,128)S(1)} %collective-permute-done.18.refs_14_), channel_id=1, source_target_pairs={{0,224},{1,33},{2,226},{3,35},{4,228},{5,37},{6,230},{7,39},{8,232... | collective-permute-start | bytes 638984 | tf_op jit(solution)/shard_map/ppermute | solution.py:468

commit v6 on v5

--- a/solution.py
+++ b/solution.py
@@ -14,6 +14,7 @@
 LEVEL_SUM = 6
 ZLEN = 8
 QUARTERS = 4
+FACTS = 14
 ORDER = (2, 1, 3)
 INNER_LIMIT = 24 * 2**20
 OUTER_LIMIT = 24 * 2**20
@@ -157,7 +158,7 @@
 
 def inner_kernel(rows, points, facts_ref, start_ref, stepped_ref, *rest):
     parts, edges = rest[:QUARTERS], rest[QUARTERS : QUARTERS + 3]
-    first, second, final, coef_ref, load_sem, part_sem, store_sem = rest[QUARTERS + 3 :]
+    first, second, final, coef_ref, load_sem, part_sem, store_sem, third = rest[QUARTERS + 3 :]
     share = (rows - 2 * STEPS) // QUARTERS
     size = share * points
     block = size + META
@@ -189,13 +190,10 @@
 
     same = lambda row: row * points
     keep = lambda row, value: value
-    buffers = [first, second, first, second, final]
+    buffers = [first, second, third, second, final]
     for step in range(1, STEPS + 1):
         place = located if step == STEPS else same
         stencil.advance(buffers[step - 1], buffers[step], [(step, rows - step)], place, keep)
-        if step == 1:
-            for copy in passed:
-                copy.wait()
 
     copies = []
     for index, part in enumerate(parts):
@@ -213,7 +211,7 @@
         )
     for copy in copies:
         copy.start()
-    for copy in copies:
+    for copy in passed + copies:
         copy.wait()
 
 
@@ -303,7 +301,8 @@
             pltpu.SemaphoreType.DMA((4,)) if olds else pltpu.SemaphoreType.DMA,
             pltpu.SemaphoreType.DMA((QUARTERS,)),
             pltpu.SemaphoreType.DMA((2 * QUARTERS,)),
-        ],
+        ]
+        + ([] if olds else [buffer]),
         compiler_params=pltpu.CompilerParams(vmem_limit_bytes=limit),
         cost_estimate=pl.CostEstimate(
             flops=25 * STEPS * tall * points * lanes, bytes_accessed=12 * tall * points * lanes,
@@ -472,7 +471,9 @@
     near = [(i, i ^ 1) for i in range(dom_size)]
     far = [(i, i - 1 + 2 * (i % 2)) for i in range(1, dom_size - 1)]
     numbers = [levels[0].astype(jnp.float32), weights.astype(jnp.float32), diffusion[0], drift[0]]
-    facts = jnp.concatenate(numbers)
+    facts = sum(
+        jnp.pad(v, (begin, FACTS - begin - v.shape[0])) for v, begin in zip(numbers, (0, 3, 4, 9))
+    )
     stepped, *inner, before, after, ends = inner_steps(facts, values)
     before = lax.ppermute(before, "dom", near)
     after = lax.ppermute(after, "dom", far)

time: 95.7 us -> 96.5 us (level)
  starting transfers between devices: 33.4 us -> 34.8 us
  waiting for transfers between devices: 38 us -> 36.8 us
    ppermute x22, waiting for transfers between devices: 28.9 us -> 27.1 us  [swap(): return lax.ppermute(v, ('grid', 'dom'), pairs)]
    ppermute x22, starting transfers between devices: 27.4 us -> 28.6 us  [swap(): return lax.ppermute(v, ('grid', 'dom'), pairs)]
  transfers between devices with their start and end apart: 26 -> 26, of which waited for: 17 -> 16; matrix products, arithmetic and copies ran while one was open for 0% -> 0% of each run, Pallas kernels for 10% -> 10%
where the time goes in v6:
time: 96.5 us; the launch traced here: 95.1 us
  waiting for transfers between devices  36.8 us (38%)
  starting transfers between devices  34.8 us (36%)
  Pallas kernels  17.9 us (19%)
  local copies, waits for them, and re-layouts  2.45 us (3%)
  between operations  1.62 us (2%)
  other arithmetic  1.59 us (2%)
    ppermute x22, starting transfers between devices, swap(): return lax.ppermute(v, ('grid', 'dom'), pairs)  28.6 us
    ppermute x22, waiting for transfers between devices, swap(): return lax.ppermute(v, ('grid', 'dom'), pairs)  27.1 us
    pallas_call x2, Pallas kernels, step_call(): pl.pallas_call(lambda *refs: kernel(rows, points, *refs), out_shape=[jax....  11.1 us
    ppermute x2, waiting for transfers between devices, per_device(): lax.ppermute(v, 'grid', [(i, i ^ 1) for i in range(grid_size)])  6.24 us
    pallas_call x2, Pallas kernels, fill(): pl.pallas_call(lambda *refs: fill_kernel(chunks, width, with_base, *refs)...  5.77 us
    ppermute x1, waiting for transfers between devices, per_device(): after = lax.ppermute(after, 'dom', far)  3.42 us
    ppermute x2, starting transfers between devices, per_device(): lax.ppermute(v, 'grid', [(i, i ^ 1) for i in range(grid_size)])  3.37 us
    ppermute x1, starting transfers between devices, per_device(): after = lax.ppermute(after, 'dom', far)  2.84 us
  transfers between devices with their start and end apart: 26, of which 16 were waited for; matrix products, arithmetic and copies ran while one was open for 0% of the time, Pallas kernels for 10%

profile of v6, /device:TPU:6, one launch (start us, length us, event | category | flops | bytes accessed | tf_op | source)
XLA Modules:
  0.0 95.1 jit_solution(1790370609307115448)
XLA Ops:
  2.7 1.2 %copy-done.1 = f32[1,32,64,128]{3,2,1,0:T(8,128)S(1)} copy-done((f32[1,32,64,128]{3,2,1,0:T(8,128)S(1)}, f32[1,32,64,128]{3,2,1,0:T(8,128)}, u32[]{:S(2)}) %copy-start.1) | copy-done | bytes 1048600
  4.0 6.8 %inner_steps.1 = (f32[2048,128]{1,0:T(8,128)}, f32[392,128]{1,0:T(8,128)S(1)}, f32[392,128]{1,0:T(8,128)S(1)}, f32[392,128]{1,0:T(8,128)S(1)}, f32[392,128]{1,0:...) custom-call(f32[14]{0:T(128)S(1)} %pad_add_fusion.1.refs_0_, ...), custom_call_target="tpu_custom_call" | custom-call | flops 26214400 | bytes 3145728 | tf_op jit(solution)/shard_map/inner_steps/pallas_call | solution.py:288
  10.7 7.3 %collective-permute-start.2 = (f32[392,128]{1,0:T(8,128)S(1)}, f32[392,128]{1,0:T(8,128)S(1)}, u32[]{:S(2)}, u32[]{:S(2)}) collective-permute-start(f32[392,128]{1,0:T(8,128)S(1)} %get-tuple-element.29), channel_id=1, source_target_pairs={{0,128},{1,129},{2,130},{3,131},{4,132},{5,133},{6,134},{7,135},{8... | collective-permute-start | bytes 602120 | tf_op jit(solution)/shard_map/ppermute | solution.py:467
  18.1 1.4 %collective-permute-start.3 = (f32[392,128]{1,0:T(8,128)S(1)}, f32[392,128]{1,0:T(8,128)S(1)}, u32[]{:S(2)}, u32[]{:S(2)}) collective-permute-start(f32[392,128]{1,0:T(8,128)S(1)} %get-tuple-element.30), channel_id=1, source_target_pairs={{0,64},{1,193},{2,66},{3,195},{4,68},{5,197},{6,70},{7,199},{8,72}... | collective-permute-start | bytes 602120 | tf_op jit(solution)/shard_map/ppermute | solution.py:467
  19.5 2.8 %collective-permute-start.1 = (f32[256,128]{1,0:T(8,128)S(1)}, f32[256,128]{1,0:T(8,128)S(1)}, u32[]{:S(2)}, u32[]{:S(2)}) collective-permute-start(f32[256,128]{1,0:T(8,128)S(1)} %get-tuple-element.25), channel_id=1, source_target_pairs={{1,2},{2,1},{3,4},{4,3},{5,6},{6,5},{7,8},{8,7},{9,10},{10,9},{11,... | collective-permute-start | bytes 393224 | tf_op jit(solution)/shard_map/ppermute | solution.py:479
  22.3 3.4 %collective-permute-done.1.refs_3_ = f32[256,128]{1,0:T(8,128)S(1)} collective-permute-done((f32[256,128]{1,0:T(8,128)S(1)}, f32[256,128]{1,0:T(8,128)S(1)}, u32[]{:S(2)}, u32[]{:S(2)}) %collective-permute-start.1) | collective-permute-done | bytes 131104 | tf_op jit(solution)/shard_map/ppermute | solution.py:479
  25.8 4.4 %outer_steps.1 = (f32[2048,128]{1,0:T(8,128)}, f32[128,128]{1,0:T(8,128)S(1)}, f32[128,128]{1,0:T(8,128)S(1)}, f32[128,128]{1,0:T(8,128)S(1)}, f32[128,128]{1,0:T(8,128)S(1)}) custom-call(f32[14]{0:T(128)S(1)} %pad_add_fusion.1.refs_0_, f32[1024,128]{1,0:T(8,128)S(1)} %get-tuple-element.23.refs_1_, ...), custom_call_target="tpu_custom_call", output_to_operand_aliasing={{0}: (4, {})} | custom-call | flops 19660800 | bytes 2359296 | tf_op jit(solution)/shard_map/outer_steps/pallas_call | solution.py:288
  30.1 5.2 %collective-permute-start.11 = (f32[128,128]{1,0:T(8,128)S(1)}, f32[128,128]{1,0:T(8,128)S(1)}, u32[]{:S(2)}, u32[]{:S(2)}) collective-permute-start(f32[128,128]{1,0:T(8,128)S(1)} %get-tuple-element.36), channel_id=1, source_target_pairs={{0,128},{1,129},{2,130},{3,131},{4,132},{5,133},{6,134},{7,135},{8... | collective-permute-start | bytes 196616 | tf_op jit(solution)/shard_map/ppermute | solution.py:467
  35.3 1.4 %collective-permute-start.12 = (f32[128,128]{1,0:T(8,128)S(1)}, f32[128,128]{1,0:T(8,128)S(1)}, u32[]{:S(2)}, u32[]{:S(2)}) collective-permute-start(f32[128,128]{1,0:T(8,128)S(1)} %get-tuple-element.37), channel_id=1, source_target_pairs={{0,64},{1,193},{2,66},{3,195},{4,68},{5,197},{6,70},{7,199},{8,72}... | collective-permute-start | bytes 196616 | tf_op jit(solution)/shard_map/ppermute | solution.py:467
  36.8 1.1 %copy-done.2 = bf16[7,208,192]{2,1,0:T(8,128)(2,1)S(1)} copy-done((bf16[7,208,192]{2,1,0:T(8,128)(2,1)S(1)}, bf16[7,208,192]{2,1,0:T(8,128)(2,1)}, u32[]{:S(2)}) %copy-start.2) | copy-done | bytes 559128
  38.4 1.1 %collective-permute-start.5 = (f32[2,208,128]{2,1,0:T(8,128)S(1)}, f32[2,208,128]{2,1,0:T(8,128)S(1)}, u32[]{:S(2)}, u32[]{:S(2)}) collective-permute-start(f32[2,208,128]{2,1,0:T(8,128)S(1)} %get-tuple-element.33), channel_id=1, source_target_pairs={{0,32},{1,225},{2,34},{3,227},{4,36},{5,229},{6,38},{7,231},{8,40}... | collective-permute-start | bytes 638984 | tf_op jit(solution)/shard_map/ppermute | solution.py:467
  39.5 1.4 %collective-permute-done.11.refs_6_ = f32[128,128]{1,0:T(8,128)S(1)} collective-permute-done((f32[128,128]{1,0:T(8,128)S(1)}, f32[128,128]{1,0:T(8,128)S(1)}, u32[]{:S(2)}, u32[]{:S(2)}) %collective-permute-start.11) | collective-permute-done | bytes 65568 | tf_op jit(solution)/shard_map/ppermute | solution.py:467
  41.5 2.8 %collective-permute-done.13.refs_8_ = f32[128,128]{1,0:T(8,128)S(1)} collective-permute-done((f32[128,128]{1,0:T(8,128)S(1)}, f32[128,128]{1,0:T(8,128)S(1)}, u32[]{:S(2)}, u32[]{:S(2)}) %collective-permute-start.13) | collective-permute-done | bytes 65568 | tf_op jit(solution)/shard_map/ppermute | solution.py:467
  46.6 1.6 %collective-permute-start.6 = (f32[2,208,128]{2,1,0:T(8,128)S(1)}, f32[2,208,128]{2,1,0:T(8,128)S(1)}, u32[]{:S(2)}, u32[]{:S(2)}) collective-permute-start(f32[2,208,128]{2,1,0:T(8,128)S(1)} %add.226), channel_id=1, source_target_pairs={{0,16},{16,0},{32,48},{48,32},{64,80},{80,64},{96,112},{112,96},{1... | collective-permute-start | bytes 638984 | tf_op jit(solution)/shard_map/ppermute | solution.py:469
  48.2 2.6 %collective-permute-done.14 = f32[2,208,128]{2,1,0:T(8,128)S(1)} collective-permute-done((f32[2,208,128]{2,1,0:T(8,128)S(1)}, f32[2,208,128]{2,1,0:T(8,128)S(1)}, u32[]{:S(2)}, u32[]{:S(2)}) %collective-permute-start.14) | collective-permute-done | bytes 213024 | tf_op jit(solution)/shard_map/ppermute | solution.py:467
  50.8 1.7 %collective-permute-start.15 = (f32[2,208,128]{2,1,0:T(8,128)S(1)}, f32[2,208,128]{2,1,0:T(8,128)S(1)}, u32[]{:S(2)}, u32[]{:S(2)}) collective-permute-start(f32[2,208,128]{2,1,0:T(8,128)S(1)} %add.228), channel_id=1, source_target_pairs={{0,16},{16,0},{32,48},{48,32},{64,80},{80,64},{96,112},{112,96},{1... | collective-permute-start | bytes 638984 | tf_op jit(solution)/shard_map/ppermute | solution.py:469
  52.5 1.2 %collective-permute-done.6 = f32[2,208,128]{2,1,0:T(8,128)S(1)} collective-permute-done((f32[2,208,128]{2,1,0:T(8,128)S(1)}, f32[2,208,128]{2,1,0:T(8,128)S(1)}, u32[]{:S(2)}, u32[]{:S(2)}) %collective-permute-start.6) | collective-permute-done | bytes 213024 | tf_op jit(solution)/shard_map/ppermute | solution.py:469
  54.1 5.0 %collective-permute-done.15 = f32[2,208,128]{2,1,0:T(8,128)S(1)} collective-permute-done((f32[2,208,128]{2,1,0:T(8,128)S(1)}, f32[2,208,128]{2,1,0:T(8,128)S(1)}, u32[]{:S(2)}, u32[]{:S(2)}) %collective-permute-start.15) | collective-permute-done | bytes 213024 | tf_op jit(solution)/shard_map/ppermute | solution.py:469
  59.8 1.5 %collective-permute-start.20 = (f32[2,208,128]{2,1,0:T(8,128)S(1)}, f32[2,208,128]{2,1,0:T(8,128)S(1)}, u32[]{:S(2)}, u32[]{:S(2)}) collective-permute-start(f32[2,208,128]{2,1,0:T(8,128)S(1)} %add.227.refs_2_), channel_id=1, source_target_pairs={{0,32},{1,225},{2,34},{3,227},{4,36},{5,229},{6,38},{7,231},{8,40}... | collective-permute-start | bytes 638984 | tf_op jit(solution)/shard_map/ppermute | solution.py:467
  61.2 2.0 %collective-permute-start.8 = (f32[2,208,128]{2,1,0:T(8,128)S(1)}, f32[2,208,128]{2,1,0:T(8,128)S(1)}, u32[]{:S(2)}, u32[]{:S(2)}) collective-permute-start(f32[2,208,128]{2,1,0:T(8,128)S(1)} %collective-permute-done.7.refs_5_), channel_id=1, source_target_pairs={{0,32},{1,225},{2,34},{3,227},{4,36},{5,229},{6,38},{7,231},{8,40}... | collective-permute-start | bytes 638984 | tf_op jit(solution)/shard_map/ppermute | solution.py:467
  63.3 1.9 %collective-permute-done.16.refs_6_ = f32[2,208,128]{2,1,0:T(8,128)S(1)} collective-permute-done((f32[2,208,128]{2,1,0:T(8,128)S(1)}, f32[2,208,128]{2,1,0:T(8,128)S(1)}, u32[]{:S(2)}, u32[]{:S(2)}) %collective-permute-start.16) | collective-permute-done | bytes 213024 | tf_op jit(solution)/shard_map/ppermute | solution.py:467
  66.0 3.7 %collective-permute-done.20.refs_4_ = f32[2,208,128]{2,1,0:T(8,128)S(1)} collective-permute-done((f32[2,208,128]{2,1,0:T(8,128)S(1)}, f32[2,208,128]{2,1,0:T(8,128)S(1)}, u32[]{:S(2)}, u32[]{:S(2)}) %collective-permute-start.20) | collective-permute-done | bytes 213024 | tf_op jit(solution)/shard_map/ppermute | solution.py:467
  70.6 1.6 %collective-permute-start.23 = (f32[2,208,128]{2,1,0:T(8,128)S(1)}, f32[2,208,128]{2,1,0:T(8,128)S(1)}, u32[]{:S(2)}, u32[]{:S(2)}) collective-permute-start(f32[2,208,128]{2,1,0:T(8,128)S(1)} %collective-permute-done.21.refs_7_), channel_id=1, source_target_pairs={{0,32},{1,225},{2,34},{3,227},{4,36},{5,229},{6,38},{7,231},{8,40}... | collective-permute-start | bytes 638984 | tf_op jit(solution)/shard_map/ppermute | solution.py:467
  72.2 2.1 %collective-permute-done.8.refs_8_ = f32[2,208,128]{2,1,0:T(8,128)S(1)} collective-permute-done((f32[2,208,128]{2,1,0:T(8,128)S(1)}, f32[2,208,128]{2,1,0:T(8,128)S(1)}, u32[]{:S(2)}, u32[]{:S(2)}) %collective-permute-start.8) | collective-permute-done | bytes 213024 | tf_op jit(solution)/shard_map/ppermute | solution.py:467
  75.2 1.6 %collective-permute-start.18 = (f32[2,208,128]{2,1,0:T(8,128)S(1)}, f32[2,208,128]{2,1,0:T(8,128)S(1)}, u32[]{:S(2)}, u32[]{:S(2)}) collective-permute-start(f32[2,208,128]{2,1,0:T(8,128)S(1)} %collective-permute-done.17.refs_11_), channel_id=1, source_target_pairs={{0,32},{1,225},{2,34},{3,227},{4,36},{5,229},{6,38},{7,231},{8,40}... | collective-permute-start | bytes 638984 | tf_op jit(solution)/shard_map/ppermute | solution.py:467
  76.8 3.0 %collective-permute-done.22.refs_9_ = f32[2,208,128]{2,1,0:T(8,128)S(1)} collective-permute-done((f32[2,208,128]{2,1,0:T(8,128)S(1)}, f32[2,208,128]{2,1,0:T(8,128)S(1)}, u32[]{:S(2)}, u32[]{:S(2)}) %collective-permute-start.22) | collective-permute-done | bytes 213024 | tf_op jit(solution)/shard_map/ppermute | solution.py:467
  79.8 1.1 %collective-permute-start.25 = (f32[2,208,128]{2,1,0:T(8,128)S(1)}, f32[2,208,128]{2,1,0:T(8,128)S(1)}, u32[]{:S(2)}, u32[]{:S(2)}) collective-permute-start(f32[2,208,128]{2,1,0:T(8,128)S(1)} %collective-permute-done.23.refs_10_), channel_id=1, source_target_pairs={{0,224},{1,33},{2,226},{3,35},{4,228},{5,37},{6,230},{7,39},{8,232... | collective-permute-start | bytes 638984 | tf_op jit(solution)/shard_map/ppermute | solution.py:467
  81.0 3.3 %collective-permute-done.9.refs_13_ = f32[2,208,128]{2,1,0:T(8,128)S(1)} collective-permute-done((f32[2,208,128]{2,1,0:T(8,128)S(1)}, f32[2,208,128]{2,1,0:T(8,128)S(1)}, u32[]{:S(2)}, u32[]{:S(2)}) %collective-permute-start.9) | collective-permute-done | bytes 213024 | tf_op jit(solution)/shard_map/ppermute | solution.py:467
  85.4 2.6 %collective-permute-done.24.refs_12_ = f32[2,208,128]{2,1,0:T(8,128)S(1)} collective-permute-done((f32[2,208,128]{2,1,0:T(8,128)S(1)}, f32[2,208,128]{2,1,0:T(8,128)S(1)}, u32[]{:S(2)}, u32[]{:S(2)}) %collective-permute-start.24) | collective-permute-done | bytes 213024 | tf_op jit(solution)/shard_map/ppermute | solution.py:467
  88.0 1.2 %collective-permute-done.25.refs_15_ = f32[2,208,128]{2,1,0:T(8,128)S(1)} collective-permute-done((f32[2,208,128]{2,1,0:T(8,128)S(1)}, f32[2,208,128]{2,1,0:T(8,128)S(1)}, u32[]{:S(2)}, u32[]{:S(2)}) %collective-permute-start.25) | collective-permute-done | bytes 213024 | tf_op jit(solution)/shard_map/ppermute | solution.py:467
  89.2 4.0 %fill.2.refs_4_ = f32[32,512,128]{2,1,0:T(8,128)} custom-call(s32[28]{0:T(128)S(1)} %stack.135.refs_0_, bf16[512,256]{1,0:T(8,128)(2,1)S(1)} %copy-done, f32[2,208,128]{2,1,0:T(8,128)S(1)} %add.227.refs_2_, f32[2,208,128]{2,1,0:T(8,128)S(1)} %add.229.refs_3_, f32[2,208,128]{2,1,0:T(8,128)S(1)} %collective-permute-done.20.refs_4_, ...), custom_call_target="tpu_custom_call" | custom-call | flops 2818572288 | bytes 10321920 | tf_op jit(solution)/shard_map/fill/pallas_call | solution.py:431
  93.2 1.8 %fill.3 = f32[32,512,128]{2,1,0:T(8,128)} custom-call(s32[4]{0:T(128)S(1)} %pad_add_fusion.refs_0_, bf16[512,256]{1,0:T(8,128)(2,1)S(1)} %copy-done, f32[2,208,128]{2,1,0:T(8,128)S(1)} %collective-permute-done.10.refs_2_, f32[2,208,128]{2,1,0:T(8,128)S(1)} %collective-permute-done.19.refs_3_, ...), custom_call_target="tpu_custom_call", output_to_operand_aliasing={{}: (4, {})} | custom-call | flops 402653184 | bytes 1474560 | tf_op jit(solution)/shard_map/fill/pallas_call | solution.py:431
  (40 shorter events, 9.6 us)
Async XLA Ops:
  0.6 88.6 %copy-start = (bf16[512,256]{1,0:T(8,128)(2,1)S(1)}, bf16[512,256]{1,0:T(8,128)(2,1)}, u32[]{:S(2)}) copy-start(bf16[512,256]{1,0:T(8,128)(2,1)} %constant.61.clone.refs_1_) | copy-start | bytes 786436
  2.7 1.2 %copy-start.1 = (f32[1,32,64,128]{3,2,1,0:T(8,128)S(1)}, f32[1,32,64,128]{3,2,1,0:T(8,128)}, u32[]{:S(2)}) copy-start(f32[1,32,64,128]{3,2,1,0:T(8,128)} %param.7) | copy-start | bytes 3145732
  10.7 26.0 %collective-permute-start.2 = (f32[392,128]{1,0:T(8,128)S(1)}, f32[392,128]{1,0:T(8,128)S(1)}, u32[]{:S(2)}, u32[]{:S(2)}) collective-permute-start(f32[392,128]{1,0:T(8,128)S(1)} %get-tuple-element.29), channel_id=1, source_target_pairs={{0,128},{1,129},{2,130},{3,131},{4,132},{5,133},{6,134},{7,135},{8... | collective-permute-start | bytes 602120 | tf_op jit(solution)/shard_map/ppermute | solution.py:467
  18.1 18.7 %collective-permute-start.3 = (f32[392,128]{1,0:T(8,128)S(1)}, f32[392,128]{1,0:T(8,128)S(1)}, u32[]{:S(2)}, u32[]{:S(2)}) collective-permute-start(f32[392,128]{1,0:T(8,128)S(1)} %get-tuple-element.30), channel_id=1, source_target_pairs={{0,64},{1,193},{2,66},{3,195},{4,68},{5,197},{6,70},{7,199},{8,72}... | collective-permute-start | bytes 602120 | tf_op jit(solution)/shard_map/ppermute | solution.py:467
  19.5 17.2 %collective-permute-start.4 = (f32[392,128]{1,0:T(8,128)S(1)}, f32[392,128]{1,0:T(8,128)S(1)}, u32[]{:S(2)}, u32[]{:S(2)}) collective-permute-start(f32[392,128]{1,0:T(8,128)S(1)} %get-tuple-element.31), channel_id=1, source_target_pairs={{0,192},{1,65},{2,194},{3,67},{4,196},{5,69},{6,198},{7,71},{8,200... | collective-permute-start | bytes 602120 | tf_op jit(solution)/shard_map/ppermute | solution.py:467
  19.5 2.9 %collective-permute-start = (f32[256,128]{1,0:T(8,128)S(1)}, f32[256,128]{1,0:T(8,128)S(1)}, u32[]{:S(2)}, u32[]{:S(2)}) collective-permute-start(f32[256,128]{1,0:T(8,128)S(1)} %get-tuple-element.24), channel_id=1, source_target_pairs={{0,1},{1,0},{2,3},{3,2},{4,5},{5,4},{6,7},{7,6},{8,9},{9,8},{10,11... | collective-permute-start | bytes 393224 | tf_op jit(solution)/shard_map/ppermute | solution.py:478
  19.5 6.3 %collective-permute-start.1 = (f32[256,128]{1,0:T(8,128)S(1)}, f32[256,128]{1,0:T(8,128)S(1)}, u32[]{:S(2)}, u32[]{:S(2)}) collective-permute-start(f32[256,128]{1,0:T(8,128)S(1)} %get-tuple-element.25), channel_id=1, source_target_pairs={{1,2},{2,1},{3,4},{4,3},{5,6},{6,5},{7,8},{8,7},{9,10},{10,9},{11,... | collective-permute-start | bytes 393224 | tf_op jit(solution)/shard_map/ppermute | solution.py:479
  30.1 10.8 %collective-permute-start.11 = (f32[128,128]{1,0:T(8,128)S(1)}, f32[128,128]{1,0:T(8,128)S(1)}, u32[]{:S(2)}, u32[]{:S(2)}) collective-permute-start(f32[128,128]{1,0:T(8,128)S(1)} %get-tuple-element.36), channel_id=1, source_target_pairs={{0,128},{1,129},{2,130},{3,131},{4,132},{5,133},{6,134},{7,135},{8... | collective-permute-start | bytes 196616 | tf_op jit(solution)/shard_map/ppermute | solution.py:467
  35.3 6.2 %collective-permute-start.12 = (f32[128,128]{1,0:T(8,128)S(1)}, f32[128,128]{1,0:T(8,128)S(1)}, u32[]{:S(2)}, u32[]{:S(2)}) collective-permute-start(f32[128,128]{1,0:T(8,128)S(1)} %get-tuple-element.37), channel_id=1, source_target_pairs={{0,64},{1,193},{2,66},{3,195},{4,68},{5,197},{6,70},{7,199},{8,72}... | collective-permute-start | bytes 196616 | tf_op jit(solution)/shard_map/ppermute | solution.py:467
  36.7 7.6 %collective-permute-start.13 = (f32[128,128]{1,0:T(8,128)S(1)}, f32[128,128]{1,0:T(8,128)S(1)}, u32[]{:S(2)}, u32[]{:S(2)}) collective-permute-start(f32[128,128]{1,0:T(8,128)S(1)} %get-tuple-element.38), channel_id=1, source_target_pairs={{0,192},{1,65},{2,194},{3,67},{4,196},{5,69},{6,198},{7,71},{8,200... | collective-permute-start | bytes 196616 | tf_op jit(solution)/shard_map/ppermute | solution.py:467
  36.7 1.1 %copy-start.2 = (bf16[7,208,192]{2,1,0:T(8,128)(2,1)S(1)}, bf16[7,208,192]{2,1,0:T(8,128)(2,1)}, u32[]{:S(2)}) copy-start(bf16[7,208,192]{2,1,0:T(8,128)(2,1)} %constant.60.clone.refs_0_) | copy-start | bytes 1677316
  38.4 8.2 %collective-permute-start.5 = (f32[2,208,128]{2,1,0:T(8,128)S(1)}, f32[2,208,128]{2,1,0:T(8,128)S(1)}, u32[]{:S(2)}, u32[]{:S(2)}) collective-permute-start(f32[2,208,128]{2,1,0:T(8,128)S(1)} %get-tuple-element.33), channel_id=1, source_target_pairs={{0,32},{1,225},{2,34},{3,227},{4,36},{5,229},{6,38},{7,231},{8,40}... | collective-permute-start | bytes 638984 | tf_op jit(solution)/shard_map/ppermute | solution.py:467
  44.9 5.9 %collective-permute-start.14 = (f32[2,208,128]{2,1,0:T(8,128)S(1)}, f32[2,208,128]{2,1,0:T(8,128)S(1)}, u32[]{:S(2)}, u32[]{:S(2)}) collective-permute-start(f32[2,208,128]{2,1,0:T(8,128)S(1)} %get-tuple-element.40), channel_id=1, source_target_pairs={{0,32},{1,225},{2,34},{3,227},{4,36},{5,229},{6,38},{7,231},{8,40}... | collective-permute-start | bytes 638984 | tf_op jit(solution)/shard_map/ppermute | solution.py:467
  46.6 7.2 %collective-permute-start.6 = (f32[2,208,128]{2,1,0:T(8,128)S(1)}, f32[2,208,128]{2,1,0:T(8,128)S(1)}, u32[]{:S(2)}, u32[]{:S(2)}) collective-permute-start(f32[2,208,128]{2,1,0:T(8,128)S(1)} %add.226), channel_id=1, source_target_pairs={{0,16},{16,0},{32,48},{48,32},{64,80},{80,64},{96,112},{112,96},{1... | collective-permute-start | bytes 638984 | tf_op jit(solution)/shard_map/ppermute | solution.py:469
  50.8 8.3 %collective-permute-start.15 = (f32[2,208,128]{2,1,0:T(8,128)S(1)}, f32[2,208,128]{2,1,0:T(8,128)S(1)}, u32[]{:S(2)}, u32[]{:S(2)}) collective-permute-start(f32[2,208,128]{2,1,0:T(8,128)S(1)} %add.228), channel_id=1, source_target_pairs={{0,16},{16,0},{32,48},{48,32},{64,80},{80,64},{96,112},{112,96},{1... | collective-permute-start | bytes 638984 | tf_op jit(solution)/shard_map/ppermute | solution.py:469
  53.8 7.4 %collective-permute-start.7 = (f32[2,208,128]{2,1,0:T(8,128)S(1)}, f32[2,208,128]{2,1,0:T(8,128)S(1)}, u32[]{:S(2)}, u32[]{:S(2)}) collective-permute-start(f32[2,208,128]{2,1,0:T(8,128)S(1)} %add.227.refs_2_), channel_id=1, source_target_pairs={{0,224},{1,33},{2,226},{3,35},{4,228},{5,37},{6,230},{7,39},{8,232... | collective-permute-start | bytes 638984 | tf_op jit(solution)/shard_map/ppermute | solution.py:467
  59.1 6.1 %collective-permute-start.16 = (f32[2,208,128]{2,1,0:T(8,128)S(1)}, f32[2,208,128]{2,1,0:T(8,128)S(1)}, u32[]{:S(2)}, u32[]{:S(2)}) collective-permute-start(f32[2,208,128]{2,1,0:T(8,128)S(1)} %add.229.refs_3_), channel_id=1, source_target_pairs={{0,32},{1,225},{2,34},{3,227},{4,36},{5,229},{6,38},{7,231},{8,40}... | collective-permute-start | bytes 638984 | tf_op jit(solution)/shard_map/ppermute | solution.py:467
  59.8 10.0 %collective-permute-start.20 = (f32[2,208,128]{2,1,0:T(8,128)S(1)}, f32[2,208,128]{2,1,0:T(8,128)S(1)}, u32[]{:S(2)}, u32[]{:S(2)}) collective-permute-start(f32[2,208,128]{2,1,0:T(8,128)S(1)} %add.227.refs_2_), channel_id=1, source_target_pairs={{0,32},{1,225},{2,34},{3,227},{4,36},{5,229},{6,38},{7,231},{8,40}... | collective-permute-start | bytes 638984 | tf_op jit(solution)/shard_map/ppermute | solution.py:467
  61.2 9.4 %collective-permute-start.21 = (f32[2,208,128]{2,1,0:T(8,128)S(1)}, f32[2,208,128]{2,1,0:T(8,128)S(1)}, u32[]{:S(2)}, u32[]{:S(2)}) collective-permute-start(f32[2,208,128]{2,1,0:T(8,128)S(1)} %add.229.refs_3_), channel_id=1, source_target_pairs={{0,224},{1,33},{2,226},{3,35},{4,228},{5,37},{6,230},{7,39},{8,232... | collective-permute-start | bytes 638984 | tf_op jit(solution)/shard_map/ppermute | solution.py:467
  61.2 13.1 %collective-permute-start.8 = (f32[2,208,128]{2,1,0:T(8,128)S(1)}, f32[2,208,128]{2,1,0:T(8,128)S(1)}, u32[]{:S(2)}, u32[]{:S(2)}) collective-permute-start(f32[2,208,128]{2,1,0:T(8,128)S(1)} %collective-permute-done.7.refs_5_), channel_id=1, source_target_pairs={{0,32},{1,225},{2,34},{3,227},{4,36},{5,229},{6,38},{7,231},{8,40}... | collective-permute-start | bytes 638984 | tf_op jit(solution)/shard_map/ppermute | solution.py:467
  65.2 10.0 %collective-permute-start.17 = (f32[2,208,128]{2,1,0:T(8,128)S(1)}, f32[2,208,128]{2,1,0:T(8,128)S(1)}, u32[]{:S(2)}, u32[]{:S(2)}) collective-permute-start(f32[2,208,128]{2,1,0:T(8,128)S(1)} %collective-permute-done.16.refs_6_), channel_id=1, source_target_pairs={{0,224},{1,33},{2,226},{3,35},{4,228},{5,37},{6,230},{7,39},{8,232... | collective-permute-start | bytes 638984 | tf_op jit(solution)/shard_map/ppermute | solution.py:467
  69.7 10.0 %collective-permute-start.22 = (f32[2,208,128]{2,1,0:T(8,128)S(1)}, f32[2,208,128]{2,1,0:T(8,128)S(1)}, u32[]{:S(2)}, u32[]{:S(2)}) collective-permute-start(f32[2,208,128]{2,1,0:T(8,128)S(1)} %collective-permute-done.20.refs_4_), channel_id=1, source_target_pairs={{0,224},{1,33},{2,226},{3,35},{4,228},{5,37},{6,230},{7,39},{8,232... | collective-permute-start | bytes 638984 | tf_op jit(solution)/shard_map/ppermute | solution.py:467
  70.6 9.1 %collective-permute-start.23 = (f32[2,208,128]{2,1,0:T(8,128)S(1)}, f32[2,208,128]{2,1,0:T(8,128)S(1)}, u32[]{:S(2)}, u32[]{:S(2)}) collective-permute-start(f32[2,208,128]{2,1,0:T(8,128)S(1)} %collective-permute-done.21.refs_7_), channel_id=1, source_target_pairs={{0,32},{1,225},{2,34},{3,227},{4,36},{5,229},{6,38},{7,231},{8,40}... | collective-permute-start | bytes 638984 | tf_op jit(solution)/shard_map/ppermute | solution.py:467
  74.3 10.0 %collective-permute-start.9 = (f32[2,208,128]{2,1,0:T(8,128)S(1)}, f32[2,208,128]{2,1,0:T(8,128)S(1)}, u32[]{:S(2)}, u32[]{:S(2)}) collective-permute-start(f32[2,208,128]{2,1,0:T(8,128)S(1)} %collective-permute-done.8.refs_8_), channel_id=1, source_target_pairs={{0,224},{1,33},{2,226},{3,35},{4,228},{5,37},{6,230},{7,39},{8,232... | collective-permute-start | bytes 638984 | tf_op jit(solution)/shard_map/ppermute | solution.py:467
  75.2 9.1 %collective-permute-start.18 = (f32[2,208,128]{2,1,0:T(8,128)S(1)}, f32[2,208,128]{2,1,0:T(8,128)S(1)}, u32[]{:S(2)}, u32[]{:S(2)}) collective-permute-start(f32[2,208,128]{2,1,0:T(8,128)S(1)} %collective-permute-done.17.refs_11_), channel_id=1, source_target_pairs={{0,32},{1,225},{2,34},{3,227},{4,36},{5,229},{6,38},{7,231},{8,40}... | collective-permute-start | bytes 638984 | tf_op jit(solution)/shard_map/ppermute | solution.py:467
  79.8 8.2 %collective-permute-start.24 = (f32[2,208,128]{2,1,0:T(8,128)S(1)}, f32[2,208,128]{2,1,0:T(8,128)S(1)}, u32[]{:S(2)}, u32[]{:S(2)}) collective-permute-start(f32[2,208,128]{2,1,0:T(8,128)S(1)} %collective-permute-done.22.refs_9_), channel_id=1, source_target_pairs={{0,32},{1,225},{2,34},{3,227},{4,36},{5,229},{6,38},{7,231},{8,40}... | collective-permute-start | bytes 638984 | tf_op jit(solution)/shard_map/ppermute | solution.py:467
  79.8 9.4 %collective-permute-start.25 = (f32[2,208,128]{2,1,0:T(8,128)S(1)}, f32[2,208,128]{2,1,0:T(8,128)S(1)}, u32[]{:S(2)}, u32[]{:S(2)}) collective-permute-start(f32[2,208,128]{2,1,0:T(8,128)S(1)} %collective-permute-done.23.refs_10_), channel_id=1, source_target_pairs={{0,224},{1,33},{2,226},{3,35},{4,228},{5,37},{6,230},{7,39},{8,232... | collective-permute-start | bytes 638984 | tf_op jit(solution)/shard_map/ppermute | solution.py:467
  84.3 8.8 %collective-permute-start.10 = (f32[2,208,128]{2,1,0:T(8,128)S(1)}, f32[2,208,128]{2,1,0:T(8,128)S(1)}, u32[]{:S(2)}, u32[]{:S(2)}) collective-permute-start(f32[2,208,128]{2,1,0:T(8,128)S(1)} %collective-permute-done.9.refs_13_), channel_id=1, source_target_pairs={{0,32},{1,225},{2,34},{3,227},{4,36},{5,229},{6,38},{7,231},{8,40}... | collective-permute-start | bytes 638984 | tf_op jit(solution)/shard_map/ppermute | solution.py:467
  84.3 8.9 %collective-permute-start.19 = (f32[2,208,128]{2,1,0:T(8,128)S(1)}, f32[2,208,128]{2,1,0:T(8,128)S(1)}, u32[]{:S(2)}, u32[]{:S(2)}) collective-permute-start(f32[2,208,128]{2,1,0:T(8,128)S(1)} %collective-permute-done.18.refs_14_), channel_id=1, source_target_pairs={{0,224},{1,33},{2,226},{3,35},{4,228},{5,37},{6,230},{7,39},{8,232... | collective-permute-start | bytes 638984 | tf_op jit(solution)/shard_map/ppermute | solution.py:467
